TPU v7x, 32 devices: a whole 2x2x4 slice. The times are simulated.
32 devices in a mesh: dp: 8 (over z, y), row: 2 (over core), col: 2 (over x).
Axes of the slice: x: 2, y: 2, z: 4, core: 2. Of those that a mesh axis runs over, the one named last changes fastest.
Arguments:
- layer_in: bfloat16 [8192, 1024], P('dp', ('row', 'col')), may hold values from -6 to 6
- lengths: int32 [8, 4], P('dp'), may hold values from 1 to 512, 1024 in all within a row
- placing: int32 [8, 1024], P('dp'), may hold values from 0 to 1023, each once within a row
- routes: int32 [8192, 2], P('dp'), may hold values from 0 to 3, all different within a row; in each aligned block of 1024 rows (0 to 1023, 1024 to 2047, ...) at most 640 rows name the same one
- cotangent: bfloat16 [8192, 1024], P('dp', ('row', 'col')), may hold values from -6 to 6
- norm_gains: float32 [2, 1024], P(None, ('row', 'col')), may hold values from 0.28 to 2.6, as said below
- gain_first: float32 [2, 1024], P(None, ('row', 'col')), may hold values from -512 to 512
- gain_second: float32 [2, 1024], P(None, ('row', 'col')), may hold values from 4096 to 65536
- rel_bias: float32 [32, 16], P(None, ('row', 'col')), may hold values from -6 to 6
- bias_first: float32 [32, 16], P(None, ('row', 'col')), may hold values from -256 to 256
- bias_second: float32 [32, 16], P(None, ('row', 'col')), may hold values from 1024 to 16384
- router: float32 [1024, 4], P(('row', 'col')), may hold values from -0.125 to 0.125
- router_first: float32 [1024, 4], P(('row', 'col')), may hold values from -5120 to 5120
- router_second: float32 [1024, 4], P(('row', 'col')), may hold values from 409600 to 6553600
- qkv_weight: float32 [2, 8, 64, 2, 3, 512], P('row', 'dp', None, None, None, 'col'), may hold values from -0.1875 to 0.1875
- qkv_first: float32 [2, 8, 64, 2, 3, 512], P('row', 'dp', None, None, None, 'col'), may hold values from -512 to 512
- qkv_second: float32 [2, 8, 64, 2, 3, 512], P('row', 'dp', None, None, None, 'col'), may hold values from 4096 to 65536
- proj_weight: float32 [2, 512, 2, 8, 64], P(None, 'col', 'row', 'dp'), may hold values from -0.5 to 0.5
- proj_first: float32 [2, 512, 2, 8, 64], P(None, 'col', 'row', 'dp'), may hold values from -160 to 160
- proj_second: float32 [2, 512, 2, 8, 64], P(None, 'col', 'row', 'dp'), may hold values from 368.64 to 5898.24
- expert_up: float32 [8, 1024, 2, 1408], P('dp', 'row', None, 'col'), may hold values from -0.1875 to 0.1875
- up_first: float32 [8, 1024, 2, 1408], P('dp', 'row', None, 'col'), may hold values from -192 to 192
- up_second: float32 [8, 1024, 2, 1408], P('dp', 'row', None, 'col'), may hold values from 512 to 8192
- expert_down: float32 [8, 1408, 1024], P('dp', 'col', 'row'), may hold values from -0.15625 to 0.15625
- down_first: float32 [8, 1408, 1024], P('dp', 'col', 'row'), may hold values from -96 to 96
- down_second: float32 [8, 1408, 1024], P('dp', 'col', 'row'), may hold values from 128 to 2048
Outputs:
- layer_out: bfloat16 [8192, 1024], P('dp', ('row', 'col'))
- input_grad: bfloat16 [8192, 1024], P('dp', ('row', 'col'))
- gains_new: float32 [2, 1024], P(None, ('row', 'col'))
- gains_moment: float32 [2, 1024], P(None, ('row', 'col'))
- gains_square: float32 [2, 1024], P(None, ('row', 'col'))
- bias_new: float32 [32, 16], P(None, ('row', 'col'))
- bias_moment: float32 [32, 16], P(None, ('row', 'col'))
- bias_square: float32 [32, 16], P(None, ('row', 'col'))
- router_new: float32 [1024, 4], P(('row', 'col'))
- router_moment: float32 [1024, 4], P(('row', 'col'))
- router_square: float32 [1024, 4], P(('row', 'col'))
- qkv_new: float32 [2, 8, 64, 2, 3, 512], P('row', 'dp', None, None, None, 'col')
- qkv_moment: float32 [2, 8, 64, 2, 3, 512], P('row', 'dp', None, None, None, 'col')
- qkv_square: float32 [2, 8, 64, 2, 3, 512], P('row', 'dp', None, None, None, 'col')
- qkv_copy: bfloat16 [2, 8, 64, 2, 3, 512], P('row', 'dp', None, None, None, 'col')
- proj_new: float32 [2, 512, 2, 8, 64], P(None, 'col', 'row', 'dp')
- proj_moment: float32 [2, 512, 2, 8, 64], P(None, 'col', 'row', 'dp')
- proj_square: float32 [2, 512, 2, 8, 64], P(None, 'col', 'row', 'dp')
- proj_copy: bfloat16 [2, 512, 2, 8, 64], P(None, 'col', 'row', 'dp')
- up_new: float32 [8, 1024, 2, 1408], P('dp', 'row', None, 'col')
- up_moment: float32 [8, 1024, 2, 1408], P('dp', 'row', None, 'col')
- up_square: float32 [8, 1024, 2, 1408], P('dp', 'row', None, 'col')
- up_copy: bfloat16 [8, 1024, 2, 1408], P('dp', 'row', None, 'col')
- down_new: float32 [8, 1408, 1024], P('dp', 'col', 'row')
- down_moment: float32 [8, 1408, 1024], P('dp', 'col', 'row')
- down_square: float32 [8, 1408, 1024], P('dp', 'col', 'row')
- down_copy: bfloat16 [8, 1408, 1024], P('dp', 'col', 'row')
Inputs may be any that keep to these rules, and one draw needn't show every extreme that they name: `lengths`: each row sums to 1024; its largest entry is 512. `placing`: each row is a permutation. `routes`: each token names 2 different experts; among the tokens of one index of dp no expert is named more than 640 times, and in some index one expert is named exactly 640 times. `norm_gains`: positive gains.
All inputs are finite; a program needn't handle non-finite values.
Results may differ from a plain program's by a relative error of at most 0.025.
Values may be sent and summed in bfloat16 or wider, within the bound.
A program may use at most 256 MiB of HBM per device.

v0:
```python
import jax
import jax.numpy as jnp
import numpy as np
from jax import lax
from jax.sharding import PartitionSpec as P

D = 1024
HEADS = 16
HD = 64
FF = 2816
TOP = 2
BUCKETS = 32
STEP = 5


bucket_edges = np.floor(16.0 * 2.0 ** (np.arange(16) * 0.375)).astype(np.int32)
norm_epsilon = 1e-06
beta_first = 0.5
beta_second = 0.5
adam_epsilon = 1e-08
weight_decay = 0.01
highest = lax.Precision.HIGHEST


def for_sending(value):
    return jax.tree.map(lambda a: a.astype(jnp.bfloat16) if a.dtype == jnp.float32 else a, value)


def norm_sums(values):
    return lax.psum(values, ("row", "col"))


def route_sums(values):
    return lax.psum(values.astype(jnp.bfloat16), ("row", "col")).astype(jnp.float32)


def by_columns(values):
    return lax.all_gather(values, "col", axis=1, tiled=True)


def to_columns(values):
    return lax.psum_scatter(values, "col", scatter_dimension=1, tiled=True)


def by_rows(values):
    return jax.tree.map(
        lambda part, own: part.astype(own.dtype),
        lax.all_gather(for_sending(values), "row", axis=1, tiled=True),
        values,
    )


def to_rows(values):
    return lax.psum_scatter(values, "row", scatter_dimension=1, tiled=True)


def hidden_share(values):
    return lax.psum_scatter(values, "row", scatter_dimension=0, tiled=True)


def hidden_whole(values):
    return lax.all_gather(values, "row", axis=0, tiled=True)


def move_slots(values):
    return lax.all_to_all(values, "dp", split_axis=0, concat_axis=0, tiled=True)


def bucket_of(distance):
    counted = jnp.zeros_like(distance)
    for edge_value in bucket_edges:
        counted = counted + (distance >= int(edge_value)).astype(jnp.int32)
    return jnp.where(distance < 16, distance, 15 + counted)


def sequence_ids(seq_lengths, length_all):
    ends = jnp.cumsum(seq_lengths)
    places = jnp.arange(length_all, dtype=jnp.int32)
    return jnp.sum((places[:, None] >= ends[None, :]).astype(jnp.int32), axis=1)


def norm_forward(resid, gain):
    inverse = lax.rsqrt(norm_sums(jnp.sum(resid * resid, axis=1)) / D + norm_epsilon)
    return (resid * inverse[:, None] * gain, inverse)


def norm_backward(resid, gain, inverse, grad_norm):
    scaled = grad_norm * gain
    row_total = norm_sums(jnp.sum(resid * scaled, axis=1))
    grad_resid = (
        scaled * inverse[:, None] - resid * (inverse * inverse * inverse * row_total / D)[:, None]
    )
    return (grad_resid, jnp.sum(grad_norm * resid * inverse[:, None], axis=0))


def geglu_unit(hidden):
    return jax.nn.gelu(hidden[..., 0, :], approximate=True) * hidden[..., 1, :]


def block_scores(block_query, key_rows, bias_table, sequence, first_row):
    block_rows = block_query.shape[0]
    key_count = key_rows.shape[0]
    products = jnp.einsum(
        "qhd,khd->hqk", block_query, key_rows, preferred_element_type=jnp.float32
    ) * HD ** (-0.5)
    row_ids = first_row + jnp.arange(block_rows, dtype=jnp.int32)
    distance = row_ids[:, None] - jnp.arange(key_count, dtype=jnp.int32)[None, :]
    buckets = bucket_of(jnp.maximum(distance, 0))
    rel_terms = jnp.zeros(products.shape, jnp.float32)
    for bucket_number in range(BUCKETS):
        rel_terms = jnp.where(
            (buckets == bucket_number)[None], bias_table[bucket_number][:, None, None], rel_terms
        )
    own_seq = lax.dynamic_slice_in_dim(sequence, first_row, block_rows, 0)
    visible = (own_seq[:, None] == sequence[None, :]) & (distance >= 0)
    return (jnp.where(visible[None], products + rel_terms, -1e30), buckets)


def attention_forward(queries, key_rows, value_rows, bias_table, sequence, block_rows):

    def one_block(first_row):
        block_query = lax.dynamic_slice_in_dim(queries, first_row, block_rows, 0)
        scores, buckets = block_scores(block_query, key_rows, bias_table, sequence, first_row)
        highest_score = jnp.max(scores, axis=2, keepdims=True)
        exponent = jnp.exp(scores - highest_score)
        denominator = jnp.sum(exponent, axis=2, keepdims=True)
        attn_weights = exponent / denominator
        attended = jnp.einsum(
            "hqk,khd->qhd",
            attn_weights.astype(jnp.bfloat16),
            value_rows,
            preferred_element_type=jnp.float32,
        )
        return (attended.astype(jnp.bfloat16), (highest_score + jnp.log(denominator))[:, :, 0])

    firsts = jnp.arange(queries.shape[0] // block_rows, dtype=jnp.int32) * block_rows
    return lax.map(one_block, firsts)


def attention_backward(
    queries, key_rows, value_rows, grad_heads, log_totals, bias_table, sequence, block_rows
):
    scale = HD ** (-0.5)

    def one_block(state_now, inputs):
        grad_keys, grad_values, grad_table = state_now
        first_row, block_lse = inputs
        block_query = lax.dynamic_slice_in_dim(queries, first_row, block_rows, 0)
        block_grad = lax.dynamic_slice_in_dim(grad_heads, first_row, block_rows, 0)
        scores, buckets = block_scores(block_query, key_rows, bias_table, sequence, first_row)
        attn_weights = jnp.exp(scores - block_lse[:, :, None])
        grad_weights = jnp.einsum(
            "qhd,khd->hqk", block_grad, value_rows, preferred_element_type=jnp.float32
        )
        inner_sum = jnp.sum(attn_weights * grad_weights, axis=2, keepdims=True)
        grad_scores = (attn_weights * (grad_weights - inner_sum)).astype(jnp.bfloat16)
        grad_queries = (
            jnp.einsum("hqk,khd->qhd", grad_scores, key_rows, preferred_element_type=jnp.float32)
            * scale
        )
        grad_keys = (
            grad_keys
            + jnp.einsum(
                "hqk,qhd->khd", grad_scores, block_query, preferred_element_type=jnp.float32
            )
            * scale
        )
        grad_values = grad_values + jnp.einsum(
            "hqk,qhd->khd",
            attn_weights.astype(jnp.bfloat16),
            block_grad,
            preferred_element_type=jnp.float32,
        )
        grad_float = grad_scores.astype(jnp.float32)
        table_terms = jnp.stack(
            [
                jnp.sum(jnp.where((buckets == bucket_number)[None], grad_float, 0.0), axis=(1, 2))
                for bucket_number in range(BUCKETS)
            ]
        )
        return ((grad_keys, grad_values, grad_table + table_terms), grad_queries)

    firsts = jnp.arange(queries.shape[0] // block_rows, dtype=jnp.int32) * block_rows
    start_state = (
        jnp.zeros(key_rows.shape, jnp.float32),
        jnp.zeros(value_rows.shape, jnp.float32),
        jnp.zeros(bias_table.shape, jnp.float32),
    )
    return lax.scan(one_block, start_state, (firsts, log_totals))


def adamw_step(weight, grad, first, second, rate):
    first_new = beta_first * first + (1.0 - beta_first) * grad
    second_new = beta_second * second + (1.0 - beta_second) * grad * grad
    moment = first_new / (1.0 - beta_first**STEP)
    spread = second_new / (1.0 - beta_second**STEP)
    weight_new = weight - rate * (
        moment / (jnp.sqrt(spread) + adam_epsilon) + weight_decay * weight
    )
    return (weight_new, first_new, second_new)


def local(
    layer_in,
    lengths,
    placing,
    routes,
    cotangent,
    norm_gains,
    gain_first,
    gain_second,
    rel_bias,
    bias_first,
    bias_second,
    router,
    router_first,
    router_second,
    qkv_weight,
    qkv_first,
    qkv_second,
    proj_weight,
    proj_first,
    proj_second,
    expert_up,
    up_first,
    up_second,
    expert_down,
    down_first,
    down_second,
):
    tokens_here = layer_in.shape[0]
    dp_count = lax.axis_size("dp")
    experts_all = dp_count // 2
    capacity = min(tokens_here, 5 * TOP * tokens_here // (4 * experts_all))
    slot_count = dp_count * capacity
    block_rows = min(512, tokens_here)
    placement = placing[0]
    resid_one = layer_in[placement].astype(jnp.float32)
    grad_out = cotangent[placement].astype(jnp.float32)
    qkv_all, proj_all = (
        lax.all_gather(qkv_weight.astype(jnp.bfloat16), "dp", axis=1, tiled=True),
        lax.all_gather(proj_weight.astype(jnp.bfloat16), "dp", axis=3, tiled=True),
    )
    qkv_mat = qkv_all.reshape(-1, qkv_all.shape[3], 3, qkv_all.shape[5])
    proj_mat = proj_all.reshape(proj_all.shape[0], proj_all.shape[1], -1)
    norm_one, inverse_one = norm_forward(resid_one, norm_gains[0])
    features_one = by_columns(norm_one.astype(jnp.bfloat16))
    qkv_local = to_rows(
        jnp.einsum("td,dnkh->tnkh", features_one, qkv_mat, preferred_element_type=jnp.float32)
    ).astype(jnp.bfloat16)
    head_count = qkv_local.shape[3] // HD
    queries = qkv_local[:, 0, 0].reshape(tokens_here, head_count, HD)
    key_rows = qkv_local[:, 0, 1].reshape(tokens_here, head_count, HD)
    value_rows = qkv_local[:, 0, 2].reshape(tokens_here, head_count, HD)
    sequence = sequence_ids(lengths[0], tokens_here)
    head_blocks, log_totals = attention_forward(
        queries, key_rows, value_rows, rel_bias, sequence, block_rows
    )
    mixed_heads = head_blocks.reshape(tokens_here, 1, -1)
    mixed_all = by_rows(mixed_heads)
    resid_two = resid_one + to_columns(
        jnp.einsum("tnh,nhd->td", mixed_all, proj_mat, preferred_element_type=jnp.float32)
    )
    norm_two, inverse_two = norm_forward(resid_two, norm_gains[1])
    features_two = norm_two.astype(jnp.bfloat16)
    features_float = features_two.astype(jnp.float32)
    logits = route_sums(jnp.dot(features_float, router, precision=highest))
    flat_routes = routes.reshape(-1)
    route_hits = (flat_routes[:, None] == jnp.arange(experts_all, dtype=jnp.int32)[None, :]).astype(
        jnp.int32
    )
    before = jnp.cumsum(route_hits, axis=0) - route_hits
    slot_place = flat_routes * capacity + jnp.sum(before * route_hits, axis=1)
    route_table = route_hits.astype(jnp.float32).reshape(tokens_here, TOP, experts_all)
    chosen = jnp.sum(route_table * logits[:, None, :], axis=2)
    gate_values = jax.nn.softmax(chosen, axis=1)

    def to_slots(row_values):
        filled = (
            jnp.zeros((experts_all * capacity, row_values.shape[1]), row_values.dtype)
            .at[slot_place]
            .set(row_values)
        )
        return jnp.repeat(filled.reshape(experts_all, capacity, -1), 2, axis=0)

    def from_slots(arrived):
        joined = jnp.sum(arrived.astype(jnp.float32).reshape(experts_all, 2, capacity, -1), axis=1)
        return joined.reshape(experts_all * capacity, -1)[slot_place].reshape(tokens_here, TOP, -1)

    slot_features = move_slots(to_slots(jnp.repeat(by_columns(features_two), TOP, axis=0))).reshape(
        slot_count, -1
    )
    up_local = expert_up[0].astype(jnp.bfloat16)
    down_local = expert_down[0].astype(jnp.bfloat16)
    hidden_own = hidden_share(
        jnp.einsum("sd,dgf->sgf", slot_features, up_local, preferred_element_type=jnp.float32)
    )
    active = hidden_whole(geglu_unit(hidden_own).astype(jnp.bfloat16))
    back_rows = to_columns(jnp.dot(active, down_local, preferred_element_type=jnp.float32)).astype(
        jnp.bfloat16
    )
    expert_rows = from_slots(move_slots(back_rows.reshape(dp_count, capacity, -1)))
    resid_three = resid_two + jnp.sum(gate_values[:, :, None] * expert_rows, axis=1)
    layer_out = jnp.zeros_like(layer_in).at[placement].set(resid_three.astype(jnp.bfloat16))
    grad_gates = route_sums(jnp.sum(grad_out[:, None, :] * expert_rows, axis=2))
    grad_rows = (
        (gate_values[:, :, None] * grad_out[:, None, :])
        .astype(jnp.bfloat16)
        .reshape(tokens_here * TOP, -1)
    )
    slot_grads = move_slots(to_slots(by_columns(grad_rows))).reshape(slot_count, -1)
    grad_down = jnp.einsum("sf,sd->fd", active, slot_grads, preferred_element_type=jnp.float32)
    grad_active = hidden_share(
        jnp.einsum("sd,fd->sf", slot_grads, down_local, preferred_element_type=jnp.float32)
    )
    pulled = jax.vjp(geglu_unit, hidden_own)[1](grad_active)[0]
    grad_hidden = hidden_whole(pulled.astype(jnp.bfloat16))
    grad_up = jnp.einsum(
        "sd,sgf->dgf", slot_features, grad_hidden, preferred_element_type=jnp.float32
    )
    back_slots = to_columns(
        jnp.einsum("sgf,dgf->sd", grad_hidden, up_local, preferred_element_type=jnp.float32)
    ).astype(jnp.bfloat16)
    grad_up_shard = grad_up[None]
    grad_down_shard = grad_down[None]
    grad_features = jnp.sum(
        from_slots(move_slots(back_slots.reshape(dp_count, capacity, -1))), axis=1
    )
    grad_chosen = gate_values * (
        grad_gates - jnp.sum(gate_values * grad_gates, axis=1, keepdims=True)
    )
    grad_logits = jnp.sum(route_table * grad_chosen[:, :, None], axis=1)
    grad_router = jnp.dot(features_float.T, grad_logits, precision=highest)
    grad_features = grad_features + jnp.dot(grad_logits, router.T, precision=highest)
    back_two, grad_gain_two = norm_backward(resid_two, norm_gains[1], inverse_two, grad_features)
    grad_two = grad_out + back_two
    grad_branch = by_columns(grad_two.astype(jnp.bfloat16))
    grad_proj = jnp.einsum(
        "tnh,td->nhd", mixed_all, grad_branch, preferred_element_type=jnp.float32
    )
    grad_heads = to_rows(
        jnp.einsum("td,nhd->tnh", grad_branch, proj_mat, preferred_element_type=jnp.float32)
    ).astype(jnp.bfloat16)
    grad_heads = grad_heads.reshape(tokens_here, head_count, HD)
    (grad_keys, grad_values, grad_bias), grad_blocks = attention_backward(
        queries, key_rows, value_rows, grad_heads, log_totals, rel_bias, sequence, block_rows
    )
    grad_queries = grad_blocks.reshape(tokens_here, -1)
    grad_qkv = jnp.stack(
        [grad_queries, grad_keys.reshape(tokens_here, -1), grad_values.reshape(tokens_here, -1)],
        axis=1,
    )[:, None].astype(jnp.bfloat16)
    grad_qkv_all = by_rows(grad_qkv)
    grad_qkv_mat = jnp.einsum(
        "td,tnkh->dnkh", features_one, grad_qkv_all, preferred_element_type=jnp.float32
    )
    grad_norm_one = to_columns(
        jnp.einsum("tnkh,dnkh->td", grad_qkv_all, qkv_mat, preferred_element_type=jnp.float32)
    )
    back_one, grad_gain_one = norm_backward(resid_one, norm_gains[0], inverse_one, grad_norm_one)
    input_grad = (
        jnp.zeros_like(layer_in).at[placement].set((grad_two + back_one).astype(jnp.bfloat16))
    )
    grad_gains, grad_bias, grad_router = lax.psum(
        (jnp.stack([grad_gain_one, grad_gain_two]), grad_bias, grad_router), "dp"
    )
    grad_qkv_part, grad_proj_part = (
        lax.psum_scatter(
            grad_qkv_mat.reshape((1, dp_count, -1) + grad_qkv_mat.shape[1:]).astype(jnp.bfloat16),
            "dp",
            scatter_dimension=1,
            tiled=True,
        ).astype(jnp.float32),
        lax.psum_scatter(
            grad_proj.reshape(grad_proj.shape[:2] + (1, dp_count, -1)).astype(jnp.bfloat16),
            "dp",
            scatter_dimension=3,
            tiled=True,
        ).astype(jnp.float32),
    )
    gains_new, gains_moment, gains_square = adamw_step(
        norm_gains, grad_gains, gain_first, gain_second, 0.5
    )
    bias_new, bias_moment, bias_square = adamw_step(
        rel_bias, grad_bias, bias_first, bias_second, 1.0
    )
    router_new, router_moment, router_square = adamw_step(
        router, grad_router, router_first, router_second, 2.0 * (2 * D) ** (-0.5)
    )
    qkv_new, qkv_moment, qkv_square = adamw_step(
        qkv_weight, grad_qkv_part, qkv_first, qkv_second, 2.0 * D ** (-0.5)
    )
    proj_new, proj_moment, proj_square = adamw_step(
        proj_weight, grad_proj_part, proj_first, proj_second, 2.0 * (HEADS * HD / 8) ** (-0.5)
    )
    up_new, up_moment, up_square = adamw_step(
        expert_up, grad_up_shard, up_first, up_second, 2.0 * D ** (-0.5)
    )
    down_new, down_moment, down_square = adamw_step(
        expert_down, grad_down_shard, down_first, down_second, 2.0 * (FF / 2) ** (-0.5)
    )
    return (
        layer_out,
        input_grad,
        gains_new,
        gains_moment,
        gains_square,
        bias_new,
        bias_moment,
        bias_square,
        router_new,
        router_moment,
        router_square,
        qkv_new,
        qkv_moment,
        qkv_square,
        qkv_new.astype(jnp.bfloat16),
        proj_new,
        proj_moment,
        proj_square,
        proj_new.astype(jnp.bfloat16),
        up_new,
        up_moment,
        up_square,
        up_new.astype(jnp.bfloat16),
        down_new,
        down_moment,
        down_square,
        down_new.astype(jnp.bfloat16),
    )


def solution(mesh):
    in_specs = (
        P("dp", ("row", "col")),
        P("dp", None),
        P("dp", None),
        P("dp", None),
        P("dp", ("row", "col")),
        P(None, ("row", "col")),
        P(None, ("row", "col")),
        P(None, ("row", "col")),
        P(None, ("row", "col")),
        P(None, ("row", "col")),
        P(None, ("row", "col")),
        P(("row", "col"), None),
        P(("row", "col"), None),
        P(("row", "col"), None),
        P("row", "dp", None, None, None, "col"),
        P("row", "dp", None, None, None, "col"),
        P("row", "dp", None, None, None, "col"),
        P(None, "col", "row", "dp", None),
        P(None, "col", "row", "dp", None),
        P(None, "col", "row", "dp", None),
        P("dp", "row", None, "col"),
        P("dp", "row", None, "col"),
        P("dp", "row", None, "col"),
        P("dp", "col", "row"),
        P("dp", "col", "row"),
        P("dp", "col", "row"),
    )
    out_specs = (
        P("dp", ("row", "col")),
        P("dp", ("row", "col")),
        P(None, ("row", "col")),
        P(None, ("row", "col")),
        P(None, ("row", "col")),
        P(None, ("row", "col")),
        P(None, ("row", "col")),
        P(None, ("row", "col")),
        P(("row", "col"), None),
        P(("row", "col"), None),
        P(("row", "col"), None),
        P("row", "dp", None, None, None, "col"),
        P("row", "dp", None, None, None, "col"),
        P("row", "dp", None, None, None, "col"),
        P("row", "dp", None, None, None, "col"),
        P(None, "col", "row", "dp", None),
        P(None, "col", "row", "dp", None),
        P(None, "col", "row", "dp", None),
        P(None, "col", "row", "dp", None),
        P("dp", "row", None, "col"),
        P("dp", "row", None, "col"),
        P("dp", "row", None, "col"),
        P("dp", "row", None, "col"),
        P("dp", "col", "row"),
        P("dp", "col", "row"),
        P("dp", "col", "row"),
        P("dp", "col", "row"),
    )
    return jax.shard_map(local, mesh=mesh, in_specs=in_specs, out_specs=out_specs, check_vma=False)
```

profile of v0, /device:TPU:0, one launch (start us, length us, event | category | flops | bytes accessed | tf_op | source)
XLA Modules:
  0.0 1616.6 jit_solution(192061183768046610)
XLA Ops:
  25.1 32.6 %all-gather.12.cloned.1.call-done = bf16[1,8,64,2,3,256]{5,2,4,3,0,1:T(8,128)(2,1)} async-done(((bf16[1,1,64,2,3,256]{5,2,4,3,0,1:T(8,128)(2,1)}), bf16[1,8,64,2,3,256]{5,2,4,3,0,1:T(8,128)(2,1)}) %all-gather.12.cloned.1.call-update) | async-done | bytes 1572880 | tf_op jit(solution)/shard_map/all_gather | solution.py:241
  59.3 20.7 %all-gather.10.cloned.1.call-done = bf16[1024,512]{1,0:T(8,128)(2,1)} async-done(((bf16[1024,256]{1,0:T(8,128)(2,1)}), bf16[1024,512]{1,0:T(8,128)(2,1)}) %all-gather.10.cloned.1.call-update) | async-done | bytes 1048592 | tf_op jit(solution)/shard_map/all_gather | solution.py:38
  104.0 120.8 %while.29 = (s32[]{:T(128)}, bf16[2,512,4,64]{1,3,2,0:T(8,128)(2,1)}, f32[2,4,512]{2,1,0:T(4,128)S(1)}, s32[2]{0:T(128)S(1)}, s32[1024]{0:T(1024)S(1)}, /*index=...) while((s32[]{:T(128)}, ...), condition=%wide.region_8.9_spmd, body=%wide.region_5.8_spmd.sunk | while | flops 668596736 | bytes 94978264 | solution.py:137
  124.0 32.0 %fusion.244 = (f32[4,512]{1,0:T(4,128)S(1)}, f32[4,512,1024]{2,1,0:T(8,128)}) fusion(f32[4]{0:T(128)S(1)} %get-tuple-element.955, pred[512,1024]{1,0:T(8,128)(4,1)} %get-tuple-element.956, f32[4]{0:T(128)S(1)} %get-tuple-element.957, pred[512,1024]{1,0:T(8,128)(4,1)} %get-tuple-element.958, f32[4]{0:T(128)S(1)} %get-tuple-element.959, ...), kind=kOutput, calls=%fused_computation.443.clone.1 | convolution fusion | flops 343930880 | bytes 26485252 | tf_op jit(solution)/shard_map/while/body/eval_jaxpr/qhd,khd->hqk/dot_general | solution.py:103
  184.1 32.0 %fusion.244 = (f32[4,512]{1,0:T(4,128)S(1)}, f32[4,512,1024]{2,1,0:T(8,128)}) fusion(f32[4]{0:T(128)S(1)} %get-tuple-element.955, pred[512,1024]{1,0:T(8,128)(4,1)} %get-tuple-element.956, f32[4]{0:T(128)S(1)} %get-tuple-element.957, pred[512,1024]{1,0:T(8,128)(4,1)} %get-tuple-element.958, f32[4]{0:T(128)S(1)} %get-tuple-element.959, ...), kind=kOutput, calls=%fused_computation.443.clone.1 | convolution fusion | flops 343930880 | bytes 26485252 | tf_op jit(solution)/shard_map/while/body/eval_jaxpr/qhd,khd->hqk/dot_general | solution.py:103
  228.4 31.8 %all_gather.33 = bf16[2,256,1,8,64]{1,4,3,0,2:T(8,128)(2,1)S(1)} all-gather(bf16[2,256,1,1,64]{1,4,3,0,2:T(8,128)(2,1)S(1)} %bitcast_convert_fusion), channel_id=1, replica_groups=mesh['dp'=8,'row'=2,'col'=2] {'dp'}, dimensions={3}, use_global_device_ids=true | all-gather | bytes 589824 | tf_op jit(solution)/shard_map/all_gather | solution.py:242
  273.6 22.9 %reduce-scatter.15.cloned.1.call-done = f32[1024,256]{1,0:T(8,128)} async-done(((f32[1024,512]{1,0:T(8,128)}), f32[1024,256]{1,0:T(8,128)}) %reduce-scatter.15.cloned.1.call-update) | async-done | bytes 1048592 | tf_op jit(solution)/shard_map/reduce_scatter | solution.py:42
  320.1 30.3 %all-gather.20.cloned.1.call-done = bf16[2048,512]{1,0:T(8,128)(2,1)} async-done(((bf16[2048,256]{1,0:T(8,128)(2,1)}), bf16[2048,512]{1,0:T(8,128)(2,1)}) %all-gather.20.cloned.1.call-update) | async-done | bytes 2097168 | tf_op jit(solution)/shard_map/all_gather | solution.py:38
  373.1 114.8 %all-to-all-done.2 = bf16[8,640,512]{2,1,0:T(8,128)(2,1)} async-done(((bf16[8,640,512]{2,1,0:T(8,128)(2,1)}), bf16[8,640,512]{2,1,0:T(8,128)(2,1)}, u32[]{:S(2)}, u32[]{:S(2)}) %all-to-all-start.2) | async-done | bytes 5242912 | tf_op jit(solution)/shard_map/all_to_all | solution.py:66
  522.0 119.7 %all_to_all.20 = bf16[8,640,512]{2,1,0:T(8,128)(2,1)S(1)} all-to-all(bf16[8,640,512]{2,1,0:T(8,128)(2,1)S(1)} %bitcast.500), channel_id=1, replica_groups=mesh['dp'=8,'row'=2,'col'=2] {'dp'}, dimensions={0} | all-to-all | bytes 10485760 | tf_op jit(solution)/shard_map/all_to_all | solution.py:66
  657.9 37.5 %reduce-scatter.17.cloned.1.call-done = f32[2560,2,704]{0,2,1:T(8,128)} async-done(((f32[5120,2,704]{0,2,1:T(8,128)}), f32[2560,2,704]{0,2,1:T(8,128)}) %reduce-scatter.17.cloned.1.call-update) | async-done | bytes 14417936 | tf_op jit(solution)/shard_map/reduce_scatter | solution.py:58
  773.5 110.5 %reduce-scatter.19.cloned.1.call-done = f32[5120,256]{1,0:T(8,128)} async-done(((f32[5120,512]{1,0:T(8,128)}), f32[5120,256]{1,0:T(8,128)}) %reduce-scatter.19.cloned.1.call-update) | async-done | bytes 5242896 | tf_op jit(solution)/shard_map/reduce_scatter | solution.py:42
  893.7 114.4 %reduce-scatter.23.cloned.1.call-done = f32[5120,256]{1,0:T(8,128)} async-done(((f32[5120,512]{1,0:T(8,128)}), f32[5120,256]{1,0:T(8,128)}) %reduce-scatter.23.cloned.1.call-update) | async-done | bytes 5242896 | tf_op jit(solution)/shard_map/reduce_scatter | solution.py:42
  1048.7 28.8 %all-to-all-done.3 = bf16[8,640,256]{2,1,0:T(8,128)(2,1)} async-done(((bf16[8,640,256]{2,1,0:T(8,128)(2,1)}), bf16[8,640,256]{2,1,0:T(8,128)(2,1)}, u32[]{:S(2)}, u32[]{:S(2)}) %all-to-all-start.3) | async-done | bytes 2621472 | tf_op jit(solution)/shard_map/all_to_all | solution.py:66
  1108.2 21.0 %all-gather.24.cloned.1.call-done = bf16[1024,512]{1,0:T(8,128)(2,1)} async-done(((bf16[1024,256]{1,0:T(8,128)(2,1)}), bf16[1024,512]{1,0:T(8,128)(2,1)}) %all-gather.24.cloned.1.call-update) | async-done | bytes 1048592 | tf_op jit(solution)/shard_map/all_gather | solution.py:38
  1144.6 228.4 %while.30 = (s32[]{:T(128)}, f32[1024,4,64]{0,2,1:T(8,128)S(1)}, f32[1024,4,64]{0,2,1:T(8,128)}, f32[32,4]{0,1:T(4,128)S(1)}, bf16[2,512,4,64]{1,3,2,0:T(8,128)(...) while((s32[]{:T(128)}, f32[1024,4,64]{0,2,1:T(8,128)S(1)}, ...), condition=%wide.region_71.72_spmd.clone, body=%wide.region_37.71_spmd.clone.sunk | while | flops 1615723264 | bytes 274789344 | solution.py:189
  1166.1 32.8 %multiply_reduce_fusion.9 = (f32[4,512]{1,0:T(4,128)S(1)}, f32[4,512,1024]{2,1,0:T(8,128)S(1)}) fusion(f32[4,512,1024]{2,1,0:T(8,128)S(1)} %fusion.257, f32[4,512]{1,0:T(4,128)S(1)} %dynamic-slice_bitcast_fusion.2, f32[4]{0:T(128)S(1)} %get-tuple-element.1053, pred[512,1024]{1,0:T(8,128)(4,1)} %get-tuple-element.1054, ...), kind=kOutput, calls=%fused_computation.170.clone.1 | convolution fusion | flops 348125184 | bytes 34882052 | tf_op jit(solution)/shard_map/while/body/eval_jaxpr/qhd,khd->hqk/dot_general | solution.py:103
  1199.1 30.9 %fusion.258 = (f32[4]{0:T(128)S(1)}, f32[4]{0:T(128)S(1)}, f32[4]{0:T(128)S(1)}, f32[4]{0:T(128)S(1)}, f32[4]{0:T(128)S(1)}, /*index=5*/f32[4]{0:T(128)S(1)}, f3...) fusion(pred[512,1024]{1,0:T(8,128)(4,1)} %get-tuple-element.103, ...), kind=kLoop, calls=%fused_computation.168.clone.1 | loop fusion | flops 83886016 | bytes 30417184 | tf_op jit(solution)/shard_map/while/body/eval_jaxpr/reduce_sum | solution.py:177
  1280.0 32.8 %multiply_reduce_fusion.9 = (f32[4,512]{1,0:T(4,128)S(1)}, f32[4,512,1024]{2,1,0:T(8,128)S(1)}) fusion(f32[4,512,1024]{2,1,0:T(8,128)S(1)} %fusion.257, f32[4,512]{1,0:T(4,128)S(1)} %dynamic-slice_bitcast_fusion.2, f32[4]{0:T(128)S(1)} %get-tuple-element.1053, pred[512,1024]{1,0:T(8,128)(4,1)} %get-tuple-element.1054, ...), kind=kOutput, calls=%fused_computation.170.clone.1 | convolution fusion | flops 348125184 | bytes 34882052 | tf_op jit(solution)/shard_map/while/body/eval_jaxpr/qhd,khd->hqk/dot_general | solution.py:103
  1313.0 30.9 %fusion.258 = (f32[4]{0:T(128)S(1)}, f32[4]{0:T(128)S(1)}, f32[4]{0:T(128)S(1)}, f32[4]{0:T(128)S(1)}, f32[4]{0:T(128)S(1)}, /*index=5*/f32[4]{0:T(128)S(1)}, f3...) fusion(pred[512,1024]{1,0:T(8,128)(4,1)} %get-tuple-element.103, ...), kind=kLoop, calls=%fused_computation.168.clone.1 | loop fusion | flops 83886016 | bytes 30417184 | tf_op jit(solution)/shard_map/while/body/eval_jaxpr/reduce_sum | solution.py:177
  1441.4 28.7 %all-reduce.6.cloned.1.call-done = bf16[2,256,1,8,64]{1,4,3,0,2:T(8,128)(2,1)} async-done(((bf16[2,256,1,8,64]{1,4,3,0,2:T(8,128)(2,1)}), bf16[2,256,1,8,64]{1,4,3,0,2:T(8,128)(2,1)}) %all-reduce.6.cloned.1.call-update) | async-done | bytes 524304
  1472.6 65.0 %reduce-scatter.29.cloned.1.call-done = bf16[1,1,64,2,3,256]{5,2,4,3,0,1:T(8,128)(2,1)} async-done(((bf16[1,8,64,2,3,256]{5,2,4,3,0,1:T(8,128)(2,1)}), bf16[1,1,64,2,3,256]{5,2,4,3,0,1:T(8,128)(2,1)}) %reduce-scatter.29.cloned.1.call-update) | async-done | bytes 196624 | tf_op jit(solution)/shard_map/reduce_scatter | solution.py:368
  1543.3 27.4 %reduce-scatter.27.cloned.1.call-done = f32[1024,256]{1,0:T(8,128)} async-done(((f32[1024,512]{1,0:T(8,128)}), f32[1024,256]{1,0:T(8,128)}) %reduce-scatter.27.cloned.1.call-update) | async-done | bytes 1048592 | tf_op jit(solution)/shard_map/reduce_scatter | solution.py:42
  1578.9 21.9 %all-reduce.3 = (f32[2,256]{1,0:T(2,128)S(1)}, f32[32,4]{0,1:T(4,128)S(1)}, f32[256,4]{0,1:T(4,128)S(1)}) all-reduce(f32[2,256]{1,0:T(2,128)S(1)} %pad_maximum_fusion.1, f32[32,4]{0,1:T(4,128)S(1)} %copy-done.66, f32[256,4]{0,1:T(4,128)S(1)} %copy-done.81), channel_id=1, replica_groups=mesh['dp'=8,'row'=2,'col'=2] {'dp'}, use_global_device_ids=true, to_apply=%region_78.79 | all-reduce | flops 1664 | bytes 13312 | tf_op jit(solution)/shard_map/psum | solution.py:364
  (535 shorter events, 571.9 us)
Async XLA Ops:
  7.2 50.5 %all-gather.12.cloned.1.call-start = ((), (), s32[]{:S(2)}) async-start(), calls=%async_computation.14 | async-start | bytes 1769472 | tf_op jit(solution)/shard_map/all_gather | solution.py:241
  9.0 70.9 %all-gather.10.cloned.1.call-start = ((), (), s32[]{:S(2)}) async-start(), calls=%async_computation.13 | async-start | bytes 1572864 | tf_op jit(solution)/shard_map/all_gather | solution.py:38
  25.1 75.3 %reduce-scatter.13.cloned.1.call-start = ((), (), s32[]{:S(2)}) async-start(), calls=%async_computation.15 | async-start | bytes 9437184 | tf_op jit(solution)/shard_map/reduce_scatter | solution.py:54
  85.7 174.5 %all-gather.14.cloned.1.call-start = ((), (), s32[]{:S(2)}) async-start(), calls=%async_computation.16 | async-start | bytes 1572864 | tf_op jit(solution)/shard_map/all_gather | solution.py:48
  228.3 68.2 %reduce-scatter.15.cloned.1.call-start = ((), (), s32[]{:S(2)}) async-start(), calls=%async_computation.17 | async-start | bytes 3145728 | tf_op jit(solution)/shard_map/reduce_scatter | solution.py:42
  263.7 86.6 %all-gather.20.cloned.1.call-start = ((), (), s32[]{:S(2)}) async-start(), calls=%async_computation.22 | async-start | bytes 3145728 | tf_op jit(solution)/shard_map/all_gather | solution.py:38
  267.8 750.2 %copy-start.37 = (bf16[1024,256]{1,0:T(8,128)(2,1)}, bf16[1024,256]{1,0:T(8,128)(2,1)S(1)}, u32[]{:S(2)}) copy-start(bf16[1024,256]{1,0:T(8,128)(2,1)S(1)} %gather_fusion.2) | copy-start | bytes 1572868
  304.3 802.7 %copy-start.61 = (f32[1024]{0:T(1024)}, f32[1024]{0:T(1024)S(1)}, u32[]{:S(2)}) copy-start(f32[1024]{0:T(1024)S(1)} %add_rsqrt_fusion) | copy-start | bytes 12292
  366.6 121.3 %all-to-all-start.2 = ((bf16[8,640,512]{2,1,0:T(8,128)(2,1)}), bf16[8,640,512]{2,1,0:T(8,128)(2,1)}, u32[]{:S(2)}, u32[]{:S(2)}) async-start(bf16[8,640,512]{2,1,0:T(8,128)(2,1)} %bitcast.499), calls=%async_computation.6 | async-start | bytes 10485760 | tf_op jit(solution)/shard_map/all_to_all | solution.py:66
  372.2 127.7 %all-gather.16.cloned.1.call-start = ((), (), s32[]{:S(2)}) async-start(), calls=%async_computation.18 | async-start | bytes 1572864 | tf_op jit(solution)/shard_map/all_gather | solution.py:38
  372.9 285.0 %reduce-scatter.21.cloned.1.call-start = ((), (), s32[]{:S(2)}) async-start(), calls=%async_computation.23 | async-start | bytes 21626880 | tf_op jit(solution)/shard_map/reduce_scatter | solution.py:58
  499.8 195.6 %reduce-scatter.17.cloned.1.call-start = ((), (), s32[]{:S(2)}) async-start(), calls=%async_computation.19 | async-start | bytes 43253760 | tf_op jit(solution)/shard_map/reduce_scatter | solution.py:58
  657.4 71.8 %all-gather.18.cloned.1.call-start = ((), (), s32[]{:S(2)}) async-start(), calls=%async_computation.20 | async-start | bytes 10813440 | tf_op jit(solution)/shard_map/all_gather | solution.py:62
  709.7 49.0 %all-gather.22.cloned.1.call-start = ((), (), s32[]{:S(2)}) async-start(), calls=%async_computation.24 | async-start | bytes 21626880 | tf_op jit(solution)/shard_map/all_gather | solution.py:62
  719.4 164.6 %reduce-scatter.19.cloned.1.call-start = ((), (), s32[]{:S(2)}) async-start(), calls=%async_computation.21 | async-start | bytes 15728640 | tf_op jit(solution)/shard_map/reduce_scatter | solution.py:42
  743.6 264.6 %reduce-scatter.23.cloned.1.call-start = ((), (), s32[]{:S(2)}) async-start(), calls=%async_computation.25 | async-start | bytes 15728640 | tf_op jit(solution)/shard_map/reduce_scatter | solution.py:42
  888.2 124.2 %all-to-all-start.1 = ((bf16[8,640,256]{2,1,0:T(8,128)(2,1)}), bf16[8,640,256]{2,1,0:T(8,128)(2,1)}, u32[]{:S(2)}, u32[]{:S(2)}) async-start(bf16[8,640,256]{2,1,0:T(8,128)(2,1)} %bitcast.505), calls=%async_computation.5 | async-start | bytes 5242880 | tf_op jit(solution)/shard_map/all_to_all | solution.py:66
  1012.4 65.1 %all-to-all-start.3 = ((bf16[8,640,256]{2,1,0:T(8,128)(2,1)}), bf16[8,640,256]{2,1,0:T(8,128)(2,1)}, u32[]{:S(2)}, u32[]{:S(2)}) async-start(bf16[8,640,256]{2,1,0:T(8,128)(2,1)} %bitcast.504), calls=%async_computation.9 | async-start | bytes 5242880 | tf_op jit(solution)/shard_map/all_to_all | solution.py:66
  1017.9 111.3 %all-gather.24.cloned.1.call-start = ((), (), s32[]{:S(2)}) async-start(), calls=%async_computation.26 | async-start | bytes 1572864 | tf_op jit(solution)/shard_map/all_gather | solution.py:38
  1108.2 34.1 %reduce-scatter.25.cloned.1.call-start = ((), (), s32[]{:S(2)}) async-start(), calls=%async_computation.27 | async-start | bytes 3145728 | tf_op jit(solution)/shard_map/reduce_scatter | solution.py:54
  1132.5 260.3 %all-gather.26.cloned.1.call-start = ((), (), s32[]{:S(2)}) async-start(), calls=%async_computation.28 | async-start | bytes 4718592 | tf_op jit(solution)/shard_map/all_gather | solution.py:48
  1379.4 90.7 %all-reduce.6.cloned.1.call-start = ((), (), s32[]{:S(2)}) async-start(), calls=%async_computation.31 | async-start | bytes 1048576
  1382.7 155.0 %reduce-scatter.29.cloned.1.call-start = ((), (), s32[]{:S(2)}) async-start(), calls=%async_computation.30 | async-start | bytes 1769472 | tf_op jit(solution)/shard_map/reduce_scatter | solution.py:368
  1397.9 172.8 %reduce-scatter.27.cloned.1.call-start = ((), (), s32[]{:S(2)}) async-start(), calls=%async_computation.29 | async-start | bytes 3145728 | tf_op jit(solution)/shard_map/reduce_scatter | solution.py:42
  (122 other events, 3660.1 us)
Sparse Core Ops, SparseCore 0:
  10.8 46.8 all-gather.11
  59.8 20.0 all-gather.9
  85.8 14.5 reduce-scatter.12
  228.4 10.1 all-gather.13
  263.9 32.6 reduce-scatter.14
  317.1 33.2 all-gather.19
  375.1 21.7 all-gather.15
  500.0 21.8 reduce-scatter.20
  657.6 37.8 reduce-scatter.16
  709.8 19.3 all-gather.17
  730.8 27.8 all-gather.21
  760.9 123.0 reduce-scatter.18
  886.3 121.8 reduce-scatter.22
  1108.3 20.8 all-gather.23
  1132.6 9.6 reduce-scatter.24
  1379.5 13.2 all-gather.25
  1396.5 73.5 all-reduce.5
  1473.4 64.2 reduce-scatter.28
  1540.0 30.6 reduce-scatter.26
where the time goes:
time: 1620 us
  waiting for transfers between devices  714 us (44%)
  matrix products  263 us (16%)
  other arithmetic  261 us (16%)
  blocking collectives  217 us (13%)
  local copies, waits for them, and re-layouts  119 us (7%)
  starting transfers between devices  18.1 us (1%)
    reduce_scatter x4, waiting for transfers between devices, to_columns(): return lax.psum_scatter(values, 'col', scatter_dimension=1, tiled=True)  275 us
    all_to_all x3, waiting for transfers between devices, move_slots(): return lax.all_to_all(values, 'dp', split_axis=0, concat_axis=0, tiled=True)  144 us
    dot_general x4, matrix products, block_scores(): jnp.einsum('qhd,khd->hqk', block_query, key_rows, preferred_element_type=...  130 us
    all_to_all x1, blocking collectives, move_slots(): return lax.all_to_all(values, 'dp', split_axis=0, concat_axis=0, tiled=True)  120 us
    reduce_sum x4, other arithmetic, one_block(): jnp.sum(jnp.where((buckets == bucket_number)[None], grad_float, 0.0), axi...  95.9 us
    all_gather x4, waiting for transfers between devices, by_columns(): return lax.all_gather(values, 'col', axis=1, tiled=True)  72 us
    and x4, other arithmetic, block_scores(): visible = (own_seq[:, None] == sequence[None, :]) & (distance >= 0)  65.7 us
    reduce_scatter x1, waiting for transfers between devices, local(): lax.psum_scatter(grad_qkv_mat.reshape((1, dp_count, -1) + grad_qkv_mat.sh...  65 us
  transfers between devices with their start and end apart: 22, of which 18 were waited for; matrix products, arithmetic and copies ran while one was open for 12% of the time, Pallas kernels for 0%

commit v1 on v0

v1 whole, which is shorter than its diff:
```python
import functools

import jax
import jax.numpy as jnp
import numpy as np
from jax import lax
from jax.experimental import pallas as pl
from jax.experimental.pallas import tpu as pltpu
from jax.sharding import Mesh, PartitionSpec as P

D = 1024
HEADS = 16
FF = 2816
TOP = 2
STEP = 5
beta_first = 0.5
beta_second = 0.5
adam_epsilon = 1e-08
weight_decay = 0.01
highest = lax.Precision.HIGHEST
EXTRA = 16
HD = 64
BUCKETS = 32
LONGEST = 512
TILE = 256
norm_epsilon = 1e-06
hidden_score = -1e30
bucket_edges = np.floor(16.0 * 2.0 ** (np.arange(16) * 0.375)).astype(np.int32)
f32 = jnp.float32
bf16 = jnp.bfloat16
MIB = 1 << 20


def dot_nn(a, b):
    return lax.dot_general(a, b, (((1,), (0,)), ((), ())), preferred_element_type=f32)


def dot_nt(a, b):
    return lax.dot_general(a, b, (((1,), (1,)), ((), ())), preferred_element_type=f32)


def dot_tn(a, b):
    return lax.dot_general(a, b, (((0,), (0,)), ((), ())), preferred_element_type=f32)


def tile_reach(tokens):
    return min(tokens // TILE, (LONGEST - 1 + TILE - 1) // TILE + 1)


def toeplitz_places(tokens):
    reach = tile_reach(tokens)
    m = np.arange(2 * TILE)
    base = np.where(m < TILE, -m, 2 * TILE - m)
    distance = np.arange(reach)[:, None] * TILE + base[None, :]
    clipped = np.maximum(distance, 0)
    buckets = np.where(
        clipped < 16, clipped, 15 + (clipped[..., None] >= bucket_edges).sum(-1)
    )
    return (distance, buckets)


def bias_vectors(rel_bias, tokens):
    distance, buckets = toeplitz_places(tokens)
    table = jnp.asarray((buckets[..., None] == np.arange(BUCKETS)).astype(np.float32))
    values = jnp.einsum("dmb,bh->hdm", table, rel_bias, precision=lax.Precision.HIGHEST)
    values = jnp.where(jnp.asarray(distance < 0)[None], hidden_score, values)
    return values.reshape(-1, 2 * TILE)


def bias_gradient(vectors, head_count, tokens):
    distance, buckets = toeplitz_places(tokens)
    table = ((buckets[..., None] == np.arange(BUCKETS)) & (distance >= 0)[..., None]).astype(np.float32)
    return jnp.einsum(
        "dmb,hdm->bh",
        jnp.asarray(table),
        vectors.reshape(head_count, distance.shape[0], 2 * TILE),
        precision=lax.Precision.HIGHEST,
    )


def fill_bias(vector_ref, bias):
    for i in range(bias.shape[0]):
        wide = jnp.broadcast_to(vector_ref[i : i + 1, :], (TILE, 2 * TILE))
        bias[i] = pltpu.roll(wide, 0, 1, stride=1, stride_axis=0)[:, :TILE]


def head_lanes(shape, head):
    return lax.broadcasted_iota(jnp.int32, shape, 1) // HD == head


def attention_forward_kernel(
    x_ref, gain_ref, weight_ref, place_row, place_col, start_ref, vector_ref,
    first_ref, qkv_ref, attended_ref, lse_ref, bias, placed_out,
):
    quarters, tokens, part = x_ref.shape
    width = quarters * part
    hc = weight_ref.shape[1] // 3
    head_count = hc // HD
    reach = bias.shape[0] // head_count
    fill_bias(vector_ref, bias)
    squares = jnp.zeros((tokens, 1), f32)
    for q in range(quarters):
        v = x_ref[q].astype(f32)
        squares = squares + jnp.sum(v * v, axis=1, keepdims=True)
    inverse = lax.rsqrt(squares / width + norm_epsilon)
    total = jnp.zeros((tokens, 3 * hc), f32)
    for q in range(quarters):
        first = (x_ref[q].astype(f32) * inverse * gain_ref[q]).astype(bf16)
        first_ref[q] = first
        total = total + dot_nn(first, weight_ref[q * part : (q + 1) * part, :])
    to_placed = jnp.where(
        place_col[...] == lax.broadcasted_iota(jnp.int32, (tokens, tokens), 1), 1.0, 0.0
    ).astype(bf16)
    scale = jnp.where(
        lax.broadcasted_iota(jnp.int32, (1, 3 * hc), 1) < hc, HD ** (-0.5), 1.0
    )
    qkv_ref[...] = dot_nn(to_placed, (total * scale).astype(bf16)).astype(bf16)
    for a in range(tokens // TILE):
        rows = slice(a * TILE, (a + 1) * TILE)
        blocks = range(max(0, a - reach + 1), a + 1)
        starts = start_ref[rows, :]
        visible = [
            b * TILE + lax.broadcasted_iota(jnp.int32, (TILE, TILE), 1) >= starts for b in blocks
        ]

        def one_head(head, carry):
            out, lse = carry
            mine = head_lanes((TILE, hc), head)
            query = jnp.where(mine, qkv_ref[rows, :hc], 0)
            scores = []
            for b, seen in zip(blocks, visible):
                s = dot_nt(query, qkv_ref[b * TILE : (b + 1) * TILE, hc : 2 * hc])
                scores.append(jnp.where(seen, s + bias[head * reach + a - b], hidden_score))
            top = functools.reduce(jnp.maximum, [jnp.max(s, axis=1, keepdims=True) for s in scores])
            exps = [jnp.exp(s - top) for s in scores]
            denominator = functools.reduce(jnp.add, [jnp.sum(e, axis=1, keepdims=True) for e in exps])
            share = 1.0 / denominator
            value = jnp.zeros((TILE, hc), f32)
            for b, e in zip(blocks, exps):
                value = value + dot_nn(
                    (e * share).astype(bf16), qkv_ref[b * TILE : (b + 1) * TILE, 2 * hc :]
                )
            lane = lax.broadcasted_iota(jnp.int32, (TILE, 128), 1)
            return (
                jnp.where(mine, value, out),
                jnp.where(lane == head, top + jnp.log(denominator), lse),
            )

        out, lse = lax.fori_loop(
            0, head_count, one_head, (jnp.zeros((TILE, hc), f32), jnp.zeros((TILE, 128), f32))
        )
        placed_out[rows, :] = out.astype(bf16)
        lse_ref[rows, :] = lse
    to_given = jnp.where(
        place_row[...] == lax.broadcasted_iota(jnp.int32, (tokens, tokens), 0), 1.0, 0.0
    ).astype(bf16)
    attended_ref[...] = dot_nn(to_given, placed_out[...]).astype(bf16)


def vmem():
    return pl.BlockSpec(memory_space=pltpu.VMEM)


def attention_forward(x, gain, weight, place_row, place_col, starts, vectors):
    quarters, tokens, part = x.shape
    hc = weight.shape[1] // 3
    return pl.pallas_call(
        attention_forward_kernel,
        out_shape=(
            jax.ShapeDtypeStruct(x.shape, bf16),
            jax.ShapeDtypeStruct((tokens, 3 * hc), bf16),
            jax.ShapeDtypeStruct((tokens, hc), bf16),
            jax.ShapeDtypeStruct((tokens, 128), f32),
        ),
        in_specs=[vmem()] * 7,
        out_specs=(vmem(),) * 4,
        scratch_shapes=[
            pltpu.VMEM((vectors.shape[0], TILE, TILE), f32),
            pltpu.VMEM((tokens, hc), bf16),
        ],
        compiler_params=pltpu.CompilerParams(vmem_limit_bytes=48 * MIB),
        name="attention_forward",
    )(x, gain, weight, place_row, place_col, starts, vectors)


def attention_backward_kernel(
    branch_ref, proj_ref, qkv_ref, lse_ref, attended_ref, first_ref, weight_ref,
    place_row, place_col, start_ref, vector_ref,
    dfirst_ref, dweight_ref, dproj_ref, dvector_ref,
    bias, dbias, grad_ref, dqkv, dkv,
):
    quarters, tokens, part = branch_ref.shape
    hc = weight_ref.shape[1] // 3
    head_count = hc // HD
    reach = bias.shape[0] // head_count
    fill_bias(vector_ref, bias)
    dbias[...] = jnp.zeros_like(dbias)
    dkv[...] = jnp.zeros_like(dkv)
    total = jnp.zeros((tokens, hc), f32)
    for q in range(quarters):
        total = total + dot_nn(branch_ref[q], proj_ref[q * part : (q + 1) * part, :])
        dproj_ref[q * part : (q + 1) * part, :] = dot_tn(branch_ref[q], attended_ref[...]).astype(bf16)
    to_placed = jnp.where(
        place_col[...] == lax.broadcasted_iota(jnp.int32, (tokens, tokens), 1), 1.0, 0.0
    ).astype(bf16)
    grad_ref[...] = dot_nn(to_placed, total.astype(bf16)).astype(bf16)
    for a in range(tokens // TILE):
        rows = slice(a * TILE, (a + 1) * TILE)
        blocks = range(max(0, a - reach + 1), a + 1)
        starts = start_ref[rows, :]
        visible = [
            b * TILE + lax.broadcasted_iota(jnp.int32, (TILE, TILE), 1) >= starts for b in blocks
        ]

        def one_head(head, dquery):
            mine = head_lanes((TILE, hc), head)
            query = jnp.where(mine, qkv_ref[rows, :hc], 0)
            grad = jnp.where(mine, grad_ref[rows, :], 0)
            lane = lax.broadcasted_iota(jnp.int32, (TILE, 128), 1)
            lse = jnp.sum(jnp.where(lane == head, lse_ref[rows, :], 0.0), axis=1, keepdims=True)
            probs, dprobs = [], []
            inner = jnp.zeros((TILE, 1), f32)
            for b, seen in zip(blocks, visible):
                keys = slice(b * TILE, (b + 1) * TILE)
                s = dot_nt(query, qkv_ref[keys, hc : 2 * hc]) + bias[head * reach + a - b]
                p = jnp.where(seen, jnp.exp(s - lse), 0.0)
                d = dot_nt(grad, qkv_ref[keys, 2 * hc :])
                inner = inner + jnp.sum(p * d, axis=1, keepdims=True)
                probs.append(p)
                dprobs.append(d)
            for b, p, d in zip(blocks, probs, dprobs):
                keys = slice(b * TILE, (b + 1) * TILE)
                ds = p * (d - inner)
                place = head * reach + a - b
                dbias[place] = dbias[place] + ds
                low = ds.astype(bf16)
                dquery = dquery + dot_nn(low, jnp.where(mine, qkv_ref[keys, hc : 2 * hc], 0))
                dkv[keys, :hc] = dkv[keys, :hc] + dot_tn(low, query)
                dkv[keys, hc:] = dkv[keys, hc:] + dot_tn(p.astype(bf16), grad)
            return dquery

        dquery = lax.fori_loop(0, head_count, one_head, jnp.zeros((TILE, hc), f32))
        dqkv[rows, :hc] = (dquery * HD ** (-0.5)).astype(bf16)
    dqkv[:, hc:] = dkv[...].astype(bf16)
    for i in range(dbias.shape[0]):
        wide = jnp.concatenate([dbias[i], jnp.zeros((TILE, TILE), f32)], axis=1)
        level = wide[:8]
        for g in range(8, TILE, 8):
            level = level + pltpu.roll(wide[g : g + 8], 2 * TILE - g, 1)
        row = level[:1]
        for s in range(1, 8):
            row = row + pltpu.roll(level[s : s + 1], 2 * TILE - s, 1)
        dvector_ref[i : i + 1, :] = row
    to_given = jnp.where(
        place_row[...] == lax.broadcasted_iota(jnp.int32, (tokens, tokens), 0), 1.0, 0.0
    ).astype(bf16)
    given = dot_nn(to_given, dqkv[...]).astype(bf16)
    for q in range(quarters):
        dims = slice(q * part, (q + 1) * part)
        dfirst_ref[q] = dot_nt(given, weight_ref[dims, :]).astype(bf16)
        dweight_ref[dims, :] = dot_tn(first_ref[q], given).astype(bf16)


def attention_backward(branch, proj, qkv, lse, attended, first, weight, place_row, place_col, starts, vectors):
    quarters, tokens, part = branch.shape
    hc = weight.shape[1] // 3
    return pl.pallas_call(
        attention_backward_kernel,
        out_shape=(
            jax.ShapeDtypeStruct(branch.shape, bf16),
            jax.ShapeDtypeStruct(weight.shape, bf16),
            jax.ShapeDtypeStruct(proj.shape, bf16),
            jax.ShapeDtypeStruct(vectors.shape, f32),
        ),
        in_specs=[vmem()] * 11,
        out_specs=(vmem(),) * 4,
        scratch_shapes=[
            pltpu.VMEM((vectors.shape[0], TILE, TILE), f32),
            pltpu.VMEM((vectors.shape[0], TILE, TILE), f32),
            pltpu.VMEM((tokens, hc), bf16),
            pltpu.VMEM((tokens, 3 * hc), bf16),
            pltpu.VMEM((tokens, 2 * hc), f32),
        ],
        compiler_params=pltpu.CompilerParams(vmem_limit_bytes=56 * MIB),
        name="attention_backward",
    )(branch, proj, qkv, lse, attended, first, weight, place_row, place_col, starts, vectors)


def half_places(rows, part):
    row = lax.broadcasted_iota(jnp.int32, (rows, EXTRA), 0) // part
    high = lax.broadcasted_iota(jnp.int32, (rows, EXTRA), 1)
    column = lax.broadcasted_iota(jnp.int32, (rows, part), 0) % part
    return (row, high, column == lax.broadcasted_iota(jnp.int32, (rows, part), 1))


def write_extra(values, part):
    row, high, column = half_places(values.shape[0], part)
    near = values.astype(bf16)
    left = (values - near.astype(f32)).astype(bf16)
    near_rows = jnp.where(row == high, 1.0, 0.0).astype(bf16)
    left_rows = jnp.where(row + 8 == high, 1.0, 0.0).astype(bf16)
    near_values = jnp.where(column, near.astype(f32), 0.0).astype(bf16)
    left_values = jnp.where(column, left.astype(f32), 0.0).astype(bf16)
    return dot_tn(near_rows, near_values) + dot_tn(left_rows, left_values)


def read_extra(extra, rows):
    part = extra.shape[1]
    row, high, column = half_places(rows, part)
    pick = jnp.where(row == high % 8, 1.0, 0.0).astype(bf16)
    return jnp.sum(jnp.where(column, dot_nn(pick, extra), 0.0), axis=1, keepdims=True)


GELU_A = 0.7978845608028654
GELU_B = 0.044715


def expert_kernel(x_ref, g_ref, up_ref, down_ref, dx_ref, y_ref, dup_ref, ddown_ref):
    quarters, _, cap, part = g_ref.shape
    x = jnp.concatenate([x_ref[q, 0, :cap] for q in range(quarters)], axis=1)
    grad = jnp.concatenate([g_ref[q, 0] for q in range(quarters)], axis=1)
    gate = read_extra(x_ref[0, 0, cap:], cap)
    a = dot_nn(x, up_ref[0])
    b = dot_nn(x, up_ref[1])
    t = jnp.tanh(GELU_A * (a + GELU_B * (a * a * a)))
    smooth = 0.5 * a * (1.0 + t)
    slope = 0.5 * (1.0 + t) + (0.5 * GELU_A) * a * (1.0 - t * t) * (1.0 + (3.0 * GELU_B) * (a * a))
    active = smooth * b
    dact = dot_nt(grad, down_ref[...]) * gate
    da = (dact * b * slope).astype(bf16)
    db = (dact * smooth).astype(bf16)
    low = active.astype(bf16)
    dx = dot_nt(da, up_ref[0]) + dot_nt(db, up_ref[1])
    extra = write_extra(jnp.sum(dact * active, axis=1, keepdims=True), part)
    y = dot_nn(low, down_ref[...])
    for q in range(quarters):
        dims = slice(q * part, (q + 1) * part)
        dx_ref[q, 0, :cap] = dx[:, dims].astype(bf16)
        dx_ref[q, 0, cap:] = extra.astype(bf16)
        y_ref[q, 0] = y[:, dims].astype(bf16)
    scaled = (active * gate).astype(bf16)

    @pl.when(pl.program_id(0) == 0)
    def _():
        dup_ref[0] = dot_tn(x, da)
        dup_ref[1] = dot_tn(x, db)
        ddown_ref[...] = dot_tn(scaled, grad)

    @pl.when(pl.program_id(0) > 0)
    def _():
        dup_ref[0] = dup_ref[0] + dot_tn(x, da)
        dup_ref[1] = dup_ref[1] + dot_tn(x, db)
        ddown_ref[...] = ddown_ref[...] + dot_tn(scaled, grad)


def expert_block(x, grads, up, down):
    quarters, sources, cap, part = grads.shape
    ext = x.shape[2]
    ff = down.shape[0]
    whole = lambda shape: pl.BlockSpec(shape, lambda i: (0,) * len(shape))
    rows = lambda n: pl.BlockSpec((quarters, 1, n, part), lambda i: (0, i, 0, 0))
    return pl.pallas_call(
        expert_kernel,
        grid=(sources,),
        out_shape=(
            jax.ShapeDtypeStruct(x.shape, bf16),
            jax.ShapeDtypeStruct(grads.shape, bf16),
            jax.ShapeDtypeStruct(up.shape, f32),
            jax.ShapeDtypeStruct(down.shape, f32),
        ),
        in_specs=[rows(ext), rows(cap), whole(up.shape), whole(down.shape)],
        out_specs=(rows(ext), rows(cap), whole(up.shape), whole(down.shape)),
        compiler_params=pltpu.CompilerParams(vmem_limit_bytes=60 * MIB),
        name="expert_block",
    )(x, grads, up, down)


def adamw_step(weight, grad, first, second, rate):
    first_new = beta_first * first + (1.0 - beta_first) * grad
    second_new = beta_second * second + (1.0 - beta_second) * grad * grad
    moment = first_new / (1.0 - beta_first**STEP)
    spread = second_new / (1.0 - beta_second**STEP)
    weight_new = weight - rate * (
        moment / (jnp.sqrt(spread) + adam_epsilon) + weight_decay * weight
    )
    return (weight_new, first_new, second_new)


def swap_rows(values):
    return lax.ppermute(values, "row", [(0, 1), (1, 0)])


def gather_quarters(values):
    return lax.all_gather(values, ("row", "col"), axis=0)


def sum_quarters(values):
    return lax.psum_scatter(values, ("row", "col"), scatter_dimension=0, tiled=False)


def cross(values, near):
    perm = [(h * 2 + r, (r if near else 1 - r) * 2 + h) for h in range(2) for r in range(2)]
    return lax.ppermute(values, ("half", "row"), perm)


def cross_back(values, near):
    perm = [((r if near else 1 - r) * 2 + h, h * 2 + r) for h in range(2) for r in range(2)]
    return lax.ppermute(values, ("half", "row"), perm)


def in_order(index, own, other):
    return jnp.where(index == 0, jnp.stack([own, other]), jnp.stack([other, own]))


def pick(values, index):
    return lax.dynamic_index_in_dim(values, index, 0, keepdims=False)


def local(
    layer_in, lengths, placing, routes, cotangent,
    norm_gains, gain_first, gain_second, rel_bias, bias_first, bias_second,
    router, router_first, router_second, qkv_weight, qkv_first, qkv_second,
    proj_weight, proj_first, proj_second, expert_up, up_first, up_second,
    expert_down, down_first, down_second,
):
    tokens, part = layer_in.shape
    experts = lax.axis_size("ex")
    dp_count = 2 * experts
    both = ("ex", "half")
    quarters = lax.axis_size("row") * lax.axis_size("col")
    row, half = lax.axis_index("row"), lax.axis_index("half")
    cap = min(tokens, 5 * TOP * tokens // (4 * experts))
    hc = qkv_weight.shape[5]
    head_count = hc // HD

    x_all = gather_quarters(layer_in)
    gains_all = gather_quarters(norm_gains)

    qkv_low = jnp.moveaxis(qkv_weight[0, 0].astype(bf16), 1, 0).reshape(2, -1, 3 * hc)
    qkv_both = in_order(row, pick(qkv_low, row), swap_rows(pick(qkv_low, 1 - row)))
    weight = lax.all_gather(qkv_both, both, axis=1).reshape(D, 3 * hc)
    proj_low = jnp.swapaxes(proj_weight[:, :, 0, 0].astype(bf16), 1, 2)
    proj_both = in_order(row, pick(proj_low, row), swap_rows(pick(proj_low, 1 - row)))
    proj = lax.all_gather(proj_both, both, axis=1).reshape(D, hc)

    up_low = jnp.swapaxes(expert_up[0].astype(bf16), 0, 1)
    down_low = expert_down[0].astype(bf16)
    up = in_order(half, cross(up_low, True), cross(up_low, False))
    up = jnp.moveaxis(up, 0, 1).reshape(2, D, -1)
    down = in_order(half, cross(down_low, True), cross(down_low, False))
    down = jnp.moveaxis(down, 0, 1).reshape(-1, D)

    places = placing[0]
    given_routes = jnp.zeros_like(routes).at[places].set(routes)
    flat = given_routes.reshape(-1)
    numbers = jnp.arange(experts, dtype=jnp.int32)
    hits = (flat[:, None] == numbers[None, :]).astype(jnp.int32)
    before = jnp.cumsum(hits, axis=0) - hits
    table = hits.astype(f32).reshape(tokens, TOP, experts)
    slot_of = jnp.sum((jnp.where(hits > 0, before + 1, 0)).reshape(tokens, TOP, experts), axis=1) - 1
    one_hot = (slot_of.T[:, None, :] == jnp.arange(cap, dtype=jnp.int32)[None, :, None]).astype(bf16)

    def to_slots(values):
        return jnp.einsum("est,tf->esf", one_hot, values, preferred_element_type=f32).astype(bf16)

    def from_slots(values):
        return jnp.einsum("est,esf->tf", one_hot, values, preferred_element_type=f32)

    def exchange(values):
        return lax.all_to_all(values, "ex", split_axis=0, concat_axis=0, tiled=True)

    slot_grads = gather_quarters(exchange(to_slots(cotangent)))

    ends = jnp.cumsum(lengths[0])
    at = jnp.arange(tokens, dtype=jnp.int32)
    starts = jnp.max(jnp.where(ends[None, :] <= at[:, None], ends[None, :], 0), axis=1).astype(jnp.int32)
    vectors = bias_vectors(rel_bias, tokens)
    first, qkv, attended, lse = attention_forward(
        x_all, gains_all[:, :1], weight, places[None, :], places[:, None], starts[:, None], vectors
    )
    partial = dot_nt(attended, proj).astype(bf16).reshape(tokens, quarters, part)
    resid_one = layer_in.astype(f32)
    second = resid_one + sum_quarters(jnp.moveaxis(partial, 1, 0)).astype(f32)

    scaled_router = norm_gains[1][:, None] * router
    sums = lax.psum(
        jnp.concatenate(
            [jnp.sum(second * second, axis=1)[None], jnp.dot(second, scaled_router, precision=highest).T]
        ),
        ("row", "col"),
    )
    inverse_two = lax.rsqrt(sums[0] / D + norm_epsilon)
    mixed = (second * inverse_two[:, None] * norm_gains[1]).astype(bf16)
    logits = sums[1:].T * inverse_two[:, None]
    chosen = jnp.sum(table * logits[:, None, :], axis=2)
    gates = jax.nn.softmax(chosen, axis=1)
    gate_of = jnp.sum(table * gates[:, :, None], axis=1)

    gate_slots = jnp.einsum("est,te->es", one_hot.astype(f32), gate_of, precision=highest)
    padded = jnp.pad(gate_slots, ((0, 0), (0, 8 * part - cap))).reshape(experts, 8, part)
    near = padded.astype(bf16)
    left = (padded - near.astype(f32)).astype(bf16)
    slots = jnp.concatenate([to_slots(mixed), near, left], axis=1)
    slot_x = gather_quarters(exchange(slots))
    dx, y, dup, ddown = expert_block(slot_x, slot_grads, up, down)
    dx_home = exchange(sum_quarters(dx))
    y_home = exchange(sum_quarters(y))

    token_y = jnp.einsum("est,esf->etf", one_hot, y_home, preferred_element_type=f32)
    layer_out = (second + jnp.einsum("etf,te->tf", token_y, gate_of, precision=highest)).astype(bf16)

    extra = dx_home[:, cap:].astype(f32)
    gate_grad_slots = (extra[:, :8] + extra[:, 8:]).reshape(experts, -1)[:, :cap]
    gate_dgate = jnp.einsum("est,es->te", one_hot.astype(f32), gate_grad_slots, precision=highest)
    grad_logits = gate_dgate - gate_of * jnp.sum(gate_dgate, axis=1, keepdims=True)
    grad_router = jnp.dot(mixed.astype(f32).T, grad_logits, precision=highest)
    grad_mixed = from_slots(dx_home[:, :cap]) + jnp.dot(grad_logits, router.T, precision=highest)
    scaled = grad_mixed * norm_gains[1]
    row_total = lax.psum(jnp.sum(second * scaled, axis=1), ("row", "col"))
    grad_two = cotangent.astype(f32) + (
        scaled * inverse_two[:, None] - second * (inverse_two**3 * row_total / D)[:, None]
    )
    grad_gain_two = jnp.sum(grad_mixed * second * inverse_two[:, None], axis=0)

    branch = gather_quarters(grad_two.astype(bf16))
    dfirst, dweight, dproj, dvectors = attention_backward(
        branch, proj, qkv, lse, attended, first, weight, places[None, :], places[:, None], starts[:, None], vectors
    )
    grad_norm_one = sum_quarters(dfirst).astype(f32)
    square_sum = jnp.sum(x_all.astype(f32) ** 2, axis=(0, 2))
    inverse_one = lax.rsqrt(square_sum / D + norm_epsilon)
    scaled = grad_norm_one * norm_gains[0]
    row_total = lax.psum(jnp.sum(resid_one * scaled, axis=1), ("row", "col"))
    back_one = scaled * inverse_one[:, None] - resid_one * (inverse_one**3 * row_total / D)[:, None]
    input_grad = (grad_two + back_one).astype(bf16)
    grad_gain_one = jnp.sum(grad_norm_one * resid_one * inverse_one[:, None], axis=0)

    grad_bias = bias_gradient(dvectors, head_count, tokens)
    grad_gains, grad_bias, grad_router = lax.psum(
        (jnp.stack([grad_gain_one, grad_gain_two]), grad_bias, grad_router), both
    )
    qkv_part = lax.psum_scatter(
        dweight.reshape(2, dp_count, -1, 3 * hc), both, scatter_dimension=1, tiled=False
    )
    qkv_part = in_order(row, pick(qkv_part, row), swap_rows(pick(qkv_part, 1 - row)))
    grad_qkv = jnp.moveaxis(qkv_part, 0, 1).reshape(qkv_weight.shape).astype(f32)
    proj_part = lax.psum_scatter(
        dproj.reshape(2, dp_count, -1, hc), both, scatter_dimension=1, tiled=False
    )
    proj_part = in_order(row, pick(proj_part, row), swap_rows(pick(proj_part, 1 - row)))
    grad_proj = jnp.swapaxes(proj_part, 1, 2).reshape(proj_weight.shape).astype(f32)
    dup = jnp.moveaxis(dup.astype(bf16).reshape(2, 2, D // 2, -1), 1, 0)
    grad_up = cross_back(pick(dup, half), True).astype(f32) + cross_back(pick(dup, 1 - half), False).astype(f32)
    grad_up = jnp.swapaxes(grad_up, 0, 1)[None]
    ddown = jnp.moveaxis(ddown.astype(bf16).reshape(-1, 2, D // 2), 1, 0)
    grad_down = cross_back(pick(ddown, half), True).astype(f32) + cross_back(pick(ddown, 1 - half), False).astype(f32)
    grad_down = grad_down[None]

    gains = adamw_step(norm_gains, grad_gains, gain_first, gain_second, 0.5)
    bias = adamw_step(rel_bias, grad_bias, bias_first, bias_second, 1.0)
    routers = adamw_step(router, grad_router, router_first, router_second, 2.0 * (2 * D) ** (-0.5))
    qkvs = adamw_step(qkv_weight, grad_qkv, qkv_first, qkv_second, 2.0 * D ** (-0.5))
    projs = adamw_step(proj_weight, grad_proj, proj_first, proj_second, 2.0 * (HEADS * HD / 8) ** (-0.5))
    ups = adamw_step(expert_up, grad_up, up_first, up_second, 2.0 * D ** (-0.5))
    downs = adamw_step(expert_down, grad_down, down_first, down_second, 2.0 * (FF / 2) ** (-0.5))
    out = (layer_out, input_grad) + gains + bias + routers
    for group in (qkvs, projs, ups, downs):
        out = out + group + (group[0].astype(bf16),)
    return out


def solution(mesh):
    shape = mesh.devices.shape
    fine = Mesh(
        mesh.devices.reshape((shape[0] // 2, 2) + shape[1:]), ("ex", "half", "row", "col")
    )
    dp, grid = ("ex", "half"), ("row", "col")
    tokens, own = P(dp, grid), P(dp, None)
    gain, router = P(None, grid), P(grid, None)
    qkv, proj = P("row", dp, None, None, None, "col"), P(None, "col", "row", dp, None)
    up, down = P(dp, "row", None, "col"), P(dp, "col", "row")
    in_specs = (
        (tokens, own, own, own, tokens) + (gain,) * 6 + (router,) * 3
        + (qkv,) * 3 + (proj,) * 3 + (up,) * 3 + (down,) * 3
    )
    out_specs = (
        (tokens, tokens) + (gain,) * 6 + (router,) * 3
        + (qkv,) * 4 + (proj,) * 4 + (up,) * 4 + (down,) * 4
    )
    return jax.shard_map(local, mesh=fine, in_specs=in_specs, out_specs=out_specs, check_vma=False)
```

time: 1620 us -> 732 us (0.45)
  waiting for transfers between devices: 714 us -> 237 us
  matrix products: 263 us -> 40 us
  other arithmetic: 261 us -> 46.2 us
  Pallas kernels: 0 us -> 98.1 us
  local copies, waits for them, and re-layouts: 119 us -> 42.4 us
  starting transfers between devices: 18.1 us -> 41.9 us
  blocking collectives: 217 us -> 200 us
    reduce_scatter x9 -> x4, waiting for transfers between devices: 401 us -> 79 us  [sum_quarters(): lax.psum_scatter(values, ('row', 'col'), scatter_dimension=0, tiled=False)]
    dot_general x28 -> x12, matrix products: 260 us -> 38 us  [the longest x1 12 us: local(): jnp.einsum('etf,te->tf', token_y, gate_of, precision=highest)]
    all_to_all x3 -> x1, waiting for transfers between devices: 144 us -> 11.5 us  [exchange(): return lax.all_to_all(values, 'ex', split_axis=0, concat_axis=0, tiled=True)]
    reduce_sum x19 -> x8, other arithmetic: 128 us -> 6.37 us  [the longest x1 2.08 us: local(): square_sum = jnp.sum(x_all.astype(f32) ** 2, axis=(0, 2))]
    pallas_call x0 -> x3, Pallas kernels: none -> 98.1 us  [the longest x1 50.3 us: expert_block(): pl.pallas_call(expert_kernel, grid=(sources,), out_shape=(jax.ShapeDtypeS...]
    all_gather x9 -> x5, waiting for transfers between devices: 140 us -> 49.5 us  [the longest x4 44.9 us: gather_quarters(): return lax.all_gather(values, ('row', 'col'), axis=0)]
    and x4 -> x0, other arithmetic: 65.7 us -> none  [block_scores(): visible = (own_seq[:, None] == sequence[None, :]) & (distance >= 0)]
    ppermute x0 -> x12, waiting for transfers between devices: none -> 47.8 us  [the longest x4 32.6 us: cross(): return lax.ppermute(values, ('half', 'row'), perm)]
  transfers between devices with their start and end apart: 22 -> 23, of which waited for: 18 -> 11; matrix products, arithmetic and copies ran while one was open for 12% -> 14% of each run, Pallas kernels for 0% -> 4%
where the time goes in v1:
time: 732 us; the launch traced here: 722 us
  waiting for transfers between devices  237 us (32%)
  blocking collectives  200 us (27%)
  Pallas kernels  98.1 us (13%)
  other arithmetic  46.2 us (6%)
  local copies, waits for them, and re-layouts  42.4 us (6%)
  starting transfers between devices  41.9 us (6%)
  matrix products  40 us (5%)
  between operations  16.2 us (2%)
    all_to_all x3, blocking collectives, exchange(): return lax.all_to_all(values, 'ex', split_axis=0, concat_axis=0, tiled=True)  109 us
    reduce_scatter x4, waiting for transfers between devices, sum_quarters(): lax.psum_scatter(values, ('row', 'col'), scatter_dimension=0, tiled=False)  79 us
    pallas_call x1, Pallas kernels, expert_block(): pl.pallas_call(expert_kernel, grid=(sources,), out_shape=(jax.ShapeDtypeS...  50.3 us
    unnamed x11, waiting for transfers between devices  48.7 us
    all_gather x4, waiting for transfers between devices, gather_quarters(): return lax.all_gather(values, ('row', 'col'), axis=0)  44.9 us
    all_gather x1, blocking collectives, local(): proj = lax.all_gather(proj_both, both, axis=1).reshape(D, hc)  35.3 us
    ppermute x4, waiting for transfers between devices, cross(): return lax.ppermute(values, ('half', 'row'), perm)  32.6 us
    pallas_call x1, Pallas kernels, attention_backward(): pl.pallas_call(attention_backward_kernel, out_shape=(jax.ShapeDtypeStruct...  27 us
  transfers between devices with their start and end apart: 23, of which 11 were waited for; matrix products, arithmetic and copies ran while one was open for 14% of the time, Pallas kernels for 4%

profile of v1, /device:TPU:0, one launch (start us, length us, event | category | flops | bytes accessed | tf_op | source)
XLA Modules:
  0.0 721.6 jit_solution(2579632680640466909)
XLA Ops:
  12.9 8.7 %all-gather.5 = f32[4,2,256]{2,1,0:T(2,128)S(1)} all-gather(f32[1,2,256]{2,1,0:T(2,128)S(1)} %bitcast.291), channel_id=3, replica_groups=mesh['ex'=4,'half'=2,'row'=2,'col'=2] {'row','col'}, dimensions={0}, use_global_device_ids=true | all-gather | bytes 10240 | tf_op jit(solution)/shard_map/all_gather | solution.py:394
  22.2 35.3 %all_gather.43 = bf16[2,8,64,256]{3,2,1,0:T(8,128)(2,1)} all-gather(bf16[2,1,64,256]{3,2,1,0:T(8,128)(2,1)S(1)} %maximum_select_fusion.4), channel_id=1, replica_groups=mesh['ex'=4,'half'=2,'row'=2,'col'=2] {'ex','half'}, dimensions={1}, use_global_device_ids=true | all-gather | bytes 589824 | tf_op jit(solution)/shard_map/all_gather | solution.py:444
  62.1 23.3 %all-gather.14.cloned.1.call-done = bf16[4096,256]{1,0:T(8,128)(2,1)} async-done(((bf16[1024,256]{1,0:T(8,128)(2,1)}), bf16[4096,256]{1,0:T(8,128)(2,1)}) %all-gather.14.cloned.1.call-update) | async-done | bytes 2097168 | tf_op jit(solution)/shard_map/all_gather | solution.py:394
  86.9 20.7 %attention_forward.1 = (bf16[4,1024,256]{2,1,0:T(8,128)(2,1)}, bf16[1024,768]{1,0:T(8,128)(2,1)S(1)}, bf16[1024,256]{1,0:T(8,128)(2,1)S(1)}, f32[1024,128]{1,0:T(8,128)S(1)}) custom-call(bf16[4,1024,256]{2,1,0:T(8,128)(2,1)} %bitcast.251, f32[4,1,256]{2,1,0:T(1,128)S(1)} %slice.50.gain_ref, bf16[1024,768]{1,0:T(8,128)(2,1)S(1)} %bitcast.246, ...), custom_call_target="tpu_custom_call" | custom-call | tf_op jit(solution)/shard_map/attention_forward/pallas_call | solution.py:167
  124.1 36.4 %all_to_all.20 = bf16[4,640,256]{2,1,0:T(8,128)(2,1)} all-to-all(bf16[4,640,256]{2,1,0:T(8,128)(2,1)S(1)} %fusion.19), channel_id=1, replica_groups=mesh['ex'=4,'half'=2,'row'=2,'col'=2] {'ex'}, dimensions={0} | all-to-all | bytes 2621440 | tf_op jit(solution)/shard_map/all_to_all | solution.py:470
  164.7 12.9 %psum.42 = f32[5,1024]{1,0:T(8,128)S(1)} all-reduce(f32[5,1024]{1,0:T(8,128)S(1)} %pad_maximum_fusion.1), channel_id=1, replica_groups=mesh['ex'=4,'half'=2,'row'=2,'col'=2] {'row','col'}, use_global_device_ids=true, to_apply=%region_8.9 | all-reduce | flops 5120 | bytes 40960 | tf_op jit(solution)/shard_map/psum | solution.py:486
  185.9 35.8 %all_to_all.21 = bf16[4,656,256]{2,1,0:T(8,128)(2,1)} all-to-all(bf16[4,656,256]{2,1,0:T(8,128)(2,1)S(1)} %pad_maximum_fusion), channel_id=1, replica_groups=mesh['ex'=4,'half'=2,'row'=2,'col'=2] {'ex'}, dimensions={0} | all-to-all | bytes 2686976 | tf_op jit(solution)/shard_map/all_to_all | solution.py:470
  226.4 12.4 %collective-permute-start.2 = (bf16[2,512,704]{1,2,0:T(8,128)(2,1)}, bf16[2,512,704]{1,2,0:T(8,128)(2,1)}, u32[]{:S(2)}, u32[]{:S(2)}) collective-permute-start(bf16[2,512,704]{1,2,0:T(8,128)(2,1)} %convert_bitcast_fusion), channel_id=1, source_target_pairs={{0,0},{2,4},{4,2},{6,6},{1,1},{3,5},{5,3},{7,7},{8,8},{10,12},{12,... | collective-permute-start | bytes 4325384 | tf_op jit(solution)/shard_map/ppermute | solution.py:403
  240.1 32.6 %collective-permute-done.5 = bf16[704,512]{1,0:T(8,128)(2,1)S(1)} collective-permute-done((bf16[704,512]{1,0:T(8,128)(2,1)S(1)}, bf16[704,512]{1,0:T(8,128)(2,1)S(1)}, u32[]{:S(2)}, u32[]{:S(2)}) %collective-permute-start.5) | collective-permute-done | bytes 720928 | tf_op jit(solution)/shard_map/ppermute | solution.py:403
  283.4 50.3 %expert_block.1 = (bf16[4,4,656,256]{3,2,1,0:T(8,128)(2,1)}, bf16[4,4,640,256]{3,2,1,0:T(8,128)(2,1)}, f32[2,1024,704]{2,1,0:T(8,128)}, f32[704,1024]{1,0:T(8,128)}) custom-call(bf16[4,4,656,256]{3,2,1,0:T(8,128)(2,1)} %bitcast.255, bf16[4,4,640,256]{3,2,1,0:T(8,128)(2,1)} %bitcast.256, bf16[2,1024,704]{2,1,0:T(8,128)(2,1)} %bitcast.250, ...), custom_call_target="tpu_custom_call" | custom-call | tf_op jit(solution)/shard_map/expert_block/pallas_call | solution.py:362
  333.8 54.4 %reduce-scatter.15.cloned.1.call-done = bf16[1,4,656,256]{3,2,1,0:T(8,128)(2,1)} async-done(((bf16[4,4,656,256]{3,2,1,0:T(8,128)(2,1)}), bf16[1,4,656,256]{3,2,1,0:T(8,128)(2,1)}) %reduce-scatter.15.cloned.1.call-update) | async-done | bytes 1343504 | tf_op jit(solution)/shard_map/reduce_scatter | solution.py:398
  388.2 36.7 %all_to_all.22 = bf16[4,656,256]{2,1,0:T(8,128)(2,1)S(1)} all-to-all(bf16[4,656,256]{2,1,0:T(8,128)(2,1)} %bitcast.264), channel_id=1, replica_groups=mesh['ex'=4,'half'=2,'row'=2,'col'=2] {'ex'}, dimensions={0} | all-to-all | bytes 2686976 | tf_op jit(solution)/shard_map/all_to_all | solution.py:470
  434.1 6.5 psum.43
  442.7 21.6 %all-gather.20.cloned.1.call-done = bf16[4096,256]{1,0:T(8,128)(2,1)} async-done(((bf16[1024,256]{1,0:T(8,128)(2,1)}), bf16[4096,256]{1,0:T(8,128)(2,1)}) %all-gather.20.cloned.1.call-update) | async-done | bytes 2097168 | tf_op jit(solution)/shard_map/all_gather | solution.py:394
  464.3 27.0 %attention_backward.1 = (bf16[4,1024,256]{2,1,0:T(8,128)(2,1)}, bf16[1024,768]{1,0:T(8,128)(2,1)}, bf16[1024,256]{1,0:T(8,128)(2,1)}, f32[12,512]{1,0:T(8,128)}) custom-call(bf16[4,1024,256]{2,1,0:T(8,128)(2,1)} %bitcast.260, bf16[1024,256]{1,0:T(8,128)(2,1)} %bitcast.257, bf16[1024,768]{1,0:T(8,128)(2,1)} %copy-done.4, f32[1024,128]{1,0:T(8,128)} %copy-done.5, ...), custom_call_target="tpu_custom_call" | custom-call | tf_op jit(solution)/shard_map/attention_backward/pallas_call | solution.py:267
  508.8 12.4 %collective-permute-start.8 = (bf16[2,512,704]{1,2,0:T(8,128)(2,1)}, bf16[2,512,704]{1,2,0:T(8,128)(2,1)}, u32[]{:S(2)}, u32[]{:S(2)}) collective-permute-start(bf16[2,512,704]{1,2,0:T(8,128)(2,1)} %bitcast.262), channel_id=1, source_target_pairs={{0,0},{4,2},{2,4},{6,6},{1,1},{5,3},{3,5},{7,7},{8,8},{12,10},{10,... | collective-permute-start | bytes 4325384 | tf_op jit(solution)/shard_map/ppermute | solution.py:408
  526.2 6.9 collective-permute-start.10
  544.6 14.2 %collective-permute-done.11 = bf16[704,512]{1,0:T(8,128)(2,1)} collective-permute-done((bf16[704,512]{1,0:T(8,128)(2,1)}, bf16[704,512]{1,0:T(8,128)(2,1)}, u32[]{:S(2)}, u32[]{:S(2)}) %collective-permute-start.11) | collective-permute-done | bytes 720928 | tf_op jit(solution)/shard_map/ppermute | solution.py:408
  564.4 6.4 fusion.74
  570.8 11.5 %all-to-all-done.2 = bf16[4,640,256]{2,1,0:T(8,128)(2,1)} async-done(((bf16[4,640,256]{2,1,0:T(8,128)(2,1)}), bf16[4,640,256]{2,1,0:T(8,128)(2,1)}, u32[]{:S(2)}, u32[]{:S(2)}) %all-to-all-start.2) | async-done | bytes 1310752 | tf_op jit(solution)/shard_map/all_to_all | solution.py:470
  586.3 12.0 %fusion.12 = f32[1024,1,256]{2,1,0:T(1,128)} fusion(f32[1024,4,1]{1,2,0:T(1,128)S(1)} %copy-done.24, f32[4,1024,256]{2,1,0:T(8,128)S(1)} %fusion.2), kind=kOutput, calls=%fused_computation.15 | convolution fusion | flops 12582912 | bytes 5259264 | tf_op jit(solution)/shard_map/etf,te->tf/dot_general | solution.py:510
  598.9 47.2 %all-reduce.7.cloned.1.call-done = (bf16[2,8,64,768]{3,2,1,0:T(8,128)(2,1)}, bf16[2,8,64,256]{3,2,1,0:T(8,128)(2,1)}) async-done(((bf16[2,8,64,768]{3,2,1,0:T(8,128)(2,1)}, bf16[2,8,64,256]{3,2,1,0:T(8,128)(2,1)}), (bf16[2,8,64,768]{3,2,1,0:T(8,128)(2,1)}, bf16[2,8,64,256]{3,2,1,0:T(8,128)(2,1)})) %all-reduce.7.cloned.1.call-update) | async-done | bytes 2097168
  655.3 24.6 %reduce-scatter.17.cloned.1.call-done = bf16[1,1024,256]{2,1,0:T(8,128)(2,1)} async-done(((bf16[4,1024,256]{2,1,0:T(8,128)(2,1)}), bf16[1,1024,256]{2,1,0:T(8,128)(2,1)}) %reduce-scatter.17.cloned.1.call-update) | async-done | bytes 524304 | tf_op jit(solution)/shard_map/reduce_scatter | solution.py:398
  687.8 21.9 %all-reduce.3 = (f32[2,256]{1,0:T(2,128)S(1)}, f32[32,4]{0,1:T(4,128)S(1)}, f32[256,4]{0,1:T(4,128)S(1)}) all-reduce(f32[2,256]{1,0:T(2,128)S(1)} %pad_maximum_fusion.2, f32[32,4]{0,1:T(4,128)S(1)} %convolution_bitcast_fusion, f32[256,4]{0,1:T(4,128)S(1)} %fusion.69), channel_id=1, replica_groups=mesh['ex'=4,'half'=2,'row'=2,'col'=2] {'ex','half'}, use_global_device_ids=true, to_apply=%region_24.25 | all-reduce | flops 1664 | bytes 13312 | tf_op jit(solution)/shard_map/psum | solution.py:539
  (275 shorter events, 133.8 us)
Async XLA Ops:
  7.3 54.9 %all-gather.12.cloned.1.call-start = ((), (), s32[]{:S(2)}) async-start(), calls=%async_computation.8 | async-start | bytes 1769472 | tf_op jit(solution)/shard_map/all_gather | solution.py:441
  8.9 1.5 collective-permute-start
  11.1 74.3 %all-gather.14.cloned.1.call-start = ((), (), s32[]{:S(2)}) async-start(), calls=%async_computation.13 | async-start | bytes 2621440 | tf_op jit(solution)/shard_map/all_gather | solution.py:394
  11.9 149.5 %reduce-scatter.11.cloned.1.call-start = ((), (), s32[]{:S(2)}) async-start(), calls=%async_computation.9 | async-start | bytes 2621440 | tf_op jit(solution)/shard_map/reduce_scatter | solution.py:398
  12.0 10.2 %collective-permute-start.1 = (bf16[64,256]{1,0:T(8,128)(2,1)S(1)}, bf16[64,256]{1,0:T(8,128)(2,1)S(1)}, u32[]{:S(2)}, u32[]{:S(2)}) collective-permute-start(bf16[64,256]{1,0:T(8,128)(2,1)S(1)} %get-tuple-element.233), channel_id=1, source_target_pairs={{0,2},{2,0},{1,3},{3,1},{4,6},{6,4},{5,7},{7,5},{8,10},{10,8},{9,1... | collective-permute-start | bytes 98312 | tf_op jit(solution)/shard_map/ppermute | solution.py:390
  111.7 171.7 %all-gather.18.cloned.1.call-start = ((), (), s32[]{:S(2)}) async-start(), calls=%async_computation.15 | async-start | bytes 6553600 | tf_op jit(solution)/shard_map/all_gather | solution.py:394
  120.3 310.0 %copy-start.47 = (s32[4,1024]{1,0:T(4,128)}, s32[4,1024]{1,0:T(4,128)S(1)}, u32[]{:S(2)}) copy-start(s32[4,1024]{1,0:T(4,128)S(1)} %copy.175) | copy-start | bytes 49156
  160.5 122.9 %all-gather.16.cloned.1.call-start = ((), (), s32[]{:S(2)}) async-start(), calls=%async_computation.14 | async-start | bytes 6717440 | tf_op jit(solution)/shard_map/all_gather | solution.py:394
  221.7 166.5 %reduce-scatter.15.cloned.1.call-start = ((), (), s32[]{:S(2)}) async-start(), calls=%async_computation.11 | async-start | bytes 6717440 | tf_op jit(solution)/shard_map/reduce_scatter | solution.py:398
  224.9 49.3 %collective-permute-start.3 = (bf16[2,512,704]{1,2,0:T(8,128)(2,1)}, bf16[2,512,704]{1,2,0:T(8,128)(2,1)}, u32[]{:S(2)}, u32[]{:S(2)}) collective-permute-start(bf16[2,512,704]{1,2,0:T(8,128)(2,1)} %convert_bitcast_fusion), channel_id=1, source_target_pairs={{0,4},{2,0},{4,6},{6,2},{1,5},{3,1},{5,7},{7,3},{8,12},{10,8},{12,... | collective-permute-start | bytes 4325384 | tf_op jit(solution)/shard_map/ppermute | solution.py:403
  226.4 47.8 %collective-permute-start.2 = (bf16[2,512,704]{1,2,0:T(8,128)(2,1)}, bf16[2,512,704]{1,2,0:T(8,128)(2,1)}, u32[]{:S(2)}, u32[]{:S(2)}) collective-permute-start(bf16[2,512,704]{1,2,0:T(8,128)(2,1)} %convert_bitcast_fusion), channel_id=1, source_target_pairs={{0,0},{2,4},{4,2},{6,6},{1,1},{3,5},{5,3},{7,7},{8,8},{10,12},{12,... | collective-permute-start | bytes 4325384 | tf_op jit(solution)/shard_map/ppermute | solution.py:403
  238.9 33.7 %collective-permute-start.5 = (bf16[704,512]{1,0:T(8,128)(2,1)S(1)}, bf16[704,512]{1,0:T(8,128)(2,1)S(1)}, u32[]{:S(2)}, u32[]{:S(2)}) collective-permute-start(bf16[704,512]{1,0:T(8,128)(2,1)S(1)} %convert_bitcast_fusion.1), channel_id=1, source_target_pairs={{0,4},{2,0},{4,6},{6,2},{1,5},{3,1},{5,7},{7,3},{8,12},{10,8},{12,... | collective-permute-start | bytes 2162696 | tf_op jit(solution)/shard_map/ppermute | solution.py:403
  239.0 33.7 %collective-permute-start.4 = (bf16[704,512]{1,0:T(8,128)(2,1)S(1)}, bf16[704,512]{1,0:T(8,128)(2,1)S(1)}, u32[]{:S(2)}, u32[]{:S(2)}) collective-permute-start(bf16[704,512]{1,0:T(8,128)(2,1)S(1)} %convert_bitcast_fusion.1), channel_id=1, source_target_pairs={{0,0},{2,4},{4,2},{6,6},{1,1},{3,5},{5,3},{7,7},{8,8},{10,12},{12,... | collective-permute-start | bytes 2162696 | tf_op jit(solution)/shard_map/ppermute | solution.py:403
  333.8 130.5 %all-gather.20.cloned.1.call-start = ((), (), s32[]{:S(2)}) async-start(), calls=%async_computation.16 | async-start | bytes 2621440 | tf_op jit(solution)/shard_map/all_gather | solution.py:394
  441.9 91.3 %reduce-scatter.13.cloned.1.call-start = ((), (), s32[]{:S(2)}) async-start(), calls=%async_computation.10 | async-start | bytes 6553600 | tf_op jit(solution)/shard_map/reduce_scatter | solution.py:398
  442.6 203.5 %all-reduce.7.cloned.1.call-start = ((), (), s32[]{:S(2)}) async-start(), calls=%async_computation.17 | async-start | bytes 4194304
  491.3 188.6 %reduce-scatter.17.cloned.1.call-start = ((), (), s32[]{:S(2)}) async-start(), calls=%async_computation.12 | async-start | bytes 2621440 | tf_op jit(solution)/shard_map/reduce_scatter | solution.py:398
  508.6 55.8 %collective-permute-start.9 = (bf16[2,512,704]{1,2,0:T(8,128)(2,1)}, bf16[2,512,704]{1,2,0:T(8,128)(2,1)}, u32[]{:S(2)}, u32[]{:S(2)}) collective-permute-start(bf16[2,512,704]{1,2,0:T(8,128)(2,1)} %bitcast.263), channel_id=1, source_target_pairs={{4,0},{0,2},{6,4},{2,6},{5,1},{1,3},{7,5},{3,7},{12,8},{8,10},{14,... | collective-permute-start | bytes 4325384 | tf_op jit(solution)/shard_map/ppermute | solution.py:408
  508.8 55.6 %collective-permute-start.8 = (bf16[2,512,704]{1,2,0:T(8,128)(2,1)}, bf16[2,512,704]{1,2,0:T(8,128)(2,1)}, u32[]{:S(2)}, u32[]{:S(2)}) collective-permute-start(bf16[2,512,704]{1,2,0:T(8,128)(2,1)} %bitcast.262), channel_id=1, source_target_pairs={{0,0},{4,2},{2,4},{6,6},{1,1},{5,3},{3,5},{7,7},{8,8},{12,10},{10,... | collective-permute-start | bytes 4325384 | tf_op jit(solution)/shard_map/ppermute | solution.py:408
  526.2 32.5 %collective-permute-start.11 = (bf16[704,512]{1,0:T(8,128)(2,1)}, bf16[704,512]{1,0:T(8,128)(2,1)}, u32[]{:S(2)}, u32[]{:S(2)}) collective-permute-start(bf16[704,512]{1,0:T(8,128)(2,1)} %bitcast.239), channel_id=1, source_target_pairs={{4,0},{0,2},{6,4},{2,6},{5,1},{1,3},{7,5},{3,7},{12,8},{8,10},{14,... | collective-permute-start | bytes 2162696 | tf_op jit(solution)/shard_map/ppermute | solution.py:408
  526.2 32.5 %collective-permute-start.10 = (bf16[704,512]{1,0:T(8,128)(2,1)}, bf16[704,512]{1,0:T(8,128)(2,1)}, u32[]{:S(2)}, u32[]{:S(2)}) collective-permute-start(bf16[704,512]{1,0:T(8,128)(2,1)} %bitcast.240), channel_id=1, source_target_pairs={{0,0},{4,2},{2,4},{6,6},{1,1},{5,3},{3,5},{7,7},{8,8},{12,10},{10,... | collective-permute-start | bytes 2162696 | tf_op jit(solution)/shard_map/ppermute | solution.py:408
  533.2 49.1 %all-to-all-start.2 = ((bf16[4,640,256]{2,1,0:T(8,128)(2,1)}), bf16[4,640,256]{2,1,0:T(8,128)(2,1)}, u32[]{:S(2)}, u32[]{:S(2)}) async-start(bf16[4,640,256]{2,1,0:T(8,128)(2,1)} %bitcast.265), calls=%async_computation.4 | async-start | bytes 2621440 | tf_op jit(solution)/shard_map/all_to_all | solution.py:470
  646.9 1.5 collective-permute-start.7
  647.9 1.5 collective-permute-start.6
  (61 other events, 2274.9 us)
Sparse Core Ops, SparseCore 0:
  11.2 50.8 all-gather.11
  63.7 21.7 all-gather.13
  111.8 31.4 reduce-scatter.10
  160.6 39.4 all-gather.17
  221.8 40.8 all-gather.15
  333.9 54.2 reduce-scatter.14
  442.0 22.2 all-gather.19
  466.8 51.3 reduce-scatter.12
  522.9 123.1 all-reduce.6
  648.7 31.1 reduce-scatter.16

commit v2 on v1

v2 whole, which is shorter than its diff:
```python
import functools

import jax
import jax.numpy as jnp
import numpy as np
from jax import lax
from jax.experimental import pallas as pl
from jax.experimental.layout import Layout, with_layout_constraint
from jax.experimental.pallas import tpu as pltpu
from jax.sharding import Mesh, PartitionSpec as P

D = 1024
HEADS = 16
FF = 2816
TOP = 2
STEP = 5
beta_first = 0.5
beta_second = 0.5
adam_epsilon = 1e-08
weight_decay = 0.01
highest = lax.Precision.HIGHEST
EXTRA = 16
HD = 64
BUCKETS = 32
LONGEST = 512
TILE = 256
norm_epsilon = 1e-06
hidden_score = -1e30
bucket_edges = np.floor(16.0 * 2.0 ** (np.arange(16) * 0.375)).astype(np.int32)
f32 = jnp.float32
bf16 = jnp.bfloat16
MIB = 1 << 20


def dot_nn(a, b):
    return lax.dot_general(a, b, (((1,), (0,)), ((), ())), preferred_element_type=f32)


def dot_nt(a, b):
    return lax.dot_general(a, b, (((1,), (1,)), ((), ())), preferred_element_type=f32)


def dot_tn(a, b):
    return lax.dot_general(a, b, (((0,), (0,)), ((), ())), preferred_element_type=f32)


def tile_reach(tokens):
    return min(tokens // TILE, (LONGEST - 1 + TILE - 1) // TILE + 1)


def toeplitz_places(tokens):
    reach = tile_reach(tokens)
    m = np.arange(2 * TILE)
    base = np.where(m < TILE, -m, 2 * TILE - m)
    distance = np.arange(reach)[:, None] * TILE + base[None, :]
    clipped = np.maximum(distance, 0)
    buckets = np.where(
        clipped < 16, clipped, 15 + (clipped[..., None] >= bucket_edges).sum(-1)
    )
    return (distance, buckets)


def bias_vectors(rel_bias, tokens):
    distance, buckets = toeplitz_places(tokens)
    table = jnp.asarray((buckets[..., None] == np.arange(BUCKETS)).astype(np.float32))
    values = jnp.einsum("dmb,bh->hdm", table, rel_bias, precision=lax.Precision.HIGHEST)
    values = jnp.where(jnp.asarray(distance < 0)[None], hidden_score, values)
    return values.reshape(-1, 2 * TILE)


def bias_gradient(vectors, head_count, tokens):
    distance, buckets = toeplitz_places(tokens)
    table = ((buckets[..., None] == np.arange(BUCKETS)) & (distance >= 0)[..., None]).astype(np.float32)
    return jnp.einsum(
        "dmb,hdm->bh",
        jnp.asarray(table),
        vectors.reshape(head_count, distance.shape[0], 2 * TILE),
        precision=lax.Precision.HIGHEST,
    )


def fill_bias(vector_ref, bias):
    for i in range(bias.shape[0]):
        wide = jnp.broadcast_to(vector_ref[i : i + 1, :], (TILE, 2 * TILE))
        bias[i] = pltpu.roll(wide, 0, 1, stride=1, stride_axis=0)[:, :TILE]


def head_lanes(shape, head):
    return lax.broadcasted_iota(jnp.int32, shape, 1) // HD == head


def attention_forward_kernel(
    x_ref, gain_ref, weight_ref, place_row, place_col, start_ref, vector_ref,
    first_ref, qkv_ref, attended_ref, lse_ref, bias, placed_out,
):
    quarters, tokens, part = x_ref.shape
    width = quarters * part
    hc = weight_ref.shape[1] // 4
    head_count = hc // HD
    reach = bias.shape[0] // head_count
    fill_bias(vector_ref, bias)
    squares = jnp.zeros((tokens, 1), f32)
    for q in range(quarters):
        v = x_ref[q].astype(f32)
        squares = squares + jnp.sum(v * v, axis=1, keepdims=True)
    inverse = lax.rsqrt(squares / width + norm_epsilon)
    total = jnp.zeros((tokens, 3 * hc), f32)
    for q in range(quarters):
        first = (x_ref[q].astype(f32) * inverse * gain_ref[q, :1]).astype(bf16)
        first_ref[q] = first
        total = total + dot_nn(first, weight_ref[q * part : (q + 1) * part, : 3 * hc])
    to_placed = jnp.where(
        place_col[...] == lax.broadcasted_iota(jnp.int32, (tokens, tokens), 1), 1.0, 0.0
    ).astype(bf16)
    scale = jnp.where(
        lax.broadcasted_iota(jnp.int32, (1, 3 * hc), 1) < hc, HD ** (-0.5), 1.0
    )
    qkv_ref[...] = dot_nn(to_placed, (total * scale).astype(bf16)).astype(bf16)
    for a in range(tokens // TILE):
        rows = slice(a * TILE, (a + 1) * TILE)
        blocks = range(max(0, a - reach + 1), a + 1)
        starts = start_ref[rows, :]
        visible = [
            b * TILE + lax.broadcasted_iota(jnp.int32, (TILE, TILE), 1) >= starts for b in blocks
        ]

        def one_head(head, carry):
            out, lse = carry
            mine = head_lanes((TILE, hc), head)
            query = jnp.where(mine, qkv_ref[rows, :hc], 0)
            scores = []
            for b, seen in zip(blocks, visible):
                s = dot_nt(query, qkv_ref[b * TILE : (b + 1) * TILE, hc : 2 * hc])
                scores.append(jnp.where(seen, s + bias[head * reach + a - b], hidden_score))
            top = functools.reduce(jnp.maximum, [jnp.max(s, axis=1, keepdims=True) for s in scores])
            exps = [jnp.exp(s - top) for s in scores]
            denominator = functools.reduce(jnp.add, [jnp.sum(e, axis=1, keepdims=True) for e in exps])
            share = 1.0 / denominator
            value = jnp.zeros((TILE, hc), f32)
            for b, e in zip(blocks, exps):
                value = value + dot_nn(
                    (e * share).astype(bf16), qkv_ref[b * TILE : (b + 1) * TILE, 2 * hc :]
                )
            lane = lax.broadcasted_iota(jnp.int32, (TILE, 128), 1)
            return (
                jnp.where(mine, value, out),
                jnp.where(lane == head, top + jnp.log(denominator), lse),
            )

        out, lse = lax.fori_loop(
            0, head_count, one_head, (jnp.zeros((TILE, hc), f32), jnp.zeros((TILE, 128), f32))
        )
        placed_out[rows, :] = out.astype(bf16)
        lse_ref[rows, :] = lse
    lane = lax.broadcasted_iota(jnp.int32, (tokens, 128), 1)
    lse_ref[...] = jnp.where(lane == 127, inverse, lse_ref[...])
    to_given = jnp.where(
        place_row[...] == lax.broadcasted_iota(jnp.int32, (tokens, tokens), 0), 1.0, 0.0
    ).astype(bf16)
    attended_ref[...] = dot_nn(to_given, placed_out[...]).astype(bf16)


def microseconds(time):
    return pl.CostEstimate(flops=0, bytes_accessed=int(time * 3.5e6), transcendentals=0)


def vmem():
    return pl.BlockSpec(memory_space=pltpu.VMEM)


def attention_forward(x, gain, weight, place_row, place_col, starts, vectors):
    quarters, tokens, part = x.shape
    hc = weight.shape[1] // 4
    return pl.pallas_call(
        attention_forward_kernel,
        out_shape=(
            jax.ShapeDtypeStruct(x.shape, bf16),
            jax.ShapeDtypeStruct((tokens, 3 * hc), bf16),
            jax.ShapeDtypeStruct((tokens, hc), bf16),
            jax.ShapeDtypeStruct((tokens, 128), f32),
        ),
        in_specs=[vmem()] * 7,
        out_specs=(vmem(),) * 4,
        scratch_shapes=[
            pltpu.VMEM((vectors.shape[0], TILE, TILE), f32),
            pltpu.VMEM((tokens, hc), bf16),
        ],
        compiler_params=pltpu.CompilerParams(vmem_limit_bytes=16 * MIB),
        cost_estimate=microseconds(20),
        name="attention_forward",
    )(x, gain, weight, place_row, place_col, starts, vectors)


def attention_backward_kernel(
    branch_ref, qkv_ref, lse_ref, attended_ref, first_ref, weight_ref,
    place_row, place_col, start_ref, vector_ref,
    dfirst_ref, dweight_ref, dvector_ref,
    bias, dbias, grad_ref, dqkv, dkv,
):
    quarters, tokens, part = branch_ref.shape
    hc = weight_ref.shape[1] // 4
    head_count = hc // HD
    reach = bias.shape[0] // head_count
    fill_bias(vector_ref, bias)
    dbias[...] = jnp.zeros_like(dbias)
    dkv[...] = jnp.zeros_like(dkv)
    total = jnp.zeros((tokens, hc), f32)
    for q in range(quarters):
        dims = slice(q * part, (q + 1) * part)
        total = total + dot_nn(branch_ref[q], weight_ref[dims, 3 * hc :])
        dweight_ref[dims, 3 * hc :] = dot_tn(branch_ref[q], attended_ref[...]).astype(bf16)
    to_placed = jnp.where(
        place_col[...] == lax.broadcasted_iota(jnp.int32, (tokens, tokens), 1), 1.0, 0.0
    ).astype(bf16)
    grad_ref[...] = dot_nn(to_placed, total.astype(bf16)).astype(bf16)
    for a in range(tokens // TILE):
        rows = slice(a * TILE, (a + 1) * TILE)
        blocks = range(max(0, a - reach + 1), a + 1)
        starts = start_ref[rows, :]
        visible = [
            b * TILE + lax.broadcasted_iota(jnp.int32, (TILE, TILE), 1) >= starts for b in blocks
        ]

        def one_head(head, dquery):
            mine = head_lanes((TILE, hc), head)
            query = jnp.where(mine, qkv_ref[rows, :hc], 0)
            grad = jnp.where(mine, grad_ref[rows, :], 0)
            lane = lax.broadcasted_iota(jnp.int32, (TILE, 128), 1)
            lse = jnp.sum(jnp.where(lane == head, lse_ref[rows, :], 0.0), axis=1, keepdims=True)
            probs, dprobs = [], []
            inner = jnp.zeros((TILE, 1), f32)
            for b, seen in zip(blocks, visible):
                keys = slice(b * TILE, (b + 1) * TILE)
                s = dot_nt(query, qkv_ref[keys, hc : 2 * hc]) + bias[head * reach + a - b]
                p = jnp.where(seen, jnp.exp(s - lse), 0.0)
                d = dot_nt(grad, qkv_ref[keys, 2 * hc :])
                inner = inner + jnp.sum(p * d, axis=1, keepdims=True)
                probs.append(p)
                dprobs.append(d)
            for b, p, d in zip(blocks, probs, dprobs):
                keys = slice(b * TILE, (b + 1) * TILE)
                ds = p * (d - inner)
                place = head * reach + a - b
                dbias[place] = dbias[place] + ds
                low = ds.astype(bf16)
                dquery = dquery + dot_nn(low, jnp.where(mine, qkv_ref[keys, hc : 2 * hc], 0))
                dkv[keys, :hc] = dkv[keys, :hc] + dot_tn(low, query)
                dkv[keys, hc:] = dkv[keys, hc:] + dot_tn(p.astype(bf16), grad)
            return dquery

        dquery = lax.fori_loop(0, head_count, one_head, jnp.zeros((TILE, hc), f32))
        dqkv[rows, :hc] = (dquery * HD ** (-0.5)).astype(bf16)
    dqkv[:, hc:] = dkv[...].astype(bf16)
    for i in range(dbias.shape[0]):
        wide = jnp.concatenate([dbias[i], jnp.zeros((TILE, TILE), f32)], axis=1)
        level = wide[:8]
        for g in range(8, TILE, 8):
            level = level + pltpu.roll(wide[g : g + 8], 2 * TILE - g, 1)
        row = level[:1]
        for s in range(1, 8):
            row = row + pltpu.roll(level[s : s + 1], 2 * TILE - s, 1)
        dvector_ref[i : i + 1, :] = row
    to_given = jnp.where(
        place_row[...] == lax.broadcasted_iota(jnp.int32, (tokens, tokens), 0), 1.0, 0.0
    ).astype(bf16)
    given = dot_nn(to_given, dqkv[...]).astype(bf16)
    for q in range(quarters):
        dims = slice(q * part, (q + 1) * part)
        dfirst_ref[q] = dot_nt(given, weight_ref[dims, : 3 * hc]).astype(bf16)
        dweight_ref[dims, : 3 * hc] = dot_tn(first_ref[q], given).astype(bf16)


def attention_backward(branch, qkv, lse, attended, first, weight, place_row, place_col, starts, vectors):
    quarters, tokens, part = branch.shape
    hc = weight.shape[1] // 4
    return pl.pallas_call(
        attention_backward_kernel,
        out_shape=(
            jax.ShapeDtypeStruct(branch.shape, bf16),
            jax.ShapeDtypeStruct(weight.shape, bf16),
            jax.ShapeDtypeStruct(vectors.shape, f32),
        ),
        in_specs=[vmem()] * 10,
        out_specs=(vmem(),) * 3,
        scratch_shapes=[
            pltpu.VMEM((vectors.shape[0], TILE, TILE), f32),
            pltpu.VMEM((vectors.shape[0], TILE, TILE), f32),
            pltpu.VMEM((tokens, hc), bf16),
            pltpu.VMEM((tokens, 3 * hc), bf16),
            pltpu.VMEM((tokens, 2 * hc), f32),
        ],
        compiler_params=pltpu.CompilerParams(vmem_limit_bytes=24 * MIB),
        cost_estimate=microseconds(28),
        name="attention_backward",
    )(branch, qkv, lse, attended, first, weight, place_row, place_col, starts, vectors)


def half_places(rows, part):
    row = lax.broadcasted_iota(jnp.int32, (rows, EXTRA), 0) // part
    high = lax.broadcasted_iota(jnp.int32, (rows, EXTRA), 1)
    column = lax.broadcasted_iota(jnp.int32, (rows, part), 0) % part
    return (row, high, column == lax.broadcasted_iota(jnp.int32, (rows, part), 1))


def write_extra(values, part):
    row, high, column = half_places(values.shape[0], part)
    near = values.astype(bf16)
    left = (values - near.astype(f32)).astype(bf16)
    near_rows = jnp.where(row == high, 1.0, 0.0).astype(bf16)
    left_rows = jnp.where(row + 8 == high, 1.0, 0.0).astype(bf16)
    near_values = jnp.where(column, near.astype(f32), 0.0).astype(bf16)
    left_values = jnp.where(column, left.astype(f32), 0.0).astype(bf16)
    return dot_tn(near_rows, near_values) + dot_tn(left_rows, left_values)


def read_extra(extra, rows):
    part = extra.shape[1]
    row, high, column = half_places(rows, part)
    pick = jnp.where(row == high % 8, 1.0, 0.0).astype(bf16)
    return jnp.sum(jnp.where(column, dot_nn(pick, extra), 0.0), axis=1, keepdims=True)


GELU_A = 0.7978845608028654
GELU_B = 0.044715


MESH = pl.DeviceIdType.MESH


def remote(src, dst, send, recv, where):
    return pltpu.make_async_remote_copy(
        src_ref=src, dst_ref=dst, send_sem=send, recv_sem=recv, device_id=where, device_id_type=MESH
    )


def greet(wheres):
    barrier = pltpu.get_barrier_semaphore()
    for where in wheres:
        pl.semaphore_signal(barrier, inc=1, device_id=where, device_id_type=MESH)
    pl.semaphore_wait(barrier, len(wheres))


def dot_exact(a, b, dims):
    return lax.dot_general(a, b, ((dims, ((), ()))), precision=highest, preferred_element_type=f32)


def grid_peers(columns):
    row, col = lax.axis_index("row"), lax.axis_index("col")
    return [
        {"row": (row + i) % 2, "col": (col + j) % columns}
        for i in range(2)
        for j in range(columns)
        if i + j > 0
    ]


def sum_of_peers(mine, got, send, recv, columns):
    copies = [
        remote(mine, got.at[i], send.at[i], recv.at[i], where)
        for i, where in enumerate(grid_peers(columns))
    ]
    for copy in copies:
        copy.start()
    for copy in copies:
        copy.wait_recv()
    total = mine[...]
    for i in range(len(copies)):
        total = total + got[i]
    for copy in copies:
        copy.wait_send()
    return total


PIECES = 4


def project_kernel(
    columns, experts,
    attended_ref, weight_ref, layer_ref, gain_ref, router_ref, slot_ref,
    second_ref, mixed_ref, gate_ref, column_ref,
    core_out, core_in, keep, col_out, col_in, stat, stat_in,
    core_send, core_recv, col_send, col_recv, stat_send, stat_recv,
):
    row, col = lax.axis_index("row"), lax.axis_index("col")
    tokens, part = layer_ref.shape
    wide = columns * part
    size = tokens // PIECES
    greet(grid_peers(columns))
    heads = slice(3 * weight_ref.shape[1] // 4, weight_ref.shape[1])
    own_rows = pl.ds(pl.multiple_of(row * wide, wide), wide)
    other_rows = pl.ds(pl.multiple_of((1 - row) * wide, wide), wide)
    cores = []
    for i in range(PIECES):
        at = slice(i * size, (i + 1) * size)
        core_out[i] = dot_nt(attended_ref[at, :], weight_ref[other_rows, heads]).astype(bf16)
        copy = remote(core_out.at[i], core_in.at[i], core_send.at[i], core_recv.at[i], {"row": 1 - row})
        copy.start()
        cores.append(copy)
        keep[i] = dot_nt(attended_ref[at, :], weight_ref[own_rows, heads])
    own_columns = pl.ds(pl.multiple_of(col * part, part), part)
    crossing = []
    for i in range(PIECES):
        cores[i].wait_recv()
        keep[i] = keep[i] + core_in[i].astype(f32)
        for k in range(1, columns):
            to = (col + k) % columns
            col_out[i, k - 1] = keep[i, :, pl.ds(pl.multiple_of(to * part, part), part)].astype(bf16)
            copy = remote(
                col_out.at[i, k - 1], col_in.at[i, k - 1], col_send.at[i, k - 1], col_recv.at[i, k - 1], {"col": to}
            )
            copy.start()
            crossing.append(copy)
    ones = jnp.where(lax.broadcasted_iota(jnp.int32, router_ref.shape, 0) == experts, 1.0, 0.0)
    for i in range(PIECES):
        at = slice(i * size, (i + 1) * size)
        total = layer_ref[at, :].astype(f32) + keep[i, :, own_columns]
        for k in range(1, columns):
            crossing[i * (columns - 1) + k - 1].wait_recv()
            total = total + col_in[i, k - 1].astype(f32)
        second_ref[at, :] = total
        stat[:, at] = dot_exact(router_ref[...], total, ((1,), (1,))) + dot_exact(
            ones, total * total, ((1,), (1,))
        )
    total = sum_of_peers(stat, stat_in, stat_send, stat_recv, columns)
    inverse = lax.rsqrt(total[experts : experts + 1] / D + norm_epsilon)
    routed = slot_ref[...] >= 0
    logits = jnp.where(routed, total * inverse, hidden_score)
    shares = jnp.where(routed, jnp.exp(logits - jnp.max(logits, axis=0, keepdims=True)), 0.0)
    gates = shares / jnp.sum(shares, axis=0, keepdims=True)
    gate_ref[...] = gates
    number = lax.broadcasted_iota(jnp.int32, gates.shape, 0)
    lanes = (gates.shape[0], 128)
    eye = jnp.where(
        lax.broadcasted_iota(jnp.int32, lanes, 0) == lax.broadcasted_iota(jnp.int32, lanes, 1), 1.0, 0.0
    )
    table = dot_exact(jnp.where(number == experts, inverse, gates), eye, ((0,), (0,)))
    column_ref[...] = table
    mixed_ref[...] = (second_ref[...] * table[:, experts : experts + 1] * gain_ref[...]).astype(bf16)
    for copy in cores + crossing:
        copy.wait_send()


def project(attended, weight, layer_in, gain, router_rows, slots, experts, columns):
    tokens, part = layer_in.shape
    size = tokens // PIECES
    rows = router_rows.shape[0]
    dma = pltpu.SemaphoreType.DMA
    return pl.pallas_call(
        functools.partial(project_kernel, columns, experts),
        out_shape=(
            jax.ShapeDtypeStruct((tokens, part), f32),
            jax.ShapeDtypeStruct((tokens, part), bf16),
            jax.ShapeDtypeStruct((rows, tokens), f32),
            jax.ShapeDtypeStruct((tokens, 128), f32),
        ),
        in_specs=[vmem()] * 6,
        out_specs=(vmem(),) * 4,
        scratch_shapes=[
            pltpu.VMEM((PIECES, size, columns * part), bf16),
            pltpu.VMEM((PIECES, size, columns * part), bf16),
            pltpu.VMEM((PIECES, size, columns * part), f32),
            pltpu.VMEM((PIECES, columns - 1, size, part), bf16),
            pltpu.VMEM((PIECES, columns - 1, size, part), bf16),
            pltpu.VMEM((rows, tokens), f32),
            pltpu.VMEM((2 * columns - 1, rows, tokens), f32),
            dma((PIECES,)), dma((PIECES,)),
            dma((PIECES, columns - 1)), dma((PIECES, columns - 1)),
            dma((2 * columns - 1,)), dma((2 * columns - 1,)),
        ],
        compiler_params=pltpu.CompilerParams(
            collective_id=1, has_side_effects=True, vmem_limit_bytes=40 * MIB
        ),
        cost_estimate=microseconds(22),
        name="project",
    )(attended, weight, layer_in, gain, router_rows, slots)


def gather_kernel(
    columns, experts,
    layer_ref, gain_ref, shard_ref,
    x_ref, gains_ref, weight_ref,
    x_send, x_recv, own_send, own_recv, pass_send, pass_recv, gain_send, gain_recv,
    swap_send, swap_recv, z_send, z_recv, y_send, y_recv, place,
):
    ex, half = lax.axis_index("ex"), lax.axis_index("half")
    row, col = lax.axis_index("row"), lax.axis_index("col")
    mine = row * columns + col
    greet(
        grid_peers(columns)
        + [{"ex": (ex + s) % experts} for s in range(1, experts)]
        + [{"half": 1 - half}]
    )
    spread = Spread(
        x_ref, layer_ref, columns, x_send, x_recv, own_send, own_recv, pass_send, pass_recv
    )
    member = 2 * ex + half
    swap = remote(
        shard_ref.at[1 - row], weight_ref.at[row, member], swap_send.at[0], swap_recv.at[0], {"row": 1 - row}
    )
    swap.start()
    arrived = remote(
        shard_ref.at[1 - row], weight_ref.at[1 - row, member], swap_send.at[0], swap_recv.at[0], {"row": 1 - row}
    )
    place_shard = pltpu.make_async_copy(shard_ref.at[row], weight_ref.at[row, member], place.at[0])
    place_shard.start()
    spread.start()
    gains_ref[mine] = gain_ref[...]
    gain_copies = [
        remote(gain_ref, gains_ref.at[mine], gain_send.at[i], gain_recv.at[i], where)
        for i, where in enumerate(grid_peers(columns))
    ]
    for copy in gain_copies:
        copy.start()

    def z_copy(s, a):
        block = weight_ref.at[a, member]
        return remote(block, block, z_send.at[s, a], z_recv.at[s, a], {"ex": (ex + s) % experts})

    def z_arrival(s, a):
        block = weight_ref.at[a, 2 * ((ex - s + experts) % experts) + half]
        return remote(block, block, z_send.at[s, a], z_recv.at[s, a], {"ex": (ex + s) % experts})

    def y_copy(s, a):
        block = weight_ref.at[a, 2 * ((ex - s + experts) % experts) + half]
        return remote(block, block, y_send.at[s, a], y_recv.at[s, a], {"half": 1 - half})

    def y_arrival(s, a):
        block = weight_ref.at[a, 2 * ((ex - s + experts) % experts) + 1 - half]
        return remote(block, block, y_send.at[s, a], y_recv.at[s, a], {"half": 1 - half})

    place_shard.wait()
    for a in (row, 1 - row):
        if a is not row:
            arrived.wait_recv()
        for s in range(1, experts):
            z_copy(s, a).start()
        y_copy(0, a).start()
    spread.hand_on()
    for s in range(1, experts):
        for a in (row, 1 - row):
            z_arrival(s, a).wait_recv()
            y_copy(s, a).start()
    spread.finish()
    for i, copy in enumerate(gain_copies):
        copy.wait()
    swap.wait_send()
    for s in range(experts):
        for a in range(2):
            y_arrival(s, a).wait_recv()
            y_copy(s, a).wait_send()
            if s > 0:
                z_copy(s, a).wait_send()


class Spread:
    def __init__(self, out, source, columns, x_send, x_recv, own_send, own_recv, pass_send, pass_recv):
        row, col = lax.axis_index("row"), lax.axis_index("col")
        mine = row * columns + col
        size = source.shape[0] // PIECES
        self.out, self.source, self.mine = out, source, mine
        self.across, self.own, self.passed = [], [], []
        for i in range(PIECES):
            at = pl.ds(i * size, size)
            for k in range(1, columns):
                self.across.append(
                    remote(
                        source.at[at], out.at[mine, at], x_send.at[i, k - 1], x_recv.at[i, k - 1],
                        {"col": (col + k) % columns},
                    )
                )
                block = out.at[row * columns + (col - k + columns) % columns, at]
                self.passed.append(
                    remote(block, block, pass_send.at[i, k - 1], pass_recv.at[i, k - 1], {"row": 1 - row})
                )
            self.own.append(
                remote(source.at[at], out.at[mine, at], own_send.at[i], own_recv.at[i], {"row": 1 - row})
            )

    def start(self):
        for copy in self.across + self.own:
            copy.start()
        self.out[self.mine] = self.source[...]

    def hand_on(self):
        for across, passed in zip(self.across, self.passed):
            across.wait_recv()
            passed.start()

    def finish(self):
        for copy in self.own + self.passed:
            copy.wait_recv()
        for copy in self.across + self.own + self.passed:
            copy.wait_send()


def spread_semaphores(columns):
    dma = pltpu.SemaphoreType.DMA
    return [dma((PIECES, columns - 1))] * 2 + [dma((PIECES,))] * 2 + [dma((PIECES, columns - 1))] * 2


def gather(layer_in, gains, shard, experts, columns):
    tokens, part = layer_in.shape
    _, rows, width = shard.shape
    quarters = 2 * columns
    dma = pltpu.SemaphoreType.DMA
    return pl.pallas_call(
        functools.partial(gather_kernel, columns, experts),
        out_shape=(
            jax.ShapeDtypeStruct((quarters, tokens, part), bf16),
            jax.ShapeDtypeStruct((quarters,) + gains.shape, f32),
            jax.ShapeDtypeStruct((2, 2 * experts, rows, width), bf16),
        ),
        in_specs=[vmem()] * 3,
        out_specs=(vmem(),) * 3,
        scratch_shapes=spread_semaphores(columns)
        + [
            dma((quarters - 1,)), dma((quarters - 1,)), dma((1,)), dma((1,)),
            dma((experts, 2)), dma((experts, 2)), dma((experts, 2)), dma((experts, 2)), dma((1,)),
        ],
        compiler_params=pltpu.CompilerParams(
            collective_id=0, has_side_effects=True, vmem_limit_bytes=40 * MIB
        ),
        cost_estimate=microseconds(30),
        name="gather",
    )(layer_in, gains, shard)


def expert_kernel(
    columns, experts,
    *refs,
):
    grad_count = columns * experts
    mixed_ref, slot_ref, gate_ref, up_hbm, down_hbm = refs[:5]
    grad_hbm = refs[5 : 5 + grad_count]
    (
    home_ref, y_hbm, dup_hbm, ddown_hbm,
    x, xs, grads, up, down, da, db, scaled, core_out, core_in, keep, col_out, col_in,
    load, grad_load, grad_send, grad_recv, z_send, z_recv, own_send, own_recv, col_send, col_recv, pass_send, pass_recv,
    core_send, core_recv, back_send, back_recv, home_send, home_recv, y_sem, store, far_send, far_recv,
    ) = refs[5 + grad_count :]
    ex, half = lax.axis_index("ex"), lax.axis_index("half")
    row, col = lax.axis_index("row"), lax.axis_index("col")
    tokens, part = mixed_ref.shape
    ext = x.shape[2]
    cap = ext - EXTRA
    quarters = 2 * columns
    wide = columns * part
    mine = row * columns + col
    last = experts - 1
    greet(
        [{"ex": (ex + s) % experts} for s in range(1, experts)]
        + [{"col": (col + k) % columns} for k in range(1, columns)]
        + [{"row": 1 - row}]
    )

    own_rows = pl.ds(pl.multiple_of(row * wide, wide), wide)
    other_rows = pl.ds(pl.multiple_of((1 - row) * wide, wide), wide)
    loads = [
        pltpu.make_async_copy(up_hbm.at[row], up.at[:, own_rows], load.at[0]),
        pltpu.make_async_copy(down_hbm.at[row], down.at[:, own_rows], load.at[1]),
    ]
    handed = [
        remote(up_hbm.at[1 - row], up.at[:, own_rows], load.at[2], load.at[3], {"row": 1 - row}),
        remote(down_hbm.at[1 - row], down.at[:, own_rows], load.at[4], load.at[5], {"row": 1 - row}),
    ]
    for s in range(experts):
        for k in range(columns):
            at = (s, k)
            place = row * columns + (col - k + columns) % columns
            block = grad_hbm[s * columns + k]
            loads.append(pltpu.make_async_copy(block, grads.at[place, s], grad_load.at[at]))
            handed.append(
                remote(block, grads.at[place, s], grad_send.at[at], grad_recv.at[at], {"row": 1 - row})
            )
    for copy in loads + handed:
        copy.start()

    def z_copy(s):
        return remote(
            xs.at[s], x.at[mine, s], z_send.at[s], z_recv.at[s], {"ex": (ex + s) % experts}
        )

    def own_copy(s):
        block = x.at[mine, s]
        return remote(block, block, own_send.at[s], own_recv.at[s], {"row": 1 - row})

    def col_copy(s, k):
        block = x.at[mine, s]
        return remote(
            block, block, col_send.at[s, k - 1], col_recv.at[s, k - 1], {"col": (col + k) % columns}
        )

    def pass_copy(s, k):
        block = x.at[row * columns + (col - k + columns) % columns, s]
        return remote(
            block, block, pass_send.at[s, k - 1], pass_recv.at[s, k - 1], {"row": 1 - row}
        )

    def spread(s):
        own_copy(s).start()
        for k in range(1, columns):
            col_copy(s, k).start()

    def hand_on(s):
        for k in range(1, columns):
            col_copy(s, k).wait_recv()
            pass_copy(s, k).start()

    def slots_of(e):
        hit = slot_ref[pl.ds(e, 1), :] == lax.broadcasted_iota(jnp.int32, (cap, tokens), 0)
        values = dot_nn(jnp.where(hit, 1.0, 0.0).astype(bf16), mixed_ref[...]).astype(bf16)
        gate = jnp.sum(jnp.where(hit, gate_ref[pl.ds(e, 1), :], 0.0), axis=1, keepdims=True)
        return values, write_extra(gate, part).astype(bf16)

    def build(s):
        values, extra = slots_of((ex + s) % experts)
        xs[s, :cap] = values
        xs[s, cap:] = extra

    def nth(p):
        far = experts // 2
        return jnp.where(p == 1, far, jnp.where((p > 1) & (p <= far), p - 1, p))

    build(nth(1))
    z_copy(nth(1)).start()
    values, extra = slots_of(ex)
    x[mine, 0, :cap] = values
    x[mine, 0, cap:] = extra
    spread(0)

    @pl.loop(2, experts)
    def _(p):
        build(nth(p))

    for copy in loads:
        copy.wait()
    for copy in handed:
        copy.wait()
    hand_on(0)
    z_copy(nth(1)).wait_send()
    z_copy(nth(2)).start()
    z_copy(nth(1)).wait_recv()
    spread(nth(1))

    def core_copy(s):
        return remote(core_out.at[s], core_in.at[s], core_send.at[s], core_recv.at[s], {"row": 1 - row})

    def back_copy(s, k):
        return remote(
            col_out.at[s, k - 1], col_in.at[s, k - 1], back_send.at[s, k - 1], back_recv.at[s, k - 1],
            {"col": (col + k) % columns},
        )

    def home_copy(s):
        return remote(
            xs.at[s], home_ref.at[s], home_send.at[s], home_recv.at[s], {"ex": (ex - s + experts) % experts}
        )

    def up_store(g):
        return pltpu.make_async_copy(up.at[g, own_rows], dup_hbm.at[row, g], store.at[g])

    def up_far(g):
        return remote(up.at[g, other_rows], dup_hbm.at[row, g], far_send.at[g], far_recv.at[g], {"row": 1 - row})

    def down_store():
        return pltpu.make_async_copy(down.at[:, own_rows], ddown_hbm.at[row], store.at[2])

    def down_far():
        return remote(down.at[:, other_rows], ddown_hbm.at[row], far_send.at[2], far_recv.at[2], {"row": 1 - row})

    def y_copy(s, slot):
        return pltpu.make_async_copy(core_in.at[pl.ds(2 * slot, 2)], y_hbm.at[:, :, s], y_sem.at[slot])

    def after_core(s, slot):
        core_copy(s).wait_recv()
        keep[slot] = keep[slot] + core_in[s].astype(f32)
        for k in range(1, columns):
            to = (col + k) % columns
            col_out[s, k - 1] = keep[slot, to].astype(bf16)
            back_copy(s, k).start()

    def after_columns(s, slot):
        total = keep[slot, col]
        for k in range(1, columns):
            back_copy(s, k).wait_recv()
            total = total + col_in[s, k - 1].astype(f32)
        return total.astype(bf16)

    def send_home(s, slot):
        xs[s] = after_columns(s, slot)
        home_copy(s).start()

    @pl.loop(0, experts)
    def _(p):
        s = nth(p)
        slot = jnp.where(p == 0, 2, p % 2)
        grad = jnp.concatenate([grads[q, s] for q in range(quarters)], axis=1)
        d = dot_nt(grad, down[...])
        own_copy(s).wait_recv()
        for k in range(1, columns):
            pass_copy(s, k).wait_recv()

        @pl.when(p > 1)
        def _():
            after_core(nth(p - 1), (p - 1) % 2)

        @pl.when(p > 2)
        def _():
            send_home(nth(p - 2), p % 2)

        rows = jnp.concatenate([x[q, s] for q in range(quarters)], axis=1)
        gate = read_extra(x[mine, s, cap:], ext)
        a = dot_nn(rows, up[0])
        b = dot_nn(rows, up[1])
        d = d * gate
        square = a * a
        t = jnp.tanh(a * (GELU_A + (GELU_A * GELU_B) * square))
        part_on = 0.5 + 0.5 * t
        smooth = a * part_on
        slope = part_on + (a * (0.5 - 0.5 * t * t)) * (GELU_A + (3 * GELU_A * GELU_B) * square)
        active = smooth * b
        da[s] = (d * b * slope).astype(bf16)
        db[s] = (d * smooth).astype(bf16)
        scaled[s] = (active * gate).astype(bf16)
        extra = write_extra(jnp.sum(d * active, axis=1, keepdims=True), part)

        @pl.when((p > 0) & (p + 2 < experts))
        def _():
            z_copy(nth(p + 2)).wait_recv()
            spread(nth(p + 2))

        @pl.when((p > 0) & (p + 1 < experts))
        def _():
            hand_on(nth(p + 1))

        @pl.when((p > 0) & (p + 3 < experts))
        def _():
            z_copy(nth(p + 2)).wait_send()
            z_copy(nth(p + 3)).start()

        for j in range(columns):
            dims = pl.ds(pl.multiple_of(((1 - row) * columns + j) * part, part), part)
            value = dot_nt(da[s], up[0, dims]) + dot_nt(db[s], up[1, dims])
            core_out[s, j] = value.astype(bf16)
            core_out[s, j, cap:] = extra.astype(bf16)
        core_copy(s).start()
        for j in range(columns):
            dims = pl.ds(pl.multiple_of((row * columns + j) * part, part), part)
            keep[slot, j] = dot_nt(da[s], up[0, dims]) + dot_nt(db[s], up[1, dims])
            keep[slot, j, cap:] = extra

        @pl.when(p == 0)
        def _():
            hand_on(nth(1))
            z_copy(nth(2)).wait_send()
            z_copy(nth(3)).start()
            z_copy(nth(2)).wait_recv()
            spread(nth(2))

    def flat(ref, *at):
        block = ref[at] if at else ref[...]
        return block.reshape(experts * ext, block.shape[-1])

    before, final = nth(last - 1), nth(last)
    z_copy(final).wait_send()
    after_core(final, last % 2)
    after_core(0, 2)
    send_home(before, (last - 1) % 2)
    @pl.loop(0, experts)
    def _(s):
        slot = s % 2

        @pl.when(s > 1)
        def _():
            y_copy(s - 2, slot).wait()

        for i in range(2):
            for j in range(columns):
                dims = slice((i * columns + j) * part, (i * columns + j + 1) * part)
                core_in[2 * slot + i, j] = dot_nn(scaled[s], down[:, dims]).astype(bf16)
        y_copy(s, slot).start()

    send_home(final, last % 2)
    low = flat(scaled)
    for q in range(quarters):
        down[:, q * part : (q + 1) * part] = dot_tn(low, flat(grads, q)).astype(bf16)
    down_store().start()
    down_far().start()
    for g, hidden in enumerate((da, db)):
        low = flat(hidden)
        for q in range(quarters):
            up[g, q * part : (q + 1) * part] = dot_tn(flat(x, q), low).astype(bf16)
        up_store(g).start()
        up_far(g).start()
    home_ref[0] = after_columns(0, 2)
    for s in range(max(0, experts - 2), experts):
        y_copy(s, s % 2).wait()
    down_store().wait()
    down_far().wait()
    for g in range(2):
        up_store(g).wait()
        up_far(g).wait()

    @pl.loop(1, experts)
    def _(s):
        home_copy(s).wait_recv()
        home_copy(s).wait_send()

    @pl.loop(0, experts)
    def _(s):
        own_copy(s).wait_send()
        core_copy(s).wait_send()
        for k in range(1, columns):
            col_copy(s, k).wait_send()
            pass_copy(s, k).wait_send()
            back_copy(s, k).wait_send()


def expert_block(mixed, slots, gates, grads, up, down, columns):
    tokens, part = mixed.shape
    quarters, experts = 2 * columns, len(grads) // columns
    ext = grads[0].shape[0]
    ff = down.shape[1]
    wide = D // 2
    dma = pltpu.SemaphoreType.DMA
    hbm = pl.BlockSpec(memory_space=pl.ANY)
    others = columns - 1
    return pl.pallas_call(
        functools.partial(expert_kernel, columns, experts),
        out_shape=(
            jax.ShapeDtypeStruct((experts, ext, part), bf16),
            jax.ShapeDtypeStruct((2, columns, experts, ext, part), bf16),
            jax.ShapeDtypeStruct((2, 2, wide, ff), bf16),
            jax.ShapeDtypeStruct((2, ff, wide), bf16),
        ),
        in_specs=[vmem()] * 3 + [hbm] * (2 + len(grads)),
        out_specs=(vmem(), hbm, hbm, hbm),
        scratch_shapes=[
            pltpu.VMEM((quarters, experts, ext, part), bf16),
            pltpu.VMEM((experts, ext, part), bf16),
            pltpu.VMEM((quarters, experts, ext, part), bf16),
            pltpu.VMEM((2, D, ff), bf16),
            pltpu.VMEM((ff, D), bf16),
            pltpu.VMEM((experts, ext, ff), bf16),
            pltpu.VMEM((experts, ext, ff), bf16),
            pltpu.VMEM((experts, ext, ff), bf16),
            pltpu.VMEM((experts, columns, ext, part), bf16),
            pltpu.VMEM((experts, columns, ext, part), bf16),
            pltpu.VMEM((3, columns, ext, part), f32),
            pltpu.VMEM((experts, others, ext, part), bf16),
            pltpu.VMEM((experts, others, ext, part), bf16),
            dma((6,)), dma((experts, columns)), dma((experts, columns)), dma((experts, columns)),
            dma((experts,)), dma((experts,)), dma((experts,)), dma((experts,)),
            dma((experts, others)), dma((experts, others)), dma((experts, others)), dma((experts, others)),
            dma((experts,)), dma((experts,)), dma((experts, others)), dma((experts, others)),
            dma((experts,)), dma((experts,)), dma((2,)), dma((3,)), dma((3,)), dma((3,)),
        ],
        compiler_params=pltpu.CompilerParams(
            collective_id=2, has_side_effects=True, vmem_limit_bytes=56 * MIB
        ),
        cost_estimate=microseconds(80),
        name="expert_block",
    )(mixed, slots, gates, up, down, *grads)


def settle_kernel(
    columns, experts,
    home_ref, slot_ref, column_ref, second_ref, mixed_ref, cotangent_ref, gain_ref, router_ref,
    branch_ref, two_ref, drouter_ref, dgain_ref,
    low, stat, stat_in, stat_send, stat_recv, *spread_sems,
):
    ex = lax.axis_index("ex")
    tokens, part = second_ref.shape
    ext = home_ref.shape[1]
    cap = ext - EXTRA
    greet(grid_peers(columns))
    lane = lax.broadcasted_iota(jnp.int32, (tokens, 128), 1)
    dmixed = jnp.zeros((tokens, part), f32)
    gate_grads = jnp.zeros((tokens, 128), f32)
    for s in range(experts):
        e = (ex + s) % experts
        place = jnp.sum(jnp.where(lane == e, slot_ref[...], 0.0), axis=1, keepdims=True)
        hit = place == lax.broadcasted_iota(jnp.int32, (tokens, ext), 1).astype(f32)
        pick_rows = jnp.where(hit, 1.0, 0.0).astype(bf16)
        dmixed = dmixed + dot_nn(pick_rows, home_ref[s])
        values = read_extra(home_ref[s, cap:], ext)
        near = values.astype(bf16)
        left = (values - near.astype(f32)).astype(bf16)
        both = jnp.concatenate(
            [jnp.broadcast_to(near, (ext, 128)), jnp.broadcast_to(left, (ext, 128))], axis=1
        )
        found = dot_nn(pick_rows, both)
        gate_grads = jnp.where(lane == e, found[:, :128] + found[:, 128:], gate_grads)
    gates = jnp.where(lane < experts, column_ref[...], 0.0)
    dlogits = gate_grads - gates * jnp.sum(gate_grads, axis=1, keepdims=True)
    rows = drouter_ref.shape[0]
    drouter_ref[...] = dot_exact(dlogits, mixed_ref[...].astype(f32), ((0,), (0,)))[:rows]
    dmixed = dmixed + dot_exact(dlogits, router_ref[...], ((1,), (0,)))
    scaled = dmixed * gain_ref[...]
    stat[...] = dot_exact(jnp.ones((8, part), f32), second_ref[...] * scaled, ((1,), (1,)))
    total = sum_of_peers(stat, stat_in, stat_send, stat_recv, columns)
    first_row = jnp.where(lax.broadcasted_iota(jnp.int32, (8, 128), 0) == 0, 1.0, 0.0)
    row_total = dot_exact(total, first_row, ((0,), (0,)))[:, :1]
    inverse = column_ref[:, experts : experts + 1]
    normed = second_ref[...] * inverse
    two = cotangent_ref[...].astype(f32) + inverse * (
        scaled - normed * (inverse * row_total / D)
    )
    two_ref[...] = two
    low[...] = two.astype(bf16)
    spread = Spread(branch_ref, low, columns, *spread_sems)
    spread.start()
    dgain_ref[...] = jnp.broadcast_to(jnp.sum(dmixed * normed, axis=0, keepdims=True), dgain_ref.shape)
    spread.hand_on()
    spread.finish()


def settle(home, slots, table, second, mixed, cotangent, gain, router_rows, rows, experts, columns):
    tokens, part = second.shape
    quarters = 2 * columns
    dma = pltpu.SemaphoreType.DMA
    return pl.pallas_call(
        functools.partial(settle_kernel, columns, experts),
        out_shape=(
            jax.ShapeDtypeStruct((quarters, tokens, part), bf16),
            jax.ShapeDtypeStruct((tokens, part), f32),
            jax.ShapeDtypeStruct((rows, part), f32),
            jax.ShapeDtypeStruct((8, part), f32),
        ),
        in_specs=[vmem()] * 8,
        out_specs=(vmem(),) * 4,
        scratch_shapes=[
            pltpu.VMEM((tokens, part), bf16),
            pltpu.VMEM((8, tokens), f32),
            pltpu.VMEM((quarters - 1, 8, tokens), f32),
            dma((quarters - 1,)), dma((quarters - 1,)),
        ]
        + spread_semaphores(columns),
        compiler_params=pltpu.CompilerParams(
            collective_id=3, has_side_effects=True, vmem_limit_bytes=40 * MIB
        ),
        cost_estimate=microseconds(25),
        name="settle",
    )(home, slots, table, second, mixed, cotangent, gain, router_rows)


def finish_kernel(
    columns, experts,
    dfirst_ref, dweight_ref, small_ref, layer_ref, two_ref, gain_ref, inverse_ref,
    input_grad_ref, grad_ref, sums_ref,
    core_in, keep, col_out, col_in, stat, stat_in, y_in, z_out, z_in, held, row_out, row_in, small, small_in,
    core_send, core_recv, col_send, col_recv, stat_send, stat_recv,
    y_send, y_recv, z_send, z_recv, row_send, row_recv, small_send, small_recv,
):
    ex, half = lax.axis_index("ex"), lax.axis_index("half")
    row, col = lax.axis_index("row"), lax.axis_index("col")
    tokens, part = layer_ref.shape
    size = tokens // PIECES
    members = 2 * experts
    others = [
        {"ex": (ex + s) % experts, "half": (half + h) % 2}
        for s in range(experts)
        for h in range(2)
        if s + h > 0
    ]
    greet(grid_peers(columns) + others)

    def core_copy(i):
        at = pl.ds(i * size, size)
        return remote(
            dfirst_ref.at[pl.ds((1 - row) * columns, columns), at], core_in.at[:, at],
            core_send.at[i], core_recv.at[i], {"row": 1 - row},
        )

    def y_copy(s):
        to = 2 * ((ex + s) % experts) + 1 - half
        return remote(dweight_ref.at[:, to], y_in.at[s], y_send.at[s], y_recv.at[s], {"half": 1 - half})

    def z_copy(s):
        return remote(z_out.at[s], z_in.at[s], z_send.at[s], z_recv.at[s], {"ex": (ex + s) % experts})

    for i in range(PIECES):
        core_copy(i).start()
    order = list(range(1, experts)) + [0]
    for s in order:
        y_copy(s).start()
    crossing = []
    for i in range(PIECES):
        at = slice(i * size, (i + 1) * size)
        core_copy(i).wait_recv()
        for j in range(columns):
            keep[j, at] = dfirst_ref[row * columns + j, at].astype(f32) + core_in[j, at].astype(f32)
        for k in range(1, columns):
            to = (col + k) % columns
            col_out[k - 1, at] = keep[to, at].astype(bf16)
            copy = remote(
                col_out.at[k - 1, pl.ds(i * size, size)], col_in.at[k - 1, pl.ds(i * size, size)],
                col_send.at[i, k - 1], col_recv.at[i, k - 1], {"col": to},
            )
            copy.start()
            crossing.append(copy)
    for s in order:
        y_copy(s).wait_recv()
        total = dweight_ref[:, 2 * ((ex + s) % experts) + half].astype(f32) + y_in[s].astype(f32)
        if s > 0:
            z_out[s] = total.astype(bf16)
            z_copy(s).start()
        else:
            held[...] = total
    for copy in crossing:
        copy.wait_recv()
    dnorm = keep[col]
    for k in range(1, columns):
        dnorm = dnorm + col_in[k - 1].astype(f32)
    v = layer_ref[...].astype(f32)
    scaled = dnorm * gain_ref[...]
    stat[...] = dot_exact(jnp.ones((8, part), f32), v * scaled, ((1,), (1,)))
    total = sum_of_peers(stat, stat_in, stat_send, stat_recv, columns)
    first_row = jnp.where(lax.broadcasted_iota(jnp.int32, (8, 128), 0) == 0, 1.0, 0.0)
    row_total = dot_exact(total, first_row, ((0,), (0,)))[:, :1]
    inverse = inverse_ref[:, 127:128]
    normed = v * inverse
    input_grad_ref[...] = (
        two_ref[...] + inverse * (scaled - normed * (inverse * row_total / D))
    ).astype(bf16)
    small[...] = small_ref[...]
    small[:8] = jnp.broadcast_to(jnp.sum(dnorm * normed, axis=0, keepdims=True), (8, part))
    smalls = [
        remote(small, small_in.at[i], small_send.at[i], small_recv.at[i], where)
        for i, where in enumerate(others)
    ]
    for copy in smalls:
        copy.start()
    for s in range(1, experts):
        z_copy(s).wait_recv()
        held[...] = held[...] + z_in[s].astype(f32)
    row_out[...] = held[1 - row].astype(bf16)
    swap = remote(row_out, row_in, row_send.at[0], row_recv.at[0], {"row": 1 - row})
    swap.start()
    grad_ref[row] = held[row]
    sums = small[...]
    for i, copy in enumerate(smalls):
        copy.wait_recv()
        sums = sums + small_in[i]
    sums_ref[...] = sums
    swap.wait_recv()
    grad_ref[1 - row] = row_in[...].astype(f32)
    swap.wait_send()
    for copy in smalls + crossing:
        copy.wait_send()
    for i in range(PIECES):
        core_copy(i).wait_send()
    for s in range(experts):
        y_copy(s).wait_send()
        if s > 0:
            z_copy(s).wait_send()


def finish(dfirst, dweight, small, layer_in, two, gain, table, experts, columns):
    quarters, tokens, part = dfirst.shape
    _, members, rows, width = dweight.shape
    dma = pltpu.SemaphoreType.DMA
    others = columns - 1
    return pl.pallas_call(
        functools.partial(finish_kernel, columns, experts),
        out_shape=(
            jax.ShapeDtypeStruct((tokens, part), bf16),
            jax.ShapeDtypeStruct((2, rows, width), f32),
            jax.ShapeDtypeStruct(small.shape, f32),
        ),
        in_specs=[vmem()] * 7,
        out_specs=(vmem(),) * 3,
        scratch_shapes=[
            pltpu.VMEM((columns, tokens, part), bf16),
            pltpu.VMEM((columns, tokens, part), f32),
            pltpu.VMEM((others, tokens, part), bf16),
            pltpu.VMEM((others, tokens, part), bf16),
            pltpu.VMEM((8, tokens), f32),
            pltpu.VMEM((quarters - 1, 8, tokens), f32),
            pltpu.VMEM((experts, 2, rows, width), bf16),
            pltpu.VMEM((experts, 2, rows, width), bf16),
            pltpu.VMEM((experts, 2, rows, width), bf16),
            pltpu.VMEM((2, rows, width), f32),
            pltpu.VMEM((rows, width), bf16),
            pltpu.VMEM((rows, width), bf16),
            pltpu.VMEM(small.shape, f32),
            pltpu.VMEM((members - 1,) + small.shape, f32),
            dma((PIECES,)), dma((PIECES,)), dma((PIECES, others)), dma((PIECES, others)),
            dma((quarters - 1,)), dma((quarters - 1,)),
            dma((experts,)), dma((experts,)), dma((experts,)), dma((experts,)),
            dma((1,)), dma((1,)), dma((members - 1,)), dma((members - 1,)),
        ],
        compiler_params=pltpu.CompilerParams(
            collective_id=4, has_side_effects=True, vmem_limit_bytes=50 * MIB
        ),
        cost_estimate=microseconds(32),
        name="finish",
    )(dfirst, dweight, small, layer_in, two, gain, table)


def adamw_step(weight, grad, first, second, rate):
    first_new = beta_first * first + (1.0 - beta_first) * grad
    second_new = beta_second * second + (1.0 - beta_second) * grad * grad
    moment = first_new / (1.0 - beta_first**STEP)
    spread = second_new / (1.0 - beta_second**STEP)
    weight_new = weight - rate * (
        moment / (jnp.sqrt(spread) + adam_epsilon) + weight_decay * weight
    )
    return (weight_new, first_new, second_new)


def pick(values, index):
    return lax.dynamic_index_in_dim(values, index, 0, keepdims=False)


def local(
    layer_in, lengths, placing, routes, cotangent,
    norm_gains, gain_first, gain_second, rel_bias, bias_first, bias_second,
    router, router_first, router_second, qkv_weight, qkv_first, qkv_second,
    proj_weight, proj_first, proj_second, expert_up, up_first, up_second,
    expert_down, down_first, down_second,
):
    tokens, part = layer_in.shape
    experts, columns = lax.axis_size("ex"), lax.axis_size("col")
    quarters = 2 * columns
    ex, half, row = lax.axis_index("ex"), lax.axis_index("half"), lax.axis_index("row")
    cap = min(tokens, 5 * TOP * tokens // (4 * experts))
    ext = cap + EXTRA
    hc = qkv_weight.shape[5]
    head_count = hc // HD
    wide = D // 2

    qkv_low = jnp.moveaxis(qkv_weight[0, 0].astype(bf16), 1, 0).reshape(2, -1, 3 * hc)
    proj_low = jnp.swapaxes(proj_weight[:, :, 0, 0].astype(bf16), 1, 2)
    shard = jnp.concatenate([qkv_low, proj_low], axis=2)
    gains_eight = jnp.pad(norm_gains, ((0, 6), (0, 0)))
    x_all, gains_all, weight = gather(layer_in, gains_eight, shard, experts, columns)
    weight = weight.reshape(D, 4 * hc)

    places = placing[0]
    given_routes = jnp.zeros_like(routes).at[places].set(routes)
    flat = given_routes.reshape(-1)
    numbers = jnp.arange(experts, dtype=jnp.int32)
    hits = (flat[:, None] == numbers[None, :]).astype(jnp.int32)
    before = jnp.cumsum(hits, axis=0)
    slot_of = jnp.sum((before * hits).reshape(tokens, TOP, experts), axis=1) - 1
    one_hot = (slot_of.T[:, None, :] == jnp.arange(ext, dtype=jnp.int32)[None, :, None]).astype(bf16)
    stat_rows = (experts + 8) // 8 * 8
    slot_rows = jnp.pad(slot_of.T, ((0, stat_rows - experts), (0, 0)), constant_values=-1)
    slot_columns = jnp.pad(slot_of.astype(f32), ((0, 0), (0, 128 - experts)), constant_values=-1.0)

    def exchange(values):
        return lax.all_to_all(values, "ex", split_axis=0, concat_axis=0, tiled=True)

    turned = (ex - numbers + experts) % experts
    slot_grads = jnp.einsum("est,tf->esf", one_hot, cotangent, preferred_element_type=f32).astype(bf16)
    up_low = jnp.swapaxes(lax.optimization_barrier(expert_up[0].astype(bf16)), 0, 1)
    down_low = expert_down[0].astype(bf16)

    x_all, slot_grads, up_low, down_low = lax.optimization_barrier((x_all, slot_grads, up_low, down_low))
    grad_rows = []
    for s in range(experts):
        block = pick(slot_grads, (ex + s) % experts)
        if s > 0:
            block = lax.ppermute(block, "ex", [(i, (i + s) % experts) for i in range(experts)])
        grad_rows.append(block)
    up_both = lax.all_gather(up_low.reshape(-1, up_low.shape[2]), "half", axis=0, tiled=True)
    up_both = up_both.reshape((2,) + up_low.shape)
    down_both = lax.all_gather(down_low, "half", axis=0, tiled=True).reshape((2,) + down_low.shape)

    ends = jnp.cumsum(lengths[0])
    at = jnp.arange(tokens, dtype=jnp.int32)
    starts = jnp.max(jnp.where(ends[None, :] <= at[:, None], ends[None, :], 0), axis=1).astype(jnp.int32)
    vectors = bias_vectors(rel_bias, tokens)
    first, qkv, attended, lse = attention_forward(
        x_all, gains_all, weight, places[None, :], places[:, None], starts[:, None], vectors
    )
    attended, *grad_rows = lax.optimization_barrier((attended, *grad_rows))
    grad_blocks = [
        lax.ppermute(block, "col", [(i, (i + k) % columns) for i in range(columns)]) if k else block
        for block in grad_rows
        for k in range(columns)
    ]
    router_rows = jnp.pad((norm_gains[1][:, None] * router).T, ((0, stat_rows - experts), (0, 0)))
    second, mixed, gates, table = project(
        attended, weight, layer_in, norm_gains[1:], router_rows, slot_rows, experts, columns
    )

    home, y, dup, ddown = expert_block(
        mixed, slot_rows, gates, grad_blocks, up_both, down_both, columns
    )
    branch, grad_two, drouter, dgain_two = settle(
        home, slot_columns, table, second, mixed, cotangent, norm_gains[1:],
        jnp.pad(router.T, ((0, 128 - experts), (0, 0))), stat_rows, experts, columns,
    )
    y_home = lax.psum_scatter(y.reshape(quarters, experts, ext, part), ("row", "col"), scatter_dimension=0, tiled=False)
    y_home = exchange(jnp.take(y_home, turned, axis=0))
    gained = jnp.einsum("est,esf->tf", one_hot, y_home, preferred_element_type=f32)
    layer_out = (second + gained).astype(bf16)

    dfirst, dweight, dvectors = attention_backward(
        branch, qkv, lse, attended, first, weight, places[None, :], places[:, None], starts[:, None], vectors
    )
    small = jnp.concatenate([jnp.zeros((8, part), f32), dgain_two, drouter, dvectors.reshape(-1, part)])
    input_grad, grad_parts, sums = finish(
        dfirst, dweight.reshape(2, 2 * experts, -1, 4 * hc), small, layer_in, grad_two, norm_gains[:1], lse,
        experts, columns,
    )
    grad_gains = jnp.stack([sums[0], sums[8]])
    grad_router = sums[16 : 16 + experts].T
    grad_bias = bias_gradient(sums[16 + stat_rows :].reshape(dvectors.shape), head_count, tokens)
    grad_qkv = jnp.moveaxis(grad_parts[:, :, : 3 * hc], 0, 1).reshape(qkv_weight.shape)
    grad_proj = jnp.swapaxes(grad_parts[:, :, 3 * hc :], 1, 2).reshape(proj_weight.shape)

    def sum_halves(parts):
        other = lax.ppermute(pick(parts, 1 - half), "half", [(0, 1), (1, 0)])
        return (pick(parts, half).astype(f32) + other.astype(f32)).astype(bf16)

    grad_up = with_layout_constraint(jnp.swapaxes(sum_halves(dup), 0, 1), Layout((0, 1, 2)))
    grad_up = grad_up[None].astype(f32)
    grad_down = sum_halves(ddown)[None].astype(f32)

    gains = adamw_step(norm_gains, grad_gains, gain_first, gain_second, 0.5)
    bias = adamw_step(rel_bias, grad_bias, bias_first, bias_second, 1.0)
    routers = adamw_step(router, grad_router, router_first, router_second, 2.0 * (2 * D) ** (-0.5))
    qkvs = adamw_step(qkv_weight, grad_qkv, qkv_first, qkv_second, 2.0 * D ** (-0.5))
    projs = adamw_step(proj_weight, grad_proj, proj_first, proj_second, 2.0 * (HEADS * HD / 8) ** (-0.5))
    ups = adamw_step(expert_up, grad_up, up_first, up_second, 2.0 * D ** (-0.5))
    downs = adamw_step(expert_down, grad_down, down_first, down_second, 2.0 * (FF / 2) ** (-0.5))
    out = (layer_out, input_grad) + gains + bias + routers
    for group in (qkvs, projs, ups, downs):
        out = out + group + (group[0].astype(bf16),)
    return out


def solution(mesh):
    shape = mesh.devices.shape
    fine = Mesh(
        mesh.devices.reshape((shape[0] // 2, 2) + shape[1:]), ("ex", "half", "row", "col")
    )
    dp, grid = ("ex", "half"), ("row", "col")
    tokens, own = P(dp, grid), P(dp, None)
    gain, router = P(None, grid), P(grid, None)
    qkv, proj = P("row", dp, None, None, None, "col"), P(None, "col", "row", dp, None)
    up, down = P(dp, "row", None, "col"), P(dp, "col", "row")
    in_specs = (
        (tokens, own, own, own, tokens) + (gain,) * 6 + (router,) * 3
        + (qkv,) * 3 + (proj,) * 3 + (up,) * 3 + (down,) * 3
    )
    out_specs = (
        (tokens, tokens) + (gain,) * 6 + (router,) * 3
        + (qkv,) * 4 + (proj,) * 4 + (up,) * 4 + (down,) * 4
    )
    return jax.shard_map(local, mesh=fine, in_specs=in_specs, out_specs=out_specs, check_vma=False)
```

time: 732 us -> 517 us (0.71)
  waiting for transfers between devices: 237 us -> 33.5 us
  blocking collectives: 200 us -> 0 us
  Pallas kernels: 98.1 us -> 293 us
  local copies, waits for them, and re-layouts: 42.4 us -> 102 us
  matrix products: 40 us -> 9.31 us
  starting transfers between devices: 41.9 us -> 21.4 us
  other arithmetic: 46.2 us -> 34.8 us
    pallas_call x1 -> x5, Pallas kernels: 50.3 us -> 253 us  [the longest x1 91.6 us: expert_block(): pl.pallas_call(functools.partial(expert_kernel, columns, experts), out_sh...]
    all_to_all x3 -> x0, blocking collectives: 109 us -> none  [exchange(): return lax.all_to_all(values, 'ex', split_axis=0, concat_axis=0, tiled=True)]
    reduce_scatter x4 -> x1, waiting for transfers between devices: 79 us -> 0.02 us  [local(): lax.psum_scatter(y.reshape(quarters, experts, ext, part), ('row', 'col'),...]
    unnamed x134 -> x133, local copies, waits for them, and re-layouts: 11 us -> 70 us
    all_gather x5 -> x2, waiting for transfers between devices: 49.5 us -> 0.02 us  [the longest x1 0.02 us: local(): lax.all_gather(down_low, 'half', axis=0, tiled=True)]
    unnamed x11 -> x3, waiting for transfers between devices: 48.7 us -> 0.73 us
    psum x4 -> x0, blocking collectives: 47.6 us -> none  [the longest x1 21.9 us: local(): lax.psum((jnp.stack([grad_gain_one, grad_gain_two]), grad_bias, grad_rout...]
    all_gather x2 -> x0, blocking collectives: 44 us -> none  [the longest x1 35.3 us: local(): proj = lax.all_gather(proj_both, both, axis=1).reshape(D, hc)]
  transfers between devices with their start and end apart: 23 -> 13, of which waited for: 11 -> 1; matrix products, arithmetic and copies ran while one was open for 14% -> 18% of each run, Pallas kernels for 4% -> 32%
where the time goes in v2:
time: 517 us; the launch traced here: 509 us
  Pallas kernels  293 us (57%)
  local copies, waits for them, and re-layouts  102 us (20%)
  other arithmetic  34.8 us (7%)
  waiting for transfers between devices  33.5 us (6%)
  starting transfers between devices  21.4 us (4%)
  between operations  14.8 us (3%)
  matrix products  9.31 us (2%)
    pallas_call x1, Pallas kernels, expert_block(): pl.pallas_call(functools.partial(expert_kernel, columns, experts), out_sh...  91.6 us
    unnamed x133, local copies, waits for them, and re-layouts  70 us
    pallas_call x1, Pallas kernels, finish(): pl.pallas_call(functools.partial(finish_kernel, columns, experts), out_sh...  45 us
    pallas_call x1, Pallas kernels, project(): pl.pallas_call(functools.partial(project_kernel, columns, experts), out_s...  41.2 us
    pallas_call x1, Pallas kernels, settle(): pl.pallas_call(functools.partial(settle_kernel, columns, experts), out_sh...  37.6 us
    pallas_call x1, Pallas kernels, gather(): pl.pallas_call(functools.partial(gather_kernel, columns, experts), out_sh...  37.4 us
    ppermute x2, waiting for transfers between devices, sum_halves(): other = lax.ppermute(pick(parts, 1 - half), 'half', [(0, 1), (1, 0)])  32.7 us
    pallas_call x1, Pallas kernels, attention_backward(): pl.pallas_call(attention_backward_kernel, out_shape=(jax.ShapeDtypeStruct...  21.8 us
  transfers between devices with their start and end apart: 13, of which 1 were waited for; matrix products, arithmetic and copies ran while one was open for 18% of the time, Pallas kernels for 32%

profile of v2, /device:TPU:0, one launch (start us, length us, event | category | flops | bytes accessed | tf_op | source)
XLA Modules:
  0.0 508.8 jit_solution(3244002824471060488)
XLA Ops:
  27.6 37.4 %gather.8 = (bf16[4,1024,256]{2,1,0:T(8,128)(2,1)S(1)}, f32[4,8,256]{2,1,0:T(8,128)S(1)}, bf16[2,8,64,1024]{3,2,1,0:T(8,128)(2,1)S(1)}) custom-call(bf16[1024,256]{1,0:T(8,128)(2,1)S(1)} %copy-done, f32[8,256]{1,0:T(8,128)S(1)} %pad.20.gain_ref, bf16[2,64,1024]{2,1,0:T(8,128)(2,1)S(1)} %pad_maximum_fusion.shard_ref), custom_call_target="tpu_custom_call" | custom-call | bytes 105000000 | tf_op jit(solution)/shard_map/gather/pallas_call | solution.py:606
  70.0 5.7 %collective-permute-start.1 = (bf16[656,256]{1,0:T(8,128)(2,1)}, bf16[656,256]{1,0:T(8,128)(2,1)}, u32[]{:S(2)}, u32[]{:S(2)}) collective-permute-start(bf16[656,256]{1,0:T(8,128)(2,1)} %get-tuple-element.281), channel_id=1, source_target_pairs={{0,16},{8,24},{16,0},{24,8},{1,17},{9,25},{17,1},{25,9},{2,18},{10... | collective-permute-start | bytes 1007624 | tf_op jit(solution)/shard_map/ppermute | solution.py:1265
  75.7 3.4 collective-permute-start.2
  82.7 18.0 %attention_forward.1 = (bf16[4,1024,256]{2,1,0:T(8,128)(2,1)S(1)}, bf16[1024,768]{1,0:T(8,128)(2,1)S(1)}, bf16[1024,256]{1,0:T(8,128)(2,1)S(1)}, f32[1024,128]{1,0:T(8,128)S(1)}) custom-call(bf16[4,1024,256]{2,1,0:T(8,128)(2,1)S(1)} %copy-done.5, f32[4,8,256]{2,1,0:T(8,128)S(1)} %get-tuple-element.63.gain_ref, bf16[1024,1024]{1,0:T(8,128)(2,1)S(1)} %bitcast.196, ...), custom_call_target="tpu_custom_call" | custom-call | bytes 70000000 | tf_op jit(solution)/shard_map/attention_forward/pallas_call | solution.py:174
  108.2 41.2 %project.1 = (f32[1024,256]{1,0:T(8,128)S(1)}, bf16[1024,256]{1,0:T(8,128)(2,1)S(1)}, f32[8,1024]{1,0:T(8,128)S(1)}, f32[1024,128]{1,0:T(8,128)S(1)}) custom-call(bf16[1024,256]{1,0:T(8,128)(2,1)S(1)} %get-tuple-element.67.attended_ref, bf16[1024,1024]{1,0:T(8,128)(2,1)S(1)} %bitcast.197, bf16[1024,256]{1,0:T(8,128)(2,1)S(1)} %copy-done.1, ...), custom_call_target="tpu_custom_call" | custom-call | bytes 77000000 | tf_op jit(solution)/shard_map/project/pallas_call | solution.py:448
  153.4 4.6 copy.259
  158.0 91.6 %expert_block.1 = (bf16[4,656,256]{2,1,0:T(8,128)(2,1)}, bf16[2,2,4,656,256]{4,3,2,1,0:T(8,128)(2,1)}, bf16[2,2,512,704]{3,2,1,0:T(8,128)(2,1)}, bf16[2,704,512]{2,1,0:T(8,128)(2,1)}) custom-call(bf16[1024,256]{1,0:T(8,128)(2,1)} %copy-done.15, s32[8,1024]{1,0:T(8,128)} %copy-done.29, f32[8,1024]{1,0:T(8,128)} %copy-done.31, ...), custom_call_target="tpu_custom_call" | custom-call | bytes 280000000 | tf_op jit(solution)/shard_map/expert_block/pallas_call | solution.py:928
  249.7 5.7 %copy.282 = f32[1,512,2,704]{3,2,1,0:T(2,128)} copy(f32[1,512,2,704]{1,3,2,0:T(8,128)} %param.49) | data formatting | bytes 5767168 | tf_op args[20]
  255.4 5.9 %copy.274 = f32[1,512,2,704]{3,2,1,0:T(2,128)} copy(f32[1,512,2,704]{1,3,2,0:T(8,128)} %param.50) | data formatting | bytes 5767168 | tf_op args[21]
  261.3 6.2 %copy.279 = f32[1,512,2,704]{3,2,1,0:T(2,128)} copy(f32[1,512,2,704]{1,3,2,0:T(8,128)} %param.51) | data formatting | bytes 5767168 | tf_op args[22]
  276.3 37.6 %settle.1 = (bf16[4,1024,256]{2,1,0:T(8,128)(2,1)S(1)}, f32[1024,256]{1,0:T(8,128)S(1)}, f32[8,256]{1,0:T(8,128)S(1)}, f32[8,256]{1,0:T(8,128)S(1)}) custom-call(bf16[4,656,256]{2,1,0:T(8,128)(2,1)S(1)} %copy-done.19, f32[1024,128]{1,0:T(8,128)S(1)} %copy-done.3, f32[1024,128]{1,0:T(8,128)S(1)} %copy-done.28, f32[1024,256]{1,0:T(8,128)S(1)} %copy-done.21, ...), custom_call_target="tpu_custom_call" | custom-call | bytes 87500000 | tf_op jit(solution)/shard_map/settle/pallas_call | solution.py:1022
  315.7 21.8 %attention_backward.1 = (bf16[4,1024,256]{2,1,0:T(8,128)(2,1)S(1)}, bf16[1024,1024]{1,0:T(8,128)(2,1)S(1)}, f32[12,512]{1,0:T(8,128)S(1)}) custom-call(bf16[4,1024,256]{2,1,0:T(8,128)(2,1)S(1)} %get-tuple-element.80.branch_ref, bf16[1024,768]{1,0:T(8,128)(2,1)S(1)} %copy-done.18, f32[1024,128]{1,0:T(8,128)S(1)} %copy-done.13, ...), custom_call_target="tpu_custom_call" | custom-call | bytes 98000000 | tf_op jit(solution)/shard_map/attention_backward/pallas_call | solution.py:276
  343.6 45.0 %finish.1 = (bf16[1024,256]{1,0:T(8,128)(2,1)S(1)}, f32[2,64,1024]{2,1,0:T(8,128)S(1)}, f32[48,256]{1,0:T(8,128)S(1)}) custom-call(bf16[4,1024,256]{2,1,0:T(8,128)(2,1)} %copy-done.6, bf16[2,8,64,1024]{3,2,1,0:T(8,128)(2,1)} %bitcast.199, f32[48,256]{1,0:T(8,128)S(1)} %pad_maximum_fusion.1.small_ref, bf16[1024,256]{1,0:T(8,128)(2,1)S(1)} %copy-done.2, ...), custom_call_target="tpu_custom_call" | custom-call | bytes 112000000 | tf_op jit(solution)/shard_map/finish/pallas_call | solution.py:1164
  397.2 4.9 copy.276
  408.7 32.7 %collective-permute-done.8 = bf16[704,512]{1,0:T(8,128)(2,1)} collective-permute-done((bf16[704,512]{1,0:T(8,128)(2,1)}, bf16[704,512]{1,0:T(8,128)(2,1)}, u32[]{:S(2)}, u32[]{:S(2)}) %collective-permute-start.8) | collective-permute-done | bytes 720928 | tf_op jit(solution)/shard_map/ppermute | solution.py:1316
  441.4 5.2 %fusion.39 = (bf16[1,704,512]{2,1,0:T(8,128)(2,1)}, f32[1,704,512]{2,1,0:T(8,128)}, f32[1,704,512]{2,1,0:T(8,128)}, f32[1,704,512]{2,1,0:T(8,128)}) fusion(f32[1,704,512]{2,1,0:T(8,128)S(1)} %copy-done.37, bf16[704,512]{1,0:T(8,128)(2,1)} %collective-permute-done.8, bf16[2,704,512]{2,1,0:T(8,128)(2,1)} %get-tuple-element.94, s32[]{:T(128)S(6)} %select_n.113, ...), kind=kLoop, calls=%fused_computation.109 | loop fusion | flops 7208960 | bytes 10813444 | tf_op jit(solution)/shard_map/convert_element_type | solution.py:1332
  446.6 3.9 copy.278
  453.8 5.7 %all-to-all-start = ((bf16[4,656,256]{2,1,0:T(8,128)(2,1)}), bf16[4,656,256]{2,1,0:T(8,128)(2,1)}, u32[]{:S(2)}, u32[]{:S(2)}) async-start(bf16[4,656,256]{2,1,0:T(8,128)(2,1)} %broadcast_select_fusion), calls=%async_computation.1 | async-start | bytes 2686976 | tf_op jit(solution)/shard_map/all_to_all | solution.py:1253
  459.5 16.0 %fusion.42 = (bf16[1,512,2,704]{3,2,1,0:T(2,128)(2,1)}, f32[1,512,2,704]{3,2,1,0:T(2,128)}, f32[1,512,2,704]{3,2,1,0:T(2,128)}, f32[1,512,2,704]{3,2,1,0:T(2,128)}) fusion(f32[1,512,2,704]{3,2,1,0:T(2,128)} %copy.282, bf16[2,512,704]{2,0,1:T(2,128)(2,1)S(1)} %copy.278, bf16[2,2,512,704]{3,1,2,0:T(2,128)(2,1)} %copy.276, s32[]{:T(128)S(6)} %select_n.113, ...), kind=kLoop, calls=%fused_computation.110 | loop fusion | flops 14417920 | bytes 21626884 | tf_op jit(solution)/shard_map/convert_element_type | solution.py:1332
  475.5 5.6 %copy.291 = f32[1,512,2,704]{1,3,2,0:T(8,128)} copy(f32[1,512,2,704]{3,2,1,0:T(2,128)} %get-tuple-element.262) | data formatting | bytes 5767168
  481.1 5.6 %copy.292 = f32[1,512,2,704]{1,3,2,0:T(8,128)} copy(f32[1,512,2,704]{3,2,1,0:T(2,128)} %get-tuple-element.263) | data formatting | bytes 5767168
  486.8 5.8 %copy.293 = f32[1,512,2,704]{1,3,2,0:T(8,128)} copy(f32[1,512,2,704]{3,2,1,0:T(2,128)} %get-tuple-element.264) | data formatting | bytes 5767168
  492.5 3.5 copy.294
  496.0 5.2 %fusion.16 = bf16[1024,256]{1,0:T(8,128)(2,1)} fusion(f32[1024,256]{1,0:T(8,128)S(1)} %copy-done.22, bf16[4,656,256]{2,1,0:T(8,128)(2,1)} %all-to-all-done, s32[4,1024]{1,0:T(4,128)S(1)} %copy.253), kind=kOutput, calls=%fused_computation.29 | convolution fusion | flops 1378942976 | bytes 2932736 | tf_op jit(solution)/shard_map/est,esf->tf/dot_general | solution.py:1298
  (211 shorter events, 75.7 us)
Async XLA Ops:
  7.2 146.2 %all-gather.3.cloned.1.call-start = ((), (), s32[]{:S(2)}) async-start(), calls=%async_computation.2 | async-start | bytes 4325376 | tf_op jit(solution)/shard_map/all_gather | solution.py:1267
  25.5 40.8 %copy-start.35 = (bf16[512,2,704]{0,2,1:T(8,128)(2,1)S(1)}, bf16[512,2,704]{0,2,1:T(8,128)(2,1)}, u32[]{:S(2)}) copy-start(bf16[512,2,704]{0,2,1:T(8,128)(2,1)} %convert_bitcast_fusion) | copy-start | bytes 4325380
  67.7 90.4 %all-gather.5.cloned.1.call-start = ((), (), s32[]{:S(2)}) async-start(), calls=%async_computation.3 | async-start | bytes 2162688 | tf_op jit(solution)/shard_map/all_gather | solution.py:1269
  68.4 382.1 %reduce-scatter.2.cloned.1.call-start = ((), (), s32[]{:S(2)}) async-start(), calls=%async_computation.4 | async-start | bytes 6717440 | tf_op jit(solution)/shard_map/reduce_scatter | solution.py:1296
  68.5 11.3 %copy-start.51 = (f32[32,4]{0,1:T(4,128)S(1)}, f32[32,4]{0,1:T(4,128)}, u32[]{:S(2)}) copy-start(f32[32,4]{0,1:T(4,128)} %param.37) | copy-start | bytes 1540
  69.7 34.3 %collective-permute-start = (bf16[656,256]{1,0:T(8,128)(2,1)}, bf16[656,256]{1,0:T(8,128)(2,1)}, u32[]{:S(2)}, u32[]{:S(2)}) collective-permute-start(bf16[656,256]{1,0:T(8,128)(2,1)} %get-tuple-element.282), channel_id=1, source_target_pairs={{0,8},{8,16},{16,24},{24,0},{1,9},{9,17},{17,25},{25,1},{2,10},{10... | collective-permute-start | bytes 1007624 | tf_op jit(solution)/shard_map/ppermute | solution.py:1265
  70.0 34.0 %collective-permute-start.1 = (bf16[656,256]{1,0:T(8,128)(2,1)}, bf16[656,256]{1,0:T(8,128)(2,1)}, u32[]{:S(2)}, u32[]{:S(2)}) collective-permute-start(bf16[656,256]{1,0:T(8,128)(2,1)} %get-tuple-element.281), channel_id=1, source_target_pairs={{0,16},{8,24},{16,0},{24,8},{1,17},{9,25},{17,1},{25,9},{2,18},{10... | collective-permute-start | bytes 1007624 | tf_op jit(solution)/shard_map/ppermute | solution.py:1265
  75.7 28.3 %collective-permute-start.2 = (bf16[656,256]{1,0:T(8,128)(2,1)}, bf16[656,256]{1,0:T(8,128)(2,1)}, u32[]{:S(2)}, u32[]{:S(2)}) collective-permute-start(bf16[656,256]{1,0:T(8,128)(2,1)} %get-tuple-element.280), channel_id=1, source_target_pairs={{0,24},{8,0},{16,8},{24,16},{1,25},{9,1},{17,9},{25,17},{2,26},{10... | collective-permute-start | bytes 1007624 | tf_op jit(solution)/shard_map/ppermute | solution.py:1265
  82.7 25.4 %copy-start.49 = (f32[256,4]{0,1:T(4,128)S(1)}, f32[256,4]{0,1:T(4,128)}, u32[]{:S(2)}) copy-start(f32[256,4]{0,1:T(4,128)} %param.40) | copy-start | bytes 12292
  82.7 25.4 %copy-start.1 = (bf16[1024,256]{1,0:T(8,128)(2,1)S(1)}, bf16[1024,256]{1,0:T(8,128)(2,1)}, u32[]{:S(2)}) copy-start(bf16[1024,256]{1,0:T(8,128)(2,1)} %layer_ref.5) | copy-start | bytes 1572868
  104.0 54.0 %collective-permute-start.3 = (bf16[656,256]{1,0:T(8,128)(2,1)}, bf16[656,256]{1,0:T(8,128)(2,1)}, u32[]{:S(2)}, u32[]{:S(2)}) collective-permute-start(bf16[656,256]{1,0:T(8,128)(2,1)} %get-tuple-element.73.refs_5_), channel_id=1, source_target_pairs={{0,1},{1,0},{2,3},{3,2},{4,5},{5,4},{6,7},{7,6},{8,9},{9,8},{10,11... | collective-permute-start | bytes 1007624 | tf_op jit(solution)/shard_map/ppermute | solution.py:1280
  105.6 52.4 %collective-permute-start.4 = (bf16[656,256]{1,0:T(8,128)(2,1)}, bf16[656,256]{1,0:T(8,128)(2,1)}, u32[]{:S(2)}, u32[]{:S(2)}) collective-permute-start(bf16[656,256]{1,0:T(8,128)(2,1)} %collective-permute-done.refs_7_), channel_id=1, source_target_pairs={{0,1},{1,0},{2,3},{3,2},{4,5},{5,4},{6,7},{7,6},{8,9},{9,8},{10,11... | collective-permute-start | bytes 1007624 | tf_op jit(solution)/shard_map/ppermute | solution.py:1280
  106.1 51.9 %collective-permute-start.5 = (bf16[656,256]{1,0:T(8,128)(2,1)}, bf16[656,256]{1,0:T(8,128)(2,1)}, u32[]{:S(2)}, u32[]{:S(2)}) collective-permute-start(bf16[656,256]{1,0:T(8,128)(2,1)} %collective-permute-done.1.refs_9_), channel_id=1, source_target_pairs={{0,1},{1,0},{2,3},{3,2},{4,5},{5,4},{6,7},{7,6},{8,9},{9,8},{10,11... | collective-permute-start | bytes 1007624 | tf_op jit(solution)/shard_map/ppermute | solution.py:1280
  107.7 50.3 %collective-permute-start.6 = (bf16[656,256]{1,0:T(8,128)(2,1)}, bf16[656,256]{1,0:T(8,128)(2,1)}, u32[]{:S(2)}, u32[]{:S(2)}) collective-permute-start(bf16[656,256]{1,0:T(8,128)(2,1)} %collective-permute-done.2.refs_11_), channel_id=1, source_target_pairs={{0,1},{1,0},{2,3},{3,2},{4,5},{5,4},{6,7},{7,6},{8,9},{9,8},{10,11... | collective-permute-start | bytes 1007624 | tf_op jit(solution)/shard_map/ppermute | solution.py:1280
  108.2 41.3 %copy-start.29 = (s32[8,1024]{1,0:T(8,128)}, s32[8,1024]{1,0:T(8,128)S(1)}, u32[]{:S(2)}) copy-start(s32[8,1024]{1,0:T(8,128)S(1)} %pad.22.clone.slot_ref.refs_1_) | copy-start | bytes 98308
  276.3 37.6 %copy-start.9 = (bf16[1024,256]{1,0:T(8,128)(2,1)S(1)}, bf16[1024,256]{1,0:T(8,128)(2,1)}, u32[]{:S(2)}) copy-start(bf16[1024,256]{1,0:T(8,128)(2,1)} %copy-done.8) | copy-start | bytes 1572868
  276.3 37.6 %copy-start.11 = (bf16[4,1024,256]{2,1,0:T(8,128)(2,1)S(1)}, bf16[4,1024,256]{2,1,0:T(8,128)(2,1)}, u32[]{:S(2)}) copy-start(bf16[4,1024,256]{2,1,0:T(8,128)(2,1)} %copy-done.10) | copy-start | bytes 6291460
  276.3 37.6 %copy-start.13 = (f32[1024,128]{1,0:T(8,128)S(1)}, f32[1024,128]{1,0:T(8,128)}, u32[]{:S(2)}) copy-start(f32[1024,128]{1,0:T(8,128)} %copy-done.12) | copy-start | bytes 1572868
  313.9 23.6 %copy-start.23 = (f32[1024,256]{1,0:T(8,128)}, f32[1024,256]{1,0:T(8,128)S(1)}, u32[]{:S(2)}) copy-start(f32[1024,256]{1,0:T(8,128)S(1)} %get-tuple-element.89.two_ref) | copy-start | bytes 3145732
  392.1 54.5 %collective-permute-start.7 = (bf16[2,512,704]{1,2,0:T(8,128)(2,1)}, bf16[2,512,704]{1,2,0:T(8,128)(2,1)}, u32[]{:S(2)}, u32[]{:S(2)}) collective-permute-start(bf16[2,512,704]{1,2,0:T(8,128)(2,1)} %bitcast.207), channel_id=1, source_target_pairs={{0,4},{4,0},{1,5},{5,1},{2,6},{6,2},{3,7},{7,3},{8,12},{12,8},{9,1... | collective-permute-start | bytes 4325384 | tf_op jit(solution)/shard_map/ppermute | solution.py:1316
  394.9 46.4 %collective-permute-start.8 = (bf16[704,512]{1,0:T(8,128)(2,1)}, bf16[704,512]{1,0:T(8,128)(2,1)}, u32[]{:S(2)}, u32[]{:S(2)}) collective-permute-start(bf16[704,512]{1,0:T(8,128)(2,1)} %dynamic-slice_bitcast_fusion), channel_id=1, source_target_pairs={{0,4},{4,0},{1,5},{5,1},{2,6},{6,2},{3,7},{7,3},{8,12},{12,8},{9,1... | collective-permute-start | bytes 2162696 | tf_op jit(solution)/shard_map/ppermute | solution.py:1316
  403.3 38.1 %copy-start.37 = (f32[1,704,512]{2,1,0:T(8,128)S(1)}, f32[1,704,512]{2,1,0:T(8,128)}, u32[]{:S(2)}) copy-start(f32[1,704,512]{2,1,0:T(8,128)} %param.52) | copy-start | bytes 4325380
  403.3 38.1 %copy-start.40 = (f32[1,704,512]{2,1,0:T(8,128)S(1)}, f32[1,704,512]{2,1,0:T(8,128)}, u32[]{:S(2)}) copy-start(f32[1,704,512]{2,1,0:T(8,128)} %param.53) | copy-start | bytes 4325380
  453.8 42.3 %all-to-all-start = ((bf16[4,656,256]{2,1,0:T(8,128)(2,1)}), bf16[4,656,256]{2,1,0:T(8,128)(2,1)}, u32[]{:S(2)}, u32[]{:S(2)}) async-start(bf16[4,656,256]{2,1,0:T(8,128)(2,1)} %broadcast_select_fusion), calls=%async_computation.1 | async-start | bytes 2686976 | tf_op jit(solution)/shard_map/all_to_all | solution.py:1253
  (49 other events, 151.5 us)
Sparse Core Ops, SparseCore 0:
  67.8 44.6 all-gather.2
  114.6 25.7 all-gather.4
  249.8 60.9 reduce-scatter.1

commit v3 on v2

v3 whole, which is shorter than its diff:
```python
import functools

import jax
import jax.numpy as jnp
import numpy as np
from jax import lax
from jax.experimental import pallas as pl
from jax.experimental.pallas import tpu as pltpu
from jax.sharding import Mesh, PartitionSpec as P

D = 1024
HEADS = 16
FF = 2816
TOP = 2
STEP = 5
beta_first = 0.5
beta_second = 0.5
adam_epsilon = 1e-08
weight_decay = 0.01
highest = lax.Precision.HIGHEST
EXTRA = 16
HD = 64
BUCKETS = 32
LONGEST = 512
TILE = 256
norm_epsilon = 1e-06
hidden_score = -1e30
bucket_edges = np.floor(16.0 * 2.0 ** (np.arange(16) * 0.375)).astype(np.int32)
f32 = jnp.float32
bf16 = jnp.bfloat16
MIB = 1 << 20


def dot_nn(a, b):
    return lax.dot_general(a, b, (((1,), (0,)), ((), ())), preferred_element_type=f32)


def dot_nt(a, b):
    return lax.dot_general(a, b, (((1,), (1,)), ((), ())), preferred_element_type=f32)


def dot_tn(a, b):
    return lax.dot_general(a, b, (((0,), (0,)), ((), ())), preferred_element_type=f32)


def tile_reach(tokens):
    return min(tokens // TILE, (LONGEST - 1 + TILE - 1) // TILE + 1)


def toeplitz_places(tokens):
    reach = tile_reach(tokens)
    m = np.arange(2 * TILE)
    base = np.where(m < TILE, -m, 2 * TILE - m)
    distance = np.arange(reach)[:, None] * TILE + base[None, :]
    clipped = np.maximum(distance, 0)
    buckets = np.where(
        clipped < 16, clipped, 15 + (clipped[..., None] >= bucket_edges).sum(-1)
    )
    return (distance, buckets)


def bias_vectors(rel_bias, tokens):
    distance, buckets = toeplitz_places(tokens)
    table = jnp.asarray((buckets[..., None] == np.arange(BUCKETS)).astype(np.float32))
    values = jnp.einsum("dmb,bh->hdm", table, rel_bias, precision=lax.Precision.HIGHEST)
    values = jnp.where(jnp.asarray(distance < 0)[None], hidden_score, values)
    return values.reshape(-1, 2 * TILE)


def bias_gradient(vectors, head_count, tokens):
    distance, buckets = toeplitz_places(tokens)
    table = ((buckets[..., None] == np.arange(BUCKETS)) & (distance >= 0)[..., None]).astype(np.float32)
    return jnp.einsum(
        "dmb,hdm->bh",
        jnp.asarray(table),
        vectors.reshape(head_count, distance.shape[0], 2 * TILE),
        precision=lax.Precision.HIGHEST,
    )


def fill_bias(vector_ref, bias):
    for i in range(bias.shape[0]):
        wide = jnp.broadcast_to(vector_ref[i : i + 1, :], (TILE, 2 * TILE))
        bias[i] = pltpu.roll(wide, 0, 1, stride=1, stride_axis=0)[:, :TILE]


def head_lanes(shape, head):
    return lax.broadcasted_iota(jnp.int32, shape, 1) // HD == head


def given_table(place_row, tokens):
    return jnp.where(
        place_row[...] == lax.broadcasted_iota(jnp.int32, (tokens, tokens), 0), 1.0, 0.0
    ).astype(bf16)


def sequence_starts(length_ref, tokens):
    at = lax.broadcasted_iota(jnp.int32, (tokens, 1), 0)
    starts = jnp.zeros((tokens, 1), jnp.int32)
    end = 0
    for k in range(length_ref.shape[1]):
        end = end + length_ref[0, k]
        starts = jnp.where(at >= end, end, starts)
    return starts


def attention_forward_kernel(
    x_ref, gain_ref, weight_ref, place_row, length_ref, vector_ref,
    first_ref, qkv_ref, attended_ref, lse_ref, bias, placed_out, between,
):
    quarters, tokens, part = x_ref.shape
    width = quarters * part
    hc = weight_ref.shape[1] // 4
    head_count = hc // HD
    reach = bias.shape[0] // head_count
    fill_bias(vector_ref, bias)
    squares = jnp.zeros((tokens, 1), f32)
    for q in range(quarters):
        v = x_ref[q].astype(f32)
        squares = squares + jnp.sum(v * v, axis=1, keepdims=True)
    inverse = lax.rsqrt(squares / width + norm_epsilon)
    total = jnp.zeros((tokens, 3 * hc), f32)
    for q in range(quarters):
        first = (x_ref[q].astype(f32) * inverse * gain_ref[q, :1]).astype(bf16)
        first_ref[q] = first
        total = total + dot_nn(first, weight_ref[q * part : (q + 1) * part, : 3 * hc])
    to_given = given_table(place_row, tokens)
    all_starts = sequence_starts(length_ref, tokens)
    scale = jnp.where(
        lax.broadcasted_iota(jnp.int32, (1, 3 * hc), 1) < hc, HD ** (-0.5), 1.0
    )
    qkv_ref[...] = dot_tn(to_given, (total * scale).astype(bf16)).astype(bf16)
    between(-1)
    for a in range(tokens // TILE):
        rows = slice(a * TILE, (a + 1) * TILE)
        blocks = range(max(0, a - reach + 1), a + 1)
        starts = all_starts[rows, :]
        visible = [
            b * TILE + lax.broadcasted_iota(jnp.int32, (TILE, TILE), 1) >= starts for b in blocks
        ]

        def one_head(head, carry):
            out, lse = carry
            mine = head_lanes((TILE, hc), head)
            query = jnp.where(mine, qkv_ref[rows, :hc], 0)
            scores = []
            for b, seen in zip(blocks, visible):
                s = dot_nt(query, qkv_ref[b * TILE : (b + 1) * TILE, hc : 2 * hc])
                scores.append(jnp.where(seen, s + bias[head * reach + a - b], hidden_score))
            top = functools.reduce(jnp.maximum, [jnp.max(s, axis=1, keepdims=True) for s in scores])
            exps = [jnp.exp(s - top) for s in scores]
            denominator = functools.reduce(jnp.add, [jnp.sum(e, axis=1, keepdims=True) for e in exps])
            share = 1.0 / denominator
            value = jnp.zeros((TILE, hc), f32)
            for b, e in zip(blocks, exps):
                value = value + dot_nn(
                    (e * share).astype(bf16), qkv_ref[b * TILE : (b + 1) * TILE, 2 * hc :]
                )
            lane = lax.broadcasted_iota(jnp.int32, (TILE, 128), 1)
            return (
                jnp.where(mine, value, out),
                jnp.where(lane == head, top + jnp.log(denominator), lse),
            )

        out, lse = lax.fori_loop(
            0, head_count, one_head, (jnp.zeros((TILE, hc), f32), jnp.zeros((TILE, 128), f32))
        )
        placed_out[rows, :] = out.astype(bf16)
        lse_ref[rows, :] = lse
        between(a)
    lane = lax.broadcasted_iota(jnp.int32, (tokens, 128), 1)
    lse_ref[...] = jnp.where(lane == 127, inverse, lse_ref[...])
    attended_ref[...] = dot_nn(to_given, placed_out[...]).astype(bf16)


def microseconds(time):
    return pl.CostEstimate(flops=0, bytes_accessed=int(time * 3.5e6), transcendentals=0)


def vmem():
    return pl.BlockSpec(memory_space=pltpu.VMEM)


def hbm():
    return pl.BlockSpec(memory_space=pltpu.HBM)


def attention_backward_kernel(
    branch_ref, qkv_ref, lse_ref, attended_ref, first_ref, weight_ref,
    place_row, length_ref, vector_ref,
    dfirst_ref, dweight_ref, dvector_ref,
    bias, dbias, grad_ref, dqkv, dkv, between, after_dfirst,
):
    quarters, tokens, part = branch_ref.shape
    hc = weight_ref.shape[1] // 4
    head_count = hc // HD
    reach = bias.shape[0] // head_count
    fill_bias(vector_ref, bias)
    dbias[...] = jnp.zeros_like(dbias)
    dkv[...] = jnp.zeros_like(dkv)
    total = jnp.zeros((tokens, hc), f32)
    for q in range(quarters):
        dims = slice(q * part, (q + 1) * part)
        total = total + dot_nn(branch_ref[q], weight_ref[dims, 3 * hc :])
        dweight_ref[dims, 3 * hc :] = dot_tn(branch_ref[q], attended_ref[...]).astype(bf16)
    to_given = given_table(place_row, tokens)
    all_starts = sequence_starts(length_ref, tokens)
    grad_ref[...] = dot_tn(to_given, total.astype(bf16)).astype(bf16)
    for a in range(tokens // TILE):
        rows = slice(a * TILE, (a + 1) * TILE)
        blocks = range(max(0, a - reach + 1), a + 1)
        starts = all_starts[rows, :]
        visible = [
            b * TILE + lax.broadcasted_iota(jnp.int32, (TILE, TILE), 1) >= starts for b in blocks
        ]

        def one_head(head, dquery):
            mine = head_lanes((TILE, hc), head)
            query = jnp.where(mine, qkv_ref[rows, :hc], 0)
            grad = jnp.where(mine, grad_ref[rows, :], 0)
            lane = lax.broadcasted_iota(jnp.int32, (TILE, 128), 1)
            lse = jnp.sum(jnp.where(lane == head, lse_ref[rows, :], 0.0), axis=1, keepdims=True)
            probs, dprobs = [], []
            inner = jnp.zeros((TILE, 1), f32)
            for b, seen in zip(blocks, visible):
                keys = slice(b * TILE, (b + 1) * TILE)
                s = dot_nt(query, qkv_ref[keys, hc : 2 * hc]) + bias[head * reach + a - b]
                p = jnp.where(seen, jnp.exp(s - lse), 0.0)
                d = dot_nt(grad, qkv_ref[keys, 2 * hc :])
                inner = inner + jnp.sum(p * d, axis=1, keepdims=True)
                probs.append(p)
                dprobs.append(d)
            for b, p, d in zip(blocks, probs, dprobs):
                keys = slice(b * TILE, (b + 1) * TILE)
                ds = p * (d - inner)
                place = head * reach + a - b
                dbias[place] = dbias[place] + ds
                low = ds.astype(bf16)
                dquery = dquery + dot_nn(low, jnp.where(mine, qkv_ref[keys, hc : 2 * hc], 0))
                dkv[keys, :hc] = dkv[keys, :hc] + dot_tn(low, query)
                dkv[keys, hc:] = dkv[keys, hc:] + dot_tn(p.astype(bf16), grad)
            return dquery

        dquery = lax.fori_loop(0, head_count, one_head, jnp.zeros((TILE, hc), f32))
        dqkv[rows, :hc] = (dquery * HD ** (-0.5)).astype(bf16)
        between(a)
    dqkv[:, hc:] = dkv[...].astype(bf16)
    given = dot_nn(to_given, dqkv[...]).astype(bf16)
    for q in range(quarters):
        dfirst_ref[q] = dot_nt(given, weight_ref[q * part : (q + 1) * part, : 3 * hc]).astype(bf16)
    after_dfirst()
    for q in range(quarters):
        dims = slice(q * part, (q + 1) * part)
        dweight_ref[dims, : 3 * hc] = dot_tn(first_ref[q], given).astype(bf16)
    for i in range(dbias.shape[0]):
        wide = jnp.concatenate([dbias[i], jnp.zeros((TILE, TILE), f32)], axis=1)
        level = wide[:8]
        for g in range(8, TILE, 8):
            level = level + pltpu.roll(wide[g : g + 8], 2 * TILE - g, 1)
        row = level[:1]
        for s in range(1, 8):
            row = row + pltpu.roll(level[s : s + 1], 2 * TILE - s, 1)
        dvector_ref[i : i + 1, :] = row


def half_places(rows, part):
    row = lax.broadcasted_iota(jnp.int32, (rows, EXTRA), 0) // part
    high = lax.broadcasted_iota(jnp.int32, (rows, EXTRA), 1)
    column = lax.broadcasted_iota(jnp.int32, (rows, part), 0) % part
    return (row, high, column == lax.broadcasted_iota(jnp.int32, (rows, part), 1))


def write_extra(values, part):
    row, high, column = half_places(values.shape[0], part)
    near = values.astype(bf16)
    left = (values - near.astype(f32)).astype(bf16)
    near_rows = jnp.where(row == high, 1.0, 0.0).astype(bf16)
    left_rows = jnp.where(row + 8 == high, 1.0, 0.0).astype(bf16)
    near_values = jnp.where(column, near.astype(f32), 0.0).astype(bf16)
    left_values = jnp.where(column, left.astype(f32), 0.0).astype(bf16)
    return dot_tn(near_rows, near_values) + dot_tn(left_rows, left_values)


def read_extra(extra, rows):
    part = extra.shape[1]
    row, high, column = half_places(rows, part)
    pick = jnp.where(row == high % 8, 1.0, 0.0).astype(bf16)
    return jnp.sum(jnp.where(column, dot_nn(pick, extra), 0.0), axis=1, keepdims=True)


GELU_A = 0.7978845608028654
GELU_B = 0.044715


MESH = pl.DeviceIdType.MESH


def remote(src, dst, send, recv, where):
    return pltpu.make_async_remote_copy(
        src_ref=src, dst_ref=dst, send_sem=send, recv_sem=recv, device_id=where, device_id_type=MESH
    )


def greet(wheres):
    barrier = pltpu.get_barrier_semaphore()
    for where in wheres:
        pl.semaphore_signal(barrier, inc=1, device_id=where, device_id_type=MESH)
    pl.semaphore_wait(barrier, len(wheres))


def dot_exact(a, b, dims):
    return lax.dot_general(a, b, ((dims, ((), ()))), precision=highest, preferred_element_type=f32)


def grid_peers(columns):
    row, col = lax.axis_index("row"), lax.axis_index("col")
    return [
        {"row": (row + i) % 2, "col": (col + j) % columns}
        for i in range(2)
        for j in range(columns)
        if i + j > 0
    ]


def sum_of_peers(mine, got, send, recv, columns):
    copies = [
        remote(mine, got.at[i], send.at[i], recv.at[i], where)
        for i, where in enumerate(grid_peers(columns))
    ]
    for copy in copies:
        copy.start()
    for copy in copies:
        copy.wait_recv()
    total = mine[...]
    for i in range(len(copies)):
        total = total + got[i]
    for copy in copies:
        copy.wait_send()
    return total


PIECES = 4


def project_part(
    columns, experts,
    attended_ref, weight_ref, layer_ref, gain_ref, router_ref, slot_ref,
    second_ref, mixed_ref, gate_ref, column_ref,
    core_out, core_in, keep, col_out, col_in, stat, stat_in,
    core_send, core_recv, col_send, col_recv, stat_send, stat_recv, after_crossing,
):
    row, col = lax.axis_index("row"), lax.axis_index("col")
    tokens, part = layer_ref.shape
    wide = columns * part
    size = tokens // PIECES
    heads = slice(3 * weight_ref.shape[1] // 4, weight_ref.shape[1])
    own_rows = pl.ds(pl.multiple_of(row * wide, wide), wide)
    other_rows = pl.ds(pl.multiple_of((1 - row) * wide, wide), wide)
    cores = []
    for i in range(PIECES):
        at = slice(i * size, (i + 1) * size)
        core_out[i] = dot_nt(attended_ref[at, :], weight_ref[other_rows, heads]).astype(bf16)
        copy = remote(core_out.at[i], core_in.at[i], core_send.at[i], core_recv.at[i], {"row": 1 - row})
        copy.start()
        cores.append(copy)
        keep[i] = dot_nt(attended_ref[at, :], weight_ref[own_rows, heads])
    own_columns = pl.ds(pl.multiple_of(col * part, part), part)
    crossing = []
    for i in range(PIECES):
        cores[i].wait_recv()
        keep[i] = keep[i] + core_in[i].astype(f32)
        for k in range(1, columns):
            to = (col + k) % columns
            col_out[i, k - 1] = keep[i, :, pl.ds(pl.multiple_of(to * part, part), part)].astype(bf16)
            copy = remote(
                col_out.at[i, k - 1], col_in.at[i, k - 1], col_send.at[i, k - 1], col_recv.at[i, k - 1], {"col": to}
            )
            copy.start()
            crossing.append(copy)
    after_crossing()
    ones = jnp.where(lax.broadcasted_iota(jnp.int32, router_ref.shape, 0) == experts, 1.0, 0.0)
    for i in range(PIECES):
        at = slice(i * size, (i + 1) * size)
        total = layer_ref[at, :].astype(f32) + keep[i, :, own_columns]
        for k in range(1, columns):
            crossing[i * (columns - 1) + k - 1].wait_recv()
            total = total + col_in[i, k - 1].astype(f32)
        second_ref[at, :] = total
        stat[:, at] = dot_exact(router_ref[...] * gain_ref[...], total, ((1,), (1,))) + dot_exact(
            ones, total * total, ((1,), (1,))
        )
    total = sum_of_peers(stat, stat_in, stat_send, stat_recv, columns)
    inverse = lax.rsqrt(total[experts : experts + 1] / D + norm_epsilon)
    routed = slot_ref[...] >= 0
    logits = jnp.where(routed, total * inverse, hidden_score)
    shares = jnp.where(routed, jnp.exp(logits - jnp.max(logits, axis=0, keepdims=True)), 0.0)
    gates = shares / jnp.sum(shares, axis=0, keepdims=True)
    gate_ref[...] = gates
    number = lax.broadcasted_iota(jnp.int32, gates.shape, 0)
    lanes = (gates.shape[0], 128)
    eye = jnp.where(
        lax.broadcasted_iota(jnp.int32, lanes, 0) == lax.broadcasted_iota(jnp.int32, lanes, 1), 1.0, 0.0
    )
    table = dot_exact(jnp.where(number == experts, inverse, gates), eye, ((0,), (0,)))
    column_ref[...] = table
    mixed_ref[...] = (second_ref[...] * table[:, experts : experts + 1] * gain_ref[...]).astype(bf16)
    for copy in cores + crossing:
        copy.wait_send()


def nearest_first(experts):
    return sorted(range(1, experts), key=lambda s: min(s, experts - s))


def farthest_first(experts):
    far = experts // 2
    return [far] + [s for s in range(1, experts) if s != far]


def attend_kernel(columns, experts, *refs):
    x_hbm, gains_ref, weight_hbm, place_row, length_ref, vector_ref, layer_ref, gain_ref, router_ref, slot_ref = refs[:10]
    grad_rows = refs[10 : 10 + experts]
    (
        first_hbm, qkv_hbm, attended_hbm, lse_hbm, second_hbm, column_hbm, mixed_ref, gate_ref, came, crossed,
        first_ref, qkv_ref, attended_ref, lse_ref, second_ref, column_ref,
        bias, placed_out, core_out, core_in, keep, col_out, col_in, stat, stat_in,
        core_send, core_recv, col_send, col_recv, stat_send, stat_recv,
        z_send, z_recv, x_send, x_recv, store, x_ref, weight_ref, load,
    ) = refs[10 + experts :]
    loads = [
        pltpu.make_async_copy(x_hbm, x_ref, load.at[0]),
        pltpu.make_async_copy(weight_hbm, weight_ref, load.at[1]),
    ]
    for copy in loads:
        copy.start()
    ex, col = lax.axis_index("ex"), lax.axis_index("col")
    greet(grid_peers(columns) + [{"ex": (ex + s) % experts} for s in range(1, experts)])

    def z_copy(s):
        return remote(grad_rows[s], came.at[s], z_send.at[s], z_recv.at[s], {"ex": (ex + s) % experts})

    def x_copy(s, k):
        return remote(
            came.at[s], crossed.at[s, k - 1], x_send.at[s, k - 1], x_recv.at[s, k - 1], {"col": (col + k) % columns}
        )

    order = farthest_first(experts)
    z_copy(order[0]).start()
    done = [0]
    for copy in loads:
        copy.wait()

    def advance():
        n = done[0]
        z_copy(order[n]).wait_send()
        if n + 1 < len(order):
            z_copy(order[n + 1]).start()
        z_copy(order[n]).wait_recv()
        if n + 1 < len(order):
            for k in range(1, columns):
                x_copy(order[n], k).start()
        done[0] = n + 1

    def between(a):
        if a == 2:
            advance()

    attention_forward_kernel(
        x_ref, gains_ref, weight_ref, place_row, length_ref, vector_ref,
        first_ref, qkv_ref, attended_ref, lse_ref, bias, placed_out, between,
    )

    def stored(pairs, first):
        copies = [pltpu.make_async_copy(a, b, store.at[first + i]) for i, (a, b) in enumerate(pairs)]
        for copy in copies:
            copy.start()
        return copies

    stores = stored(
        [(first_ref, first_hbm), (qkv_ref, qkv_hbm), (attended_ref, attended_hbm), (lse_ref, lse_hbm)], 0
    )

    def after_crossing():
        while done[0] + 1 < len(order):
            advance()

    project_part(
        columns, experts,
        attended_ref, weight_ref, layer_ref, gain_ref, router_ref, slot_ref,
        second_ref, mixed_ref, gate_ref, column_ref,
        core_out, core_in, keep, col_out, col_in, stat, stat_in,
        core_send, core_recv, col_send, col_recv, stat_send, stat_recv, after_crossing,
    )
    stores = stores + stored([(second_ref, second_hbm), (column_ref, column_hbm)], 4)
    advance()
    for copy in stores:
        copy.wait()
    for s in order[:-1]:
        for k in range(1, columns):
            x_copy(s, k).wait()


def attend(x, gains, weight, placing, lengths, vectors, layer_in, gain, router_rows, slots, grad_rows, columns):
    quarters, tokens, part = x.shape
    experts = len(grad_rows)
    ext = grad_rows[0].shape[0]
    hc = weight.shape[1] // 4
    size = tokens // PIECES
    rows = router_rows.shape[0]
    dma = pltpu.SemaphoreType.DMA
    others = columns - 1
    kept = (
        jax.ShapeDtypeStruct(x.shape, bf16),
        jax.ShapeDtypeStruct((tokens, 3 * hc), bf16),
        jax.ShapeDtypeStruct((tokens, hc), bf16),
        jax.ShapeDtypeStruct((tokens, 128), f32),
        jax.ShapeDtypeStruct((tokens, part), f32),
        jax.ShapeDtypeStruct((tokens, 128), f32),
    )
    return pl.pallas_call(
        functools.partial(attend_kernel, columns, experts),
        out_shape=kept
        + (
            jax.ShapeDtypeStruct((tokens, part), bf16),
            jax.ShapeDtypeStruct((rows, tokens), f32),
            jax.ShapeDtypeStruct((experts, ext, part), bf16),
            jax.ShapeDtypeStruct((experts, others, ext, part), bf16),
        ),
        in_specs=[hbm(), vmem(), hbm(), vmem(), pl.BlockSpec(memory_space=pltpu.SMEM)]
        + [vmem()] * 5
        + [hbm()] * experts,
        out_specs=(hbm(),) * 6 + (vmem(),) * 2 + (hbm(),) * 2,
        scratch_shapes=[pltpu.VMEM(each.shape, each.dtype) for each in kept]
        + [
            pltpu.VMEM((vectors.shape[0], TILE, TILE), f32),
            pltpu.VMEM((tokens, hc), bf16),
            pltpu.VMEM((PIECES, size, columns * part), bf16),
            pltpu.VMEM((PIECES, size, columns * part), bf16),
            pltpu.VMEM((PIECES, size, columns * part), f32),
            pltpu.VMEM((PIECES, others, size, part), bf16),
            pltpu.VMEM((PIECES, others, size, part), bf16),
            pltpu.VMEM((rows, tokens), f32),
            pltpu.VMEM((quarters - 1, rows, tokens), f32),
            dma((PIECES,)), dma((PIECES,)), dma((PIECES, others)), dma((PIECES, others)),
            dma((quarters - 1,)), dma((quarters - 1,)),
            dma((experts,)), dma((experts,)), dma((experts, others)), dma((experts, others)), dma((6,)),
            pltpu.VMEM(x.shape, bf16), pltpu.VMEM(weight.shape, bf16), dma((2,)),
        ],
        compiler_params=pltpu.CompilerParams(
            collective_id=1, has_side_effects=True, vmem_limit_bytes=52 * MIB
        ),
        cost_estimate=microseconds(45),
        name="attend",
    )(x, gains, weight, placing, lengths, vectors, layer_in, gain, router_rows, slots, *grad_rows)


def gather_kernel(columns, experts, *refs):
    layer_ref, gain_ref, shard_ref, place_row, route_ref, cotangent_ref = refs[:6]
    x_ref, gains_ref, weight_ref, slot_row_ref, slot_column_ref, crossed_ref = refs[6:12]
    slot_grads = refs[12 : 12 + experts]
    (
        x_send, x_recv, own_send, own_recv, pass_send, pass_recv, gain_send, gain_recv,
        swap_send, swap_recv, z_send, z_recv, y_send, y_recv, place, cross_send, cross_recv,
        stay, slots, slot_store,
    ) = refs[12 + experts :]
    ex, half = lax.axis_index("ex"), lax.axis_index("half")
    row, col = lax.axis_index("row"), lax.axis_index("col")
    mine = row * columns + col
    tokens, part = layer_ref.shape
    greet(
        grid_peers(columns)
        + [{"ex": (ex + s) % experts} for s in range(1, experts)]
        + [{"half": 1 - half}]
    )
    spread = Spread(
        x_ref, layer_ref, columns, x_send, x_recv, own_send, own_recv, pass_send, pass_recv, stay
    )
    member = 2 * ex + half
    swap = remote(
        shard_ref.at[1 - row], weight_ref.at[row, member], swap_send.at[0], swap_recv.at[0], {"row": 1 - row}
    )
    swap.start()
    arrived = remote(
        shard_ref.at[1 - row], weight_ref.at[1 - row, member], swap_send.at[0], swap_recv.at[0], {"row": 1 - row}
    )
    place_shard = pltpu.make_async_copy(shard_ref.at[row], weight_ref.at[row, member], place.at[0])
    place_shard.start()
    spread.start()

    def z_copy(s, a):
        block = weight_ref.at[a, member]
        return remote(block, block, z_send.at[s, a], z_recv.at[s, a], {"ex": (ex + s) % experts})

    def z_arrival(s, a):
        block = weight_ref.at[a, 2 * ((ex - s + experts) % experts) + half]
        return remote(block, block, z_send.at[s, a], z_recv.at[s, a], {"ex": (ex + s) % experts})

    def y_copy(s, a):
        block = weight_ref.at[a, 2 * ((ex - s + experts) % experts) + half]
        return remote(block, block, y_send.at[s, a], y_recv.at[s, a], {"half": 1 - half})

    def y_arrival(s, a):
        block = weight_ref.at[a, 2 * ((ex - s + experts) % experts) + 1 - half]
        return remote(block, block, y_send.at[s, a], y_recv.at[s, a], {"half": 1 - half})

    queue = [(s, a) for s in nearest_first(experts) for a in (row, 1 - row)]
    place_shard.wait()
    z_copy(*queue[0]).start()
    y_copy(0, row).start()
    arrived.wait_recv()
    z_copy(*queue[1]).start()
    y_copy(0, 1 - row).start()
    gains_ref[mine] = gain_ref[...]
    gain_copies = [
        remote(gain_ref, gains_ref.at[mine], gain_send.at[i], gain_recv.at[i], where)
        for i, where in enumerate(grid_peers(columns))
    ]
    for copy in gain_copies:
        copy.start()

    lane = lax.broadcasted_iota(jnp.int32, (tokens, 128), 1)
    placed_hits = (route_ref[:, :1] == lane) | (route_ref[:, 1:2] == lane)
    to_given = given_table(place_row, tokens)
    hits = dot_nn(to_given, jnp.where(placed_hits, 1.0, 0.0).astype(bf16))
    low_hits = hits.astype(bf16)
    first_at = lax.broadcasted_iota(jnp.int32, (tokens, tokens), 0)
    second_at = lax.broadcasted_iota(jnp.int32, (tokens, tokens), 1)
    up_to = jnp.where(second_at <= first_at, 1.0, 0.0).astype(bf16)
    slot_column_ref[...] = jnp.where(hits > 0.5, dot_nn(up_to, low_hits) - 1.0, -1.0)
    from_on = jnp.where(first_at <= second_at, 1.0, 0.0).astype(bf16)
    same = jnp.where(first_at == second_at, 1.0, 0.0).astype(bf16)
    rows = slot_row_ref.shape[0]
    row_counts = dot_tn(low_hits, from_on)[:rows]
    slot_row_ref[...] = jnp.where(dot_tn(low_hits, same)[:rows] > 0.5, row_counts - 1.0, -1.0)

    def cotangent_slots(s):
        e = (ex + s) % experts
        ext = slot_grads[s].shape[0]
        hit = slot_row_ref[pl.ds(e, 1), :] == lax.broadcasted_iota(jnp.int32, (ext, tokens), 0).astype(f32)
        slots[s] = dot_nn(jnp.where(hit, 1.0, 0.0).astype(bf16), cotangent_ref[...]).astype(bf16)
        pltpu.make_async_copy(slots.at[s], slot_grads[s], slot_store.at[s]).start()

    crossing = [
        remote(
            slots.at[0], crossed_ref.at[k - 1], cross_send.at[k - 1], cross_recv.at[k - 1],
            {"col": (col + k) % columns},
        )
        for k in range(1, columns)
    ]
    cotangent_slots(0)
    for copy in crossing:
        copy.start()
    made = 1
    for i, (s, a) in enumerate(queue):
        z_copy(s, a).wait_send()
        if i + 2 < len(queue):
            z_copy(*queue[i + 2]).start()
        z_arrival(s, a).wait_recv()
        y_copy(s, a).start()
        if i == 0:
            spread.hand_on()
        while made < experts * (i + 1) // len(queue):
            cotangent_slots(made)
            made += 1
    spread.finish()
    for copy in gain_copies + crossing:
        copy.wait()
    for s in range(experts):
        pltpu.make_async_copy(slots.at[s], slot_grads[s], slot_store.at[s]).wait()
    swap.wait_send()
    for s in range(experts):
        for a in range(2):
            y_arrival(s, a).wait_recv()
            y_copy(s, a).wait_send()


class Spread:
    def __init__(
        self, out, source, columns, x_send, x_recv, own_send, own_recv, pass_send, pass_recv, stay=None
    ):
        self.stay = stay
        row, col = lax.axis_index("row"), lax.axis_index("col")
        mine = row * columns + col
        size = source.shape[0] // PIECES
        self.out, self.source, self.mine = out, source, mine
        self.across, self.own, self.passed = [], [], []
        for i in range(PIECES):
            at = pl.ds(i * size, size)
            for k in range(1, columns):
                self.across.append(
                    remote(
                        source.at[at], out.at[mine, at], x_send.at[i, k - 1], x_recv.at[i, k - 1],
                        {"col": (col + k) % columns},
                    )
                )
                block = out.at[row * columns + (col - k + columns) % columns, at]
                self.passed.append(
                    remote(block, block, pass_send.at[i, k - 1], pass_recv.at[i, k - 1], {"row": 1 - row})
                )
            self.own.append(
                remote(source.at[at], out.at[mine, at], own_send.at[i], own_recv.at[i], {"row": 1 - row})
            )

    def start(self):
        for i in range(PIECES):
            self.start_piece(i)

    def start_piece(self, i):
        others = len(self.across) // PIECES
        for copy in self.across[i * others : (i + 1) * others] + [self.own[i]]:
            copy.start()
        size = self.source.shape[0] // PIECES
        at = pl.ds(i * size, size)
        if self.stay is None:
            self.out[self.mine, at] = self.source[at]
        else:
            pltpu.make_async_copy(self.source.at[at], self.out.at[self.mine, at], self.stay.at[i]).start()

    def hand_on(self):
        for across, passed in zip(self.across, self.passed):
            across.wait_recv()
            passed.start()

    def finish(self):
        if self.stay is not None:
            size = self.source.shape[0] // PIECES
            for i in range(PIECES):
                at = pl.ds(i * size, size)
                pltpu.make_async_copy(self.source.at[at], self.out.at[self.mine, at], self.stay.at[i]).wait()
        for copy in self.own + self.passed:
            copy.wait_recv()
        for copy in self.across + self.own + self.passed:
            copy.wait_send()


def spread_semaphores(columns):
    dma = pltpu.SemaphoreType.DMA
    return [dma((PIECES, columns - 1))] * 2 + [dma((PIECES,))] * 2 + [dma((PIECES, columns - 1))] * 2


def gather(layer_in, gains, shard, place_row, routes, cotangent, stat_rows, ext, experts, columns):
    tokens, part = layer_in.shape
    _, rows, width = shard.shape
    quarters = 2 * columns
    dma = pltpu.SemaphoreType.DMA
    return pl.pallas_call(
        functools.partial(gather_kernel, columns, experts),
        out_shape=(
            jax.ShapeDtypeStruct((quarters, tokens, part), bf16),
            jax.ShapeDtypeStruct((quarters,) + gains.shape, f32),
            jax.ShapeDtypeStruct((2, 2 * experts, rows, width), bf16),
            jax.ShapeDtypeStruct((stat_rows, tokens), f32),
            jax.ShapeDtypeStruct((tokens, 128), f32),
            jax.ShapeDtypeStruct((columns - 1, ext, part), bf16),
        )
        + (jax.ShapeDtypeStruct((ext, part), bf16),) * experts,
        in_specs=[vmem()] * 6,
        out_specs=(hbm(), vmem(), hbm(), vmem(), vmem()) + (hbm(),) * (1 + experts),
        scratch_shapes=spread_semaphores(columns)
        + [
            dma((quarters - 1,)), dma((quarters - 1,)), dma((1,)), dma((1,)),
            dma((experts, 2)), dma((experts, 2)), dma((experts, 2)), dma((experts, 2)), dma((1,)),
            dma((columns - 1,)), dma((columns - 1,)), dma((PIECES,)),
            pltpu.VMEM((experts, ext, part), bf16), dma((experts,)),
        ],
        compiler_params=pltpu.CompilerParams(
            collective_id=0, has_side_effects=True, vmem_limit_bytes=52 * MIB
        ),
        cost_estimate=microseconds(30),
        name="gather",
    )(layer_in, gains, shard, place_row, routes, cotangent)


def expert_kernel(
    columns, experts,
    *refs,
):
    mixed_ref, slot_ref, gate_ref, weight_hbm, own_grads, own_crossed, came, crossed = refs[:8]
    (
        home_ref, y_hbm, y_far, keep_up, keep_down, away_up, away_down,
        x, xs, grads, weight, da, db, scaled, core_out, core_in, keep, col_out, col_in,
        load, grad_load, grad_send, grad_recv, z_send, z_recv, own_send, own_recv, col_send, col_recv, pass_send, pass_recv,
        core_send, core_recv, back_send, back_recv, home_send, home_recv, y_send, y_recv, y_sem, store, far_send, far_recv,
        free, last_send, last_recv, on_send, on_recv, y_far_send, y_far_recv,
    ) = refs[8:]
    ex, half = lax.axis_index("ex"), lax.axis_index("half")
    row, col = lax.axis_index("row"), lax.axis_index("col")
    tokens, part = mixed_ref.shape
    ext = x.shape[2]
    cap = ext - EXTRA
    quarters = 2 * columns
    wide = columns * part
    mine = row * columns + col
    last = experts - 1
    greet(
        [{"ex": (ex + s) % experts} for s in range(1, experts)]
        + [{"col": (col + k) % columns} for k in range(1, columns)]
        + [{"row": 1 - row}]
    )

    own_dims = pl.ds(pl.multiple_of(row * wide, wide), wide)
    other_dims = pl.ds(pl.multiple_of((1 - row) * wide, wide), wide)
    loads = [pltpu.make_async_copy(weight_hbm.at[row], weight.at[:, :, own_dims], load.at[0])]
    handed = [
        remote(weight_hbm.at[1 - row], weight.at[:, :, own_dims], load.at[1], load.at[2], {"row": 1 - row})
    ]
    final_chunk = farthest_first(experts)[-1]
    for s in range(experts):
        for k in range(columns):
            if k and s == final_chunk:
                continue
            at = (s, k)
            place = row * columns + (col - k + columns) % columns
            if s == 0:
                block = own_crossed.at[k - 1] if k else own_grads
            else:
                block = crossed.at[s, k - 1] if k else came.at[s]
            loads.append(pltpu.make_async_copy(block, grads.at[place, s], grad_load.at[at]))
            handed.append(
                remote(block, grads.at[place, s], grad_send.at[at], grad_recv.at[at], {"row": 1 - row})
            )
    for copy in loads + handed:
        copy.start()

    def last_copy(k):
        return remote(
            came.at[final_chunk], grads.at[mine, final_chunk], last_send.at[k - 1], last_recv.at[k - 1],
            {"col": (col + k) % columns},
        )

    def last_on(k):
        block = grads.at[row * columns + (col - k + columns) % columns, final_chunk]
        return remote(block, block, on_send.at[k - 1], on_recv.at[k - 1], {"row": 1 - row})

    def z_copy(s):
        return remote(
            xs.at[s], x.at[mine, s], z_send.at[s], z_recv.at[s], {"ex": (ex + s) % experts}
        )

    def own_copy(s):
        block = x.at[mine, s]
        return remote(block, block, own_send.at[s], own_recv.at[s], {"row": 1 - row})

    def col_copy(s, k):
        block = x.at[mine, s]
        return remote(
            block, block, col_send.at[s, k - 1], col_recv.at[s, k - 1], {"col": (col + k) % columns}
        )

    def pass_copy(s, k):
        block = x.at[row * columns + (col - k + columns) % columns, s]
        return remote(
            block, block, pass_send.at[s, k - 1], pass_recv.at[s, k - 1], {"row": 1 - row}
        )

    def spread(s):
        own_copy(s).start()
        for k in range(1, columns):
            col_copy(s, k).start()

    def hand_on(s):
        for k in range(1, columns):
            col_copy(s, k).wait_recv()
            pass_copy(s, k).start()

    def slots_of(e):
        hit = slot_ref[pl.ds(e, 1), :] == lax.broadcasted_iota(jnp.int32, (cap, tokens), 0).astype(f32)
        values = dot_nn(jnp.where(hit, 1.0, 0.0).astype(bf16), mixed_ref[...]).astype(bf16)
        gate = jnp.sum(jnp.where(hit, gate_ref[pl.ds(e, 1), :], 0.0), axis=1, keepdims=True)
        return values, write_extra(gate, part).astype(bf16)

    def build(s):
        values, extra = slots_of((ex + s) % experts)
        xs[s, :cap] = values
        xs[s, cap:] = extra

    def nth(p):
        far = experts // 2
        return jnp.where(p == 1, far, jnp.where((p > 1) & (p <= far), p - 1, p))

    build(nth(1))
    z_copy(nth(1)).start()
    values, extra = slots_of(ex)
    x[mine, 0, :cap] = values
    x[mine, 0, cap:] = extra
    spread(0)
    for k in range(1, columns):
        last_copy(k).start()

    @pl.loop(2, experts)
    def _(p):
        build(nth(p))

    for copy in loads:
        copy.wait()
    for copy in handed:
        copy.wait()
    hand_on(0)
    z_copy(nth(1)).wait_send()
    z_copy(nth(2)).start()
    z_copy(nth(1)).wait_recv()
    spread(nth(1))

    def core_copy(s):
        return remote(core_out.at[s], core_in.at[s], core_send.at[s], core_recv.at[s], {"row": 1 - row})

    def back_copy(s, k):
        return remote(
            col_out.at[s, k - 1], col_in.at[s, k - 1], back_send.at[s, k - 1], back_recv.at[s, k - 1],
            {"col": (col + k) % columns},
        )

    def home_copy(s):
        return remote(
            xs.at[s], home_ref.at[s], home_send.at[s], home_recv.at[s], {"ex": (ex - s + experts) % experts}
        )

    def stores(ups, downs):
        parts = [(weight.at[:2], ups, 0), (weight.at[2], downs, 1)]
        return [
            (
                pltpu.make_async_copy(source.at[(slice(None),) * (2 - i) + (own_dims,)], out, store.at[i]),
                remote(
                    source.at[(slice(None),) * (2 - i) + (other_dims,)], out, far_send.at[i], far_recv.at[i],
                    {"row": 1 - row},
                ),
            )
            for source, out, i in parts
        ]

    def store_gradients(i):
        for mine_here, (ups, downs) in ((True, (keep_up, keep_down)), (False, (away_up, away_down))):

            @pl.when((row == half) == mine_here)
            def _():
                for copy in stores(ups, downs)[i]:
                    copy.start()

    def wait_gradients(i):
        for copy in stores(keep_up, keep_down)[i]:
            copy.wait()

    def y_share(s):
        return remote(core_out.at[s], core_in.at[s], y_send.at[s], y_recv.at[s], {"row": 1 - row})

    def y_copy(s):
        return pltpu.make_async_copy(core_in.at[s], y_hbm.at[:, s], y_sem.at[s])

    def after_core(s, slot):
        core_copy(s).wait_recv()
        keep[slot] = keep[slot] + core_in[s].astype(f32)
        for k in range(1, columns):
            to = (col + k) % columns
            col_out[s, k - 1] = keep[slot, to].astype(bf16)
            back_copy(s, k).start()

    def after_columns(s, slot):
        total = keep[slot, col]
        for k in range(1, columns):
            back_copy(s, k).wait_recv()
            total = total + col_in[s, k - 1].astype(f32)
        return total.astype(bf16)

    def send_home(s, slot):
        xs[s] = after_columns(s, slot)
        home_copy(s).start()

    @pl.loop(0, experts)
    def _(p):
        s = nth(p)
        slot = jnp.where(p == 0, 2, p % 2)

        @pl.when(p == 1)
        def _():
            for k in range(1, columns):
                last_copy(k).wait_recv()
                last_on(k).start()

        @pl.when(p == last)
        def _():
            for k in range(1, columns):
                last_on(k).wait_recv()

        grad = jnp.concatenate([grads[q, s] for q in range(quarters)], axis=1)
        d = dot_nt(grad, weight[2])
        own_copy(s).wait_recv()
        for k in range(1, columns):
            pass_copy(s, k).wait_recv()

        @pl.when(p > 1)
        def _():
            after_core(nth(p - 1), (p - 1) % 2)

        @pl.when(p > 2)
        def _():
            send_home(nth(p - 2), p % 2)

        rows = jnp.concatenate([x[q, s] for q in range(quarters)], axis=1)
        gate = read_extra(x[mine, s, cap:], ext)
        a = dot_nt(rows, weight[0])
        b = dot_nt(rows, weight[1])
        d = d * gate
        square = a * a
        t = jnp.tanh(a * (GELU_A + (GELU_A * GELU_B) * square))
        part_on = 0.5 + 0.5 * t
        smooth = a * part_on
        slope = part_on + (a * (0.5 - 0.5 * t * t)) * (GELU_A + (3 * GELU_A * GELU_B) * square)
        active = smooth * b
        da[s] = (d * b * slope).astype(bf16)
        db[s] = (d * smooth).astype(bf16)
        scaled[s] = (active * gate).astype(bf16)
        extra = write_extra(jnp.sum(d * active, axis=1, keepdims=True), part)

        @pl.when((p > 0) & (p + 2 < experts))
        def _():
            z_copy(nth(p + 2)).wait_recv()
            spread(nth(p + 2))

        @pl.when((p > 0) & (p + 1 < experts))
        def _():
            hand_on(nth(p + 1))

        @pl.when((p > 0) & (p + 3 < experts))
        def _():
            z_copy(nth(p + 2)).wait_send()
            z_copy(nth(p + 3)).start()

        for j in range(columns):
            dims = pl.ds(pl.multiple_of(((1 - row) * columns + j) * part, part), part)
            value = dot_nn(da[s], weight[0, :, dims]) + dot_nn(db[s], weight[1, :, dims])
            core_out[s, j] = value.astype(bf16)
            core_out[s, j, cap:] = extra.astype(bf16)
        core_copy(s).start()
        for j in range(columns):
            dims = pl.ds(pl.multiple_of((row * columns + j) * part, part), part)
            keep[slot, j] = dot_nn(da[s], weight[0, :, dims]) + dot_nn(db[s], weight[1, :, dims])
            keep[slot, j, cap:] = extra

        @pl.when(p == 0)
        def _():
            hand_on(nth(1))
            z_copy(nth(2)).wait_send()
            z_copy(nth(3)).start()
            z_copy(nth(2)).wait_recv()
            spread(nth(2))

    def flat(ref, *at):
        block = ref[at] if at else ref[...]
        return block.reshape(experts * ext, block.shape[-1])

    before, final = nth(last - 1), nth(last)
    z_copy(final).wait_send()
    after_core(final, last % 2)
    after_core(0, 2)
    pl.semaphore_signal(free, inc=1, device_id={"row": 1 - row}, device_id_type=MESH)
    send_home(before, (last - 1) % 2)

    pl.semaphore_wait(free, 1)

    @pl.loop(0, experts)
    def _(s):
        core_copy(s).wait_send()
        for j in range(columns):
            dims = pl.ds(pl.multiple_of(((1 - row) * columns + j) * part, part), part)
            core_out[s, j] = dot_nn(scaled[s], weight[2, :, dims]).astype(bf16)
        y_share(s).start()

    def y_far_copy(k):
        return remote(
            core_in.at[nth(1), (col + k) % columns], y_far.at[k - 1], y_far_send.at[k - 1], y_far_recv.at[k - 1],
            {"col": (col + k) % columns},
        )

    @pl.loop(0, experts)
    def _(p):
        s = nth((p + 1) % experts)
        y_share(s).wait_recv()
        for j in range(columns):
            dims = pl.ds(pl.multiple_of((row * columns + j) * part, part), part)
            value = dot_nn(scaled[s], weight[2, :, dims]) + core_in[s, j].astype(f32)
            core_in[s, j] = value.astype(bf16)
        y_copy(s).start()

        @pl.when(p == 0)
        def _():
            for k in range(1, columns):
                y_far_copy(k).start()

    send_home(final, last % 2)
    for g, hidden in enumerate((da, db)):
        low = flat(hidden)
        for q in range(quarters):
            weight[g, :, q * part : (q + 1) * part] = dot_tn(low, flat(x, q)).astype(bf16)
    store_gradients(0)
    low = flat(scaled)
    for q in range(quarters):
        weight[2, :, q * part : (q + 1) * part] = dot_tn(low, flat(grads, q)).astype(bf16)
    store_gradients(1)
    home_ref[0] = after_columns(0, 2)
    wait_gradients(0)
    wait_gradients(1)
    for k in range(1, columns):
        y_far_copy(k).wait()
        last_copy(k).wait_send()
        last_on(k).wait_send()

    @pl.loop(1, experts)
    def _(s):
        home_copy(s).wait_recv()
        home_copy(s).wait_send()

    @pl.loop(0, experts)
    def _(s):
        own_copy(s).wait_send()
        y_share(s).wait_send()
        y_copy(s).wait()
        for k in range(1, columns):
            col_copy(s, k).wait_send()
            pass_copy(s, k).wait_send()
            back_copy(s, k).wait_send()


def expert_block(mixed, slots, gates, weights, own_grads, own_crossed, came, crossed, columns):
    tokens, part = mixed.shape
    quarters = 2 * columns
    experts, ext, _ = came.shape
    _, _, ff, wide = weights.shape
    dma = pltpu.SemaphoreType.DMA
    others = columns - 1
    return pl.pallas_call(
        functools.partial(expert_kernel, columns, experts),
        out_shape=(
            jax.ShapeDtypeStruct((experts, ext, part), bf16),
            jax.ShapeDtypeStruct((columns, experts, ext, part), bf16),
            jax.ShapeDtypeStruct((others, ext, part), bf16),
        )
        + (jax.ShapeDtypeStruct((2, ff, wide), bf16), jax.ShapeDtypeStruct((ff, wide), bf16)) * 2,
        in_specs=[vmem()] * 3 + [hbm()] * 5,
        out_specs=(vmem(),) + (hbm(),) * 6,
        scratch_shapes=[
            pltpu.VMEM((quarters, experts, ext, part), bf16),
            pltpu.VMEM((experts, ext, part), bf16),
            pltpu.VMEM((quarters, experts, ext, part), bf16),
            pltpu.VMEM((3, ff, D), bf16),
            pltpu.VMEM((experts, ext, ff), bf16),
            pltpu.VMEM((experts, ext, ff), bf16),
            pltpu.VMEM((experts, ext, ff), bf16),
            pltpu.VMEM((experts, columns, ext, part), bf16),
            pltpu.VMEM((experts, columns, ext, part), bf16),
            pltpu.VMEM((3, columns, ext, part), f32),
            pltpu.VMEM((experts, others, ext, part), bf16),
            pltpu.VMEM((experts, others, ext, part), bf16),
            dma((3,)), dma((experts, columns)), dma((experts, columns)), dma((experts, columns)),
            dma((experts,)), dma((experts,)), dma((experts,)), dma((experts,)),
            dma((experts, others)), dma((experts, others)), dma((experts, others)), dma((experts, others)),
            dma((experts,)), dma((experts,)), dma((experts, others)), dma((experts, others)),
            dma((experts,)), dma((experts,)), dma((experts,)), dma((experts,)), dma((experts,)),
            dma((2,)), dma((2,)), dma((2,)), pltpu.SemaphoreType.REGULAR,
            dma((others,)), dma((others,)), dma((others,)), dma((others,)), dma((others,)), dma((others,)),
        ],
        compiler_params=pltpu.CompilerParams(
            collective_id=2, has_side_effects=True, vmem_limit_bytes=56 * MIB
        ),
        cost_estimate=microseconds(80),
        name="expert_block",
    )(mixed, slots, gates, weights, own_grads, own_crossed, came, crossed)


def settle_part(
    columns, experts,
    home_ref, slot_ref, column_ref, second_ref, mixed_ref, cotangent_ref, gain_ref, router_ref,
    branch_ref, two_ref, drouter_ref, dgain_ref,
    low, dmixed_ref, dlogit_ref, stat, stat_in, stat_send, stat_recv, *rest,
):
    *spread_sems, after_spread = rest
    ex = lax.axis_index("ex")
    tokens, part = second_ref.shape
    ext = home_ref.shape[1]
    cap = ext - EXTRA
    size = tokens // PIECES
    lane = lax.broadcasted_iota(jnp.int32, (size, 128), 1)
    extras = []
    for s in range(experts):
        values = read_extra(home_ref[s, cap:], ext)
        near = values.astype(bf16)
        left = (values - near.astype(f32)).astype(bf16)
        extras.append(
            jnp.concatenate([jnp.broadcast_to(near, (ext, 128)), jnp.broadcast_to(left, (ext, 128))], axis=1)
        )
    peers = grid_peers(columns)
    spread = Spread(branch_ref, low, columns, *spread_sems)

    def stat_copy(i, n):
        at = pl.ds(i * size, size)
        return remote(
            stat.at[:, at], stat_in.at[n, :, at], stat_send.at[i, n], stat_recv.at[i, n], peers[n]
        )

    def combine(i):
        at = slice(i * size, (i + 1) * size)
        dmixed = jnp.zeros((size, part), f32)
        gate_grads = jnp.zeros((size, 128), f32)
        for s in range(experts):
            e = (ex + s) % experts
            place = jnp.sum(jnp.where(lane == e, slot_ref[at, :], 0.0), axis=1, keepdims=True)
            hit = place == lax.broadcasted_iota(jnp.int32, (size, ext), 1).astype(f32)
            pick_rows = jnp.where(hit, 1.0, 0.0).astype(bf16)
            dmixed = dmixed + dot_nn(pick_rows, home_ref[s])
            found = dot_nn(pick_rows, extras[s])
            gate_grads = jnp.where(lane == e, found[:, :128] + found[:, 128:], gate_grads)
        gates = jnp.where(lane < experts, column_ref[at, :], 0.0)
        dlogits = gate_grads - gates * jnp.sum(gate_grads, axis=1, keepdims=True)
        dlogit_ref[at, :] = dlogits
        dmixed = dmixed + dot_exact(dlogits[:, : router_ref.shape[0]], router_ref[...], ((1,), (0,)))
        dmixed_ref[at, :] = dmixed
        stat[:, at] = dot_exact(
            jnp.ones((8, part), f32), second_ref[at, :] * dmixed * gain_ref[...], ((1,), (1,))
        )
        for n in range(len(peers)):
            stat_copy(i, n).start()

    first_row = jnp.where(lax.broadcasted_iota(jnp.int32, (8, 128), 0) == 0, 1.0, 0.0)

    def close(i):
        at = slice(i * size, (i + 1) * size)
        total = stat[:, at]
        for n in range(len(peers)):
            stat_copy(i, n).wait_recv()
            total = total + stat_in[n, :, at]
        row_total = dot_exact(total, first_row, ((0,), (0,)))[:, :1]
        inverse = column_ref[at, experts : experts + 1]
        two = cotangent_ref[at, :].astype(f32) + inverse * (
            dmixed_ref[at, :] * gain_ref[...] - second_ref[at, :] * (inverse * inverse * row_total / D)
        )
        two_ref[at, :] = two
        low[at, :] = two.astype(bf16)
        spread.start_piece(i)

    for i in range(PIECES):
        combine(i)
        if i > 0:
            close(i - 1)
    close(PIECES - 1)
    after_spread()
    rows = drouter_ref.shape[0]
    drouter_ref[...] = dot_exact(dlogit_ref[...], mixed_ref[...].astype(f32), ((0,), (0,)))[:rows]
    normed = second_ref[...] * column_ref[:, experts : experts + 1]
    dgain_ref[...] = jnp.broadcast_to(
        jnp.sum(dmixed_ref[...] * normed, axis=0, keepdims=True), dgain_ref.shape
    )
    spread.hand_on()
    spread.finish()
    for i in range(PIECES):
        for n in range(len(peers)):
            stat_copy(i, n).wait_send()


def finish_part(
    columns, experts,
    dfirst_ref, dweight_ref, small, layer_ref, two_ref, gain_ref, inverse_ref,
    input_grad_ref, qkv_grad_ref, proj_grad_ref, sums_ref,
    core_in, keep, col_out, col_in, stat, stat_in, y_in, z_out, z_in, held, row_out, row_in, small_in,
    core_send, core_recv, col_send, col_recv, stat_send, stat_recv,
    y_send, y_recv, z_send, z_recv, row_send, row_recv, small_send, small_recv, others, while_waiting,
):
    ex, half = lax.axis_index("ex"), lax.axis_index("half")
    row, col = lax.axis_index("row"), lax.axis_index("col")
    tokens, part = layer_ref.shape
    size = tokens // PIECES
    members = 2 * experts
    rows = held.shape[1]
    hc = held.shape[2] // 4

    def core_copy(i):
        at = pl.ds(i * size, size)
        return remote(
            dfirst_ref.at[pl.ds((1 - row) * columns, columns), at], core_in.at[:, at],
            core_send.at[i], core_recv.at[i], {"row": 1 - row},
        )

    def block_of(member, a):
        return pl.ds(pl.multiple_of((a * members + member) * rows, rows), rows)

    def y_copy(s, a):
        to = 2 * ((ex + s) % experts) + 1 - half
        return remote(
            dweight_ref.at[block_of(to, a)], y_in.at[s, a], y_send.at[s, a], y_recv.at[s, a], {"half": 1 - half}
        )

    def z_copy(s, a):
        return remote(
            z_out.at[s, a], z_in.at[s, a], z_send.at[s, a], z_recv.at[s, a], {"ex": (ex + s) % experts}
        )

    queue = [(s, a) for s in nearest_first(experts)[::-1] + [0] for a in range(2)]
    crossing = []
    cell = {}

    def start():
        for i in range(PIECES):
            core_copy(i).start()

    def cross():
        for i in range(PIECES):
            at = slice(i * size, (i + 1) * size)
            core_copy(i).wait_recv()
            for j in range(columns):
                keep[j, at] = dfirst_ref[row * columns + j, at].astype(f32) + core_in[j, at].astype(f32)
            for k in range(1, columns):
                to = (col + k) % columns
                col_out[k - 1, at] = keep[to, at].astype(bf16)
                copy = remote(
                    col_out.at[k - 1, pl.ds(i * size, size)], col_in.at[k - 1, pl.ds(i * size, size)],
                    col_send.at[i, k - 1], col_recv.at[i, k - 1], {"col": to},
                )
                copy.start()
                crossing.append(copy)

    def normed():
        return layer_ref[...].astype(f32) * inverse_ref[:, 127:128]

    peers = grid_peers(columns)

    def stat_copy(n):
        return remote(stat, stat_in.at[n], stat_send.at[n], stat_recv.at[n], peers[n])

    def arrive():
        for copy in crossing:
            copy.wait_recv()
        dnorm = keep[col]
        for k in range(1, columns):
            dnorm = dnorm + col_in[k - 1].astype(f32)
        keep[col] = dnorm
        stat[...] = dot_exact(
            jnp.ones((8, part), f32), layer_ref[...].astype(f32) * (dnorm * gain_ref[...]), ((1,), (1,))
        )
        for n in range(len(peers)):
            stat_copy(n).start()
        small[:8] = jnp.broadcast_to(jnp.sum(dnorm * normed(), axis=0, keepdims=True), (8, part))
        cell["smalls"] = [
            remote(small, small_in.at[i], small_send.at[i], small_recv.at[i], where)
            for i, where in enumerate(others)
        ]
        for copy in cell["smalls"]:
            copy.start()

    def close():
        total = stat[...]
        for n in range(len(peers)):
            stat_copy(n).wait_recv()
            total = total + stat_in[n]
        first_row = jnp.where(lax.broadcasted_iota(jnp.int32, (8, 128), 0) == 0, 1.0, 0.0)
        row_total = dot_exact(total, first_row, ((0,), (0,)))[:, :1]
        inverse = inverse_ref[:, 127:128]
        input_grad_ref[...] = (
            two_ref[...] + inverse * (keep[col] * gain_ref[...] - normed() * (inverse * row_total / D))
        ).astype(bf16)

    def rest():
        for at in queue[:2]:
            y_copy(*at).start()
        cross()
        for n, (s, a) in enumerate(queue):
            y_copy(s, a).wait_send()
            if n + 2 < len(queue):
                y_copy(*queue[n + 2]).start()
            y_copy(s, a).wait_recv()
            own = dweight_ref[block_of(2 * ((ex + s) % experts) + half, a), :]
            total = own.astype(f32) + y_in[s, a].astype(f32)
            if s > 0:
                z_out[s, a] = total.astype(bf16)
                z_copy(s, a).start()
            else:
                held[a] = total
            if n == len(queue) // 2:
                arrive()
            if n == len(queue) - 2:
                close()
        while_waiting()
        for s in nearest_first(experts)[::-1]:
            for a in range(2):
                z_copy(s, a).wait_recv()
                held[a] = held[a] + z_in[s, a].astype(f32)
        row_out[...] = held[1 - row].astype(bf16)
        swap = remote(row_out, row_in, row_send.at[0], row_recv.at[0], {"row": 1 - row})
        swap.start()
        sums = small[...]
        for i, copy in enumerate(cell["smalls"]):
            copy.wait_recv()
            sums = sums + small_in[i]
        sums_ref[...] = sums
        swap.wait_recv()
        for at_row, values in ((row, held[row]), (1 - row, row_in[...].astype(f32))):
            proj_grad_ref[at_row] = values[:, 3 * hc :]
            for k in range(3):
                qkv_grad_ref[:, k, at_row, :] = values[:, k * hc : (k + 1) * hc]
        swap.wait_send()
        for copy in cell["smalls"] + crossing:
            copy.wait_send()
        for n in range(len(peers)):
            stat_copy(n).wait_send()
        for i in range(PIECES):
            core_copy(i).wait_send()
        for s, a in queue:
            if s > 0:
                z_copy(s, a).wait_send()

    return start, rest


def tail_kernel(columns, experts, *refs):
    (
        home_ref, slot_ref, column_ref, second_ref, mixed_ref, cotangent_ref, gain_two, router_ref,
        qkv_ref, lse_ref, attended_ref, first_ref, weight_ref, place_row, length_ref, vector_ref,
        layer_ref, gain_one, y_hbm, y_far, away_up, away_down,
    ) = refs[:22]
    layer_out_ref, input_grad_ref, qkv_grad_ref, proj_grad_ref, sums_ref, came_up, came_down = refs[22:29]
    scratch = list(refs[29:])

    def take(count):
        taken = scratch[:count]
        del scratch[:count]
        return taken

    branch_ref, two_ref, drouter_ref, dgain_ref, dfirst_ref, dweight_ref, dvector_ref, small = take(8)
    y_own, y_in, y_home = take(3)
    y_load, y_send, y_recv, y_away, y_came, half_send, half_recv = take(7)
    y_far_in = take(1)[0]
    settle_scratch = take(7 + 6)
    attention_scratch = take(5)
    finish_scratch = take(13 + 14)
    ex, half, col = lax.axis_index("ex"), lax.axis_index("half"), lax.axis_index("col")
    members = [
        {"ex": (ex + s) % experts, "half": (half + h) % 2}
        for s in range(experts)
        for h in range(2)
        if s + h > 0
    ]
    greet(grid_peers(columns) + members)

    halves = [
        remote(source, out, half_send.at[i], half_recv.at[i], {"half": 1 - half})
        for i, (source, out) in enumerate(((away_up, came_up), (away_down, came_down)))
    ]
    for copy in halves:
        copy.start()

    far, *near = farthest_first(experts)
    y_stay = pltpu.make_async_copy(y_hbm.at[col], y_own, y_load.at[0])
    y_stay.start()
    y_far_load = pltpu.make_async_copy(y_far, y_far_in, y_load.at[1])
    y_far_load.start()

    def y_cross(s, k):
        to = (col + k) % columns
        return remote(
            y_hbm.at[to, s], y_in.at[s, k - 1], y_send.at[s, k - 1], y_recv.at[s, k - 1], {"col": to}
        )

    def y_copy(s):
        return remote(
            y_own.at[s], y_home.at[s], y_away.at[s], y_came.at[s], {"ex": (ex - s + experts) % experts}
        )

    def y_sum(s, others):
        total = y_own[s].astype(f32)
        for other in others:
            total = total + other.astype(f32)
        if s > 0:
            y_own[s] = total.astype(bf16)
            y_copy(s).start()
        else:
            y_home[0] = total.astype(bf16)

    def y_homeward(s):
        for k in range(1, columns):
            y_cross(s, k).wait_recv()
        y_sum(s, [y_in[s, k - 1] for k in range(1, columns)])

    def after_spread():
        for s in near + [0]:
            for k in range(1, columns):
                y_cross(s, k).start()

    y_stay.wait()
    y_far_load.wait()
    y_sum(far, [y_far_in[k - 1] for k in range(1, columns)])
    settle_part(
        columns, experts,
        home_ref, slot_ref, column_ref, second_ref, mixed_ref, cotangent_ref, gain_two, router_ref,
        branch_ref, two_ref, drouter_ref, dgain_ref, *settle_scratch, after_spread,
    )
    ways = near + [0]

    def between(a):
        last = second_ref.shape[0] // TILE - 1
        if a == last:
            while ways:
                y_homeward(ways.pop(0))
        elif a > 0 and len(ways) > 1:
            y_homeward(ways.pop(0))

    def while_waiting():
        for s in range(1, experts):
            y_copy(s).wait_recv()
        tokens = second_ref.shape[0]
        ext = y_own.shape[1]
        size = tokens // PIECES
        lane = lax.broadcasted_iota(jnp.int32, (size, 128), 1)
        for i in range(PIECES):
            at = slice(i * size, (i + 1) * size)
            total = second_ref[at, :]
            for s in range(experts):
                place = jnp.sum(jnp.where(lane == (ex + s) % experts, slot_ref[at, :], 0.0), axis=1, keepdims=True)
                hit = place == lax.broadcasted_iota(jnp.int32, (size, ext), 1).astype(f32)
                total = total + dot_nn(jnp.where(hit, 1.0, 0.0).astype(bf16), y_home[s])
            layer_out_ref[at, :] = total.astype(bf16)

    start, rest = finish_part(
        columns, experts,
        dfirst_ref, dweight_ref, small, layer_ref, two_ref, gain_one, lse_ref,
        input_grad_ref, qkv_grad_ref, proj_grad_ref, sums_ref, *finish_scratch, members, while_waiting,
    )
    attention_backward_kernel(
        branch_ref, qkv_ref, lse_ref, attended_ref, first_ref, weight_ref, place_row, length_ref, vector_ref,
        dfirst_ref, dweight_ref, dvector_ref, *attention_scratch, between, start,
    )
    part = second_ref.shape[1]
    stat_rows = drouter_ref.shape[0]
    small[8:16] = dgain_ref[...]
    small[16 : 16 + stat_rows] = drouter_ref[...]
    pieces = 2 * TILE // part
    for i in range(dvector_ref.shape[0]):
        for n in range(pieces):
            at = 16 + stat_rows + i * pieces + n
            small[at : at + 1] = dvector_ref[i : i + 1, n * part : (n + 1) * part]
    rest()
    for copy in halves:
        copy.wait()
    for s in near + [0]:
        for k in range(1, columns):
            y_cross(s, k).wait_send()
    for s in range(1, experts):
        y_copy(s).wait_send()


def tail(
    home, slots, table, second, mixed, cotangent, gain_two, router_rows,
    qkv, lse, attended, first, weight, placing, lengths, vectors, layer_in, gain_one, y, y_far, away_up, away_down,
    stat_rows, experts, columns,
):
    tokens, part = second.shape
    quarters, others = 2 * columns, columns - 1
    hc = weight.shape[1] // 4
    ext = home.shape[1]
    rows, width = D // (4 * experts), 4 * hc
    small = (16 + stat_rows + vectors.size // part, part)
    dma = pltpu.SemaphoreType.DMA
    members = 2 * experts
    return pl.pallas_call(
        functools.partial(tail_kernel, columns, experts),
        out_shape=(
            jax.ShapeDtypeStruct((tokens, part), bf16),
            jax.ShapeDtypeStruct((tokens, part), bf16),
            jax.ShapeDtypeStruct((rows, 3, 2, hc), f32),
            jax.ShapeDtypeStruct((2, rows, hc), f32),
            jax.ShapeDtypeStruct(small, f32),
            jax.ShapeDtypeStruct(away_up.shape, bf16),
            jax.ShapeDtypeStruct(away_down.shape, bf16),
        ),
        in_specs=[vmem()] * 14 + [pl.BlockSpec(memory_space=pltpu.SMEM)] + [vmem()] * 3 + [hbm()] * 4,
        out_specs=(vmem(),) * 5 + (hbm(),) * 2,
        scratch_shapes=[
            pltpu.VMEM((quarters, tokens, part), bf16),
            pltpu.VMEM((tokens, part), f32),
            pltpu.VMEM((stat_rows, part), f32),
            pltpu.VMEM((8, part), f32),
            pltpu.VMEM((quarters, tokens, part), bf16),
            pltpu.VMEM((D, width), bf16),
            pltpu.VMEM(vectors.shape, f32),
            pltpu.VMEM(small, f32),
            pltpu.VMEM((experts, ext, part), bf16),
            pltpu.VMEM((experts, others, ext, part), bf16),
            pltpu.VMEM((experts, ext, part), bf16),
            dma((2,)), dma((experts, others)), dma((experts, others)), dma((experts,)), dma((experts,)), dma((2,)), dma((2,)),
            pltpu.VMEM((others, ext, part), bf16),
            pltpu.VMEM((tokens, part), bf16),
            pltpu.VMEM((tokens, part), f32),
            pltpu.VMEM((tokens, 128), f32),
            pltpu.VMEM((8, tokens), f32),
            pltpu.VMEM((quarters - 1, 8, tokens), f32),
            dma((PIECES, quarters - 1)), dma((PIECES, quarters - 1)),
        ]
        + spread_semaphores(columns)
        + [
            pltpu.VMEM((vectors.shape[0], TILE, TILE), f32),
            pltpu.VMEM((vectors.shape[0], TILE, TILE), f32),
            pltpu.VMEM((tokens, hc), bf16),
            pltpu.VMEM((tokens, 3 * hc), bf16),
            pltpu.VMEM((tokens, 2 * hc), f32),
            pltpu.VMEM((columns, tokens, part), bf16),
            pltpu.VMEM((columns, tokens, part), f32),
            pltpu.VMEM((others, tokens, part), bf16),
            pltpu.VMEM((others, tokens, part), bf16),
            pltpu.VMEM((8, tokens), f32),
            pltpu.VMEM((quarters - 1, 8, tokens), f32),
            pltpu.VMEM((experts, 2, rows, width), bf16),
            pltpu.VMEM((experts, 2, rows, width), bf16),
            pltpu.VMEM((experts, 2, rows, width), bf16),
            pltpu.VMEM((2, rows, width), f32),
            pltpu.VMEM((rows, width), bf16),
            pltpu.VMEM((rows, width), bf16),
            pltpu.VMEM((members - 1,) + small, f32),
            dma((PIECES,)), dma((PIECES,)), dma((PIECES, others)), dma((PIECES, others)),
            dma((quarters - 1,)), dma((quarters - 1,)),
            dma((experts, 2)), dma((experts, 2)), dma((experts, 2)), dma((experts, 2)),
            dma((1,)), dma((1,)), dma((members - 1,)), dma((members - 1,)),
        ],
        compiler_params=pltpu.CompilerParams(
            collective_id=3, has_side_effects=True, vmem_limit_bytes=47 * MIB
        ),
        cost_estimate=microseconds(90),
        name="tail",
    )(
        home, slots, table, second, mixed, cotangent, gain_two, router_rows,
        qkv, lse, attended, first, weight, placing, lengths, vectors, layer_in, gain_one, y, y_far, away_up, away_down,
    )


def adamw_step(weight, grad, first, second, rate):
    first_new = beta_first * first + (1.0 - beta_first) * grad
    second_new = beta_second * second + (1.0 - beta_second) * grad * grad
    moment = first_new / (1.0 - beta_first**STEP)
    spread = second_new / (1.0 - beta_second**STEP)
    weight_new = weight - rate * (
        moment / (jnp.sqrt(spread) + adam_epsilon) + weight_decay * weight
    )
    return (weight_new, first_new, second_new)


def local(
    layer_in, lengths, placing, routes, cotangent,
    norm_gains, gain_first, gain_second, rel_bias, bias_first, bias_second,
    router, router_first, router_second, qkv_weight, qkv_first, qkv_second,
    proj_weight, proj_first, proj_second, expert_up, up_first, up_second,
    expert_down, down_first, down_second,
):
    tokens, part = layer_in.shape
    experts, columns = lax.axis_size("ex"), lax.axis_size("col")
    quarters = 2 * columns
    cap = min(tokens, 5 * TOP * tokens // (4 * experts))
    ext = cap + EXTRA
    hc = qkv_weight.shape[5]
    head_count = hc // HD
    wide = D // 2

    qkv_low = jnp.moveaxis(qkv_weight[0, 0].astype(bf16), 1, 0).reshape(2, -1, 3 * hc)
    proj_low = jnp.swapaxes(proj_weight[:, :, 0, 0].astype(bf16), 1, 2)
    shard = jnp.concatenate([qkv_low, proj_low], axis=2)
    gains_eight = jnp.pad(norm_gains, ((0, 6), (0, 0)))
    stat_rows = (experts + 8) // 8 * 8
    x_all, gains_all, weight, slot_rows, slot_columns, own_crossed, *grad_rows = gather(
        layer_in, gains_eight, shard, placing, routes, cotangent, stat_rows, ext, experts, columns
    )
    weight = weight.reshape(D, 4 * hc)
    ff = expert_down.shape[1]
    weights = jnp.concatenate(
        [jnp.transpose(expert_up[0], (1, 2, 0)).reshape(2 * ff, wide).astype(bf16), expert_down[0].astype(bf16)]
    )

    x_all, weights = lax.optimization_barrier((x_all, weights))
    weights = lax.all_gather(weights, "half", axis=0, tiled=True).reshape(2, 3, ff, wide)
    vectors = bias_vectors(rel_bias, tokens)
    router_rows = jnp.pad(router.T, ((0, stat_rows - experts), (0, 0)))
    first, qkv, attended, lse, second, table, mixed, gates, came, crossed = attend(
        x_all, gains_all, weight, placing, lengths, vectors, layer_in, norm_gains[1:], router_rows, slot_rows,
        grad_rows, columns,
    )
    home, y, y_far, keep_up, keep_down, away_up, away_down = expert_block(
        mixed, slot_rows, gates, weights, grad_rows[0], own_crossed, came, crossed, columns
    )
    layer_out, input_grad, grad_qkv, grad_proj, sums, came_up, came_down = tail(
        home, slot_columns, table, second, mixed, cotangent, norm_gains[1:],
        router_rows, qkv, lse, attended, first, weight, placing, lengths, vectors, layer_in, norm_gains[:1], y, y_far, away_up, away_down,
        stat_rows, experts, columns,
    )
    grad_gains = jnp.stack([sums[0], sums[8]])
    grad_router = sums[16 : 16 + experts].T
    grad_bias = bias_gradient(sums[16 + stat_rows :].reshape(vectors.shape), head_count, tokens)
    grad_qkv = jnp.swapaxes(grad_qkv, 1, 2).reshape(qkv_weight.shape)
    grad_proj = jnp.swapaxes(grad_proj, 1, 2).reshape(proj_weight.shape)
    grad_up = jnp.transpose(keep_up.astype(f32) + came_up.astype(f32), (2, 0, 1))[None]
    grad_down = (keep_down.astype(f32) + came_down.astype(f32))[None]
    ups = adamw_step(expert_up, grad_up, up_first, up_second, 2.0 * D ** (-0.5))
    downs = adamw_step(expert_down, grad_down, down_first, down_second, 2.0 * (FF / 2) ** (-0.5))
    gains = adamw_step(norm_gains, grad_gains, gain_first, gain_second, 0.5)
    bias = adamw_step(rel_bias, grad_bias, bias_first, bias_second, 1.0)
    routers = adamw_step(router, grad_router, router_first, router_second, 2.0 * (2 * D) ** (-0.5))
    qkvs = adamw_step(qkv_weight, grad_qkv, qkv_first, qkv_second, 2.0 * D ** (-0.5))
    projs = adamw_step(proj_weight, grad_proj, proj_first, proj_second, 2.0 * (HEADS * HD / 8) ** (-0.5))
    out = (layer_out, input_grad) + gains + bias + routers
    for group in (qkvs, projs, ups, downs):
        out = out + group + (group[0].astype(bf16),)
    return out


def solution(mesh):
    shape = mesh.devices.shape
    fine = Mesh(
        mesh.devices.reshape((shape[0] // 2, 2) + shape[1:]), ("ex", "half", "row", "col")
    )
    dp, grid = ("ex", "half"), ("row", "col")
    tokens, own = P(dp, grid), P(dp, None)
    gain, router = P(None, grid), P(grid, None)
    qkv, proj = P("row", dp, None, None, None, "col"), P(None, "col", "row", dp, None)
    up, down = P(dp, "row", None, "col"), P(dp, "col", "row")
    in_specs = (
        (tokens, own, own, own, tokens) + (gain,) * 6 + (router,) * 3
        + (qkv,) * 3 + (proj,) * 3 + (up,) * 3 + (down,) * 3
    )
    out_specs = (
        (tokens, tokens) + (gain,) * 6 + (router,) * 3
        + (qkv,) * 4 + (proj,) * 4 + (up,) * 4 + (down,) * 4
    )
    return jax.shard_map(local, mesh=fine, in_specs=in_specs, out_specs=out_specs, check_vma=False)
```

time: 517 us -> 334 us (0.65)
  local copies, waits for them, and re-layouts: 102 us -> 7.76 us
  waiting for transfers between devices: 33.5 us -> 6.07 us
  starting transfers between devices: 21.4 us -> 0.04 us
  Pallas kernels: 293 us -> 277 us
  other arithmetic: 34.8 us -> 23.2 us
  matrix products: 9.31 us -> 1.11 us
    unnamed x133 -> x77, local copies, waits for them, and re-layouts: 70 us -> 7.36 us
    ppermute x9 -> x0, waiting for transfers between devices: 32.7 us -> none  [the longest x2 32.7 us: sum_halves(): other = lax.ppermute(pick(parts, 1 - half), 'half', [(0, 1), (1, 0)])]
    pallas_call x5 -> x2, Pallas kernels: 164 us -> 142 us  [the longest x1 92.1 us: tail(): pl.pallas_call(functools.partial(tail_kernel, columns, experts), out_shap...]
    ppermute x9 -> x0, starting transfers between devices: 15.6 us -> none  [the longest x3 9.4 us: local(): lax.ppermute(block, 'ex', [(i, (i + s) % experts) for i in range(experts)])]
    dot_general x2 -> x0, matrix products: 7.25 us -> none  [the longest x1 5.16 us: local(): jnp.einsum('est,esf->tf', one_hot, y_home, preferred_element_type=f32)]
    convert_element_type x3, other arithmetic: 21.5 us -> 14.9 us  [local(): out = out + group + (group[0].astype(bf16),)]
    all_gather x2 -> x1, waiting for transfers between devices: 0.02 us -> 6.05 us  [local(): lax.all_gather(weights, 'half', axis=0, tiled=True).reshape(2, 3, ff, wide)]
    all_to_all x1 -> x0, starting transfers between devices: 5.72 us -> none  [exchange(): return lax.all_to_all(values, 'ex', split_axis=0, concat_axis=0, tiled=True)]
  transfers between devices with their start and end apart: 13 -> 1, of which waited for: 1 -> 1; matrix products, arithmetic and copies ran while one was open for 18% -> 0% of each run, Pallas kernels for 32% -> 15%
where the time goes in v3:
time: 334 us; the launch traced here: 329 us
  Pallas kernels  277 us (83%)
  other arithmetic  23.2 us (7%)
  between operations  14.7 us (4%)
  local copies, waits for them, and re-layouts  7.76 us (2%)
  waiting for transfers between devices  6.07 us (2%)
    pallas_call x1, Pallas kernels, expert_block(): pl.pallas_call(functools.partial(expert_kernel, columns, experts), out_sh...  93.5 us
    pallas_call x1, Pallas kernels, tail(): pl.pallas_call(functools.partial(tail_kernel, columns, experts), out_shap...  92.1 us
    pallas_call x1, Pallas kernels, attend(): pl.pallas_call(functools.partial(attend_kernel, columns, experts), out_sh...  50.2 us
    pallas_call x1, Pallas kernels, gather(): pl.pallas_call(functools.partial(gather_kernel, columns, experts), out_sh...  40.8 us
    convert_element_type x3, other arithmetic, local(): out = out + group + (group[0].astype(bf16),)  14.9 us
    unnamed x77, local copies, waits for them, and re-layouts  7.36 us
  transfers between devices with their start and end apart: 1, of which 1 were waited for; matrix products, arithmetic and copies ran while one was open for 0% of the time, Pallas kernels for 15%

profile of v3, /device:TPU:0, one launch (start us, length us, event | category | flops | bytes accessed | tf_op | source)
XLA Modules:
  0.0 329.4 jit_solution(1456016602349130196)
XLA Ops:
  7.3 0.9 fusion.15
  8.2 1.1 convert_bitcast_fusion.1
  9.7 1.0 copy.71.refs_4_
  10.7 1.5 convert_bitcast_fusion
  12.4 0.5 copy-done.26
  12.9 1.5 pad_maximum_fusion
  14.4 40.8 %gather.1 = (bf16[4,1024,256]{2,1,0:T(8,128)(2,1)}, f32[4,8,256]{2,1,0:T(8,128)S(1)}, bf16[2,8,64,1024]{3,2,1,0:T(8,128)(2,1)}, f32[8,1024]{1,0:T(8,128)S(1)}, f...) custom-call(bf16[1024,256]{1,0:T(8,128)(2,1)} %refs_16_.1, ...), custom_call_target="tpu_custom_call" | custom-call | bytes 105000000 | tf_op jit(solution)/shard_map/gather/pallas_call | solution.py:746
  55.9 50.2 %attend.1 = (bf16[4,1024,256]{2,1,0:T(8,128)(2,1)}, bf16[1024,768]{1,0:T(8,128)(2,1)}, bf16[1024,256]{1,0:T(8,128)(2,1)S(1)}, f32[1024,128]{1,0:T(8,128)}, f32[1...) custom-call(bf16[4,1024,256]{2,1,0:T(8,128)(2,1)} %get-tuple-element, ...), custom_call_target="tpu_custom_call" | custom-call | bytes 157500000 | tf_op jit(solution)/shard_map/attend/pallas_call | solution.py:520
  106.2 0.6 copy-done.12
  106.8 6.0 %all-gather.2.cloned.1.call-done = bf16[4224,512]{1,0:T(8,128)(2,1)} async-done(((bf16[2112,512]{1,0:T(8,128)(2,1)}), bf16[4224,512]{1,0:T(8,128)(2,1)}) %all-gather.2.cloned.1.call-update) | async-done | bytes 4325392 | tf_op jit(solution)/shard_map/all_gather | solution.py:1672
  112.8 93.5 %expert_block.1 = (bf16[4,656,256]{2,1,0:T(8,128)(2,1)}, bf16[2,4,656,256]{3,2,1,0:T(8,128)(2,1)}, bf16[1,656,256]{2,1,0:T(8,128)(2,1)}, bf16[2,704,512]{2,1,0:T...) custom-call(bf16[1024,256]{1,0:T(8,128)(2,1)} %get-tuple-element.72.refs_0_.refs_4_, ...), custom_call_target="tpu_custom_call" | custom-call | bytes 280000000 | tf_op jit(solution)/shard_map/expert_block/pallas_call | solution.py:1130
  206.4 1.1 copy-done.4
  207.5 1.0 copy-done.8
  208.5 92.1 %tail.1 = (bf16[1024,256]{1,0:T(8,128)(2,1)S(1)}, bf16[1024,256]{1,0:T(8,128)(2,1)S(1)}, f32[64,3,2,256]{3,2,1,0:T(2,128)S(1)}, f32[2,64,256]{2,1,0:T(8,128)S(1)...) custom-call(bf16[4,656,256]{2,1,0:T(8,128)(2,1)} %get-tuple-element.78.refs_0_, ...), custom_call_target="tpu_custom_call" | custom-call | bytes 315000000 | tf_op jit(solution)/shard_map/tail/pallas_call | solution.py:1560
  300.6 0.6 multiply_subtract_fusion.3
  301.2 1.9 convert_bitcast_fusion.2
  303.2 3.8 %fusion.29 = (bf16[1,1,64,2,3,256]{5,3,4,2,1,0:T(2,128)(2,1)}, f32[1,1,64,2,3,256]{5,3,4,2,1,0:T(2,128)}, f32[1,1,64,2,3,256]{5,3,4,2,1,0:T(2,128)}, f32[1,1,64,2,3,256]{5,3,4,2,1,0:T(2,128)}) fusion(f32[1,1,64,2,3,256]{5,3,4,2,1,0:T(2,128)S(1)} %copy-done.19, f32[64,3,2,256]{3,2,1,0:T(2,128)S(1)} %get-tuple-element.93, f32[1,1,64,2,3,256]{5,3,4,2,1,0:T(2,128)} %param.44, ...), kind=kLoop, calls=%fused_computation.60 | loop fusion | flops 1474560 | bytes 2949120 | tf_op jit(solution)/shard_map/convert_element_type | solution.py:1703
  307.0 0.6 multiply_subtract_fusion.4
  307.6 0.9 add_subtract_fusion
  308.6 5.0 %fusion.23 = (bf16[1,704,512]{2,1,0:T(8,128)(2,1)}, f32[1,704,512]{2,1,0:T(8,128)}, f32[1,704,512]{2,1,0:T(8,128)}, f32[1,704,512]{2,1,0:T(8,128)}) fusion(f32[1,704,512]{2,1,0:T(8,128)S(1)} %copy-done.16, bf16[704,512]{1,0:T(8,128)(2,1)S(1)} %get-tuple-element.98, bf16[704,512]{1,0:T(8,128)(2,1)S(1)} %copy-done.22, f32[1,704,512]{2,1,0:T(8,128)S(1)} %copy-done.20, ...), kind=kLoop, calls=%fused_computation.58 | loop fusion | flops 6488064 | bytes 10813440 | tf_op jit(solution)/shard_map/convert_element_type | solution.py:1703
  313.7 1.0 copy-done.21
  314.7 6.1 %fusion.26 = (bf16[1,512,2,704]{1,3,2,0:T(8,128)(2,1)}, f32[1,512,2,704]{1,3,2,0:T(8,128)}, f32[1,512,2,704]{1,3,2,0:T(8,128)}, f32[1,512,2,704]{1,3,2,0:T(8,128)}) fusion(f32[1,512,2,704]{1,3,2,0:T(8,128)S(1)} %copy-done.15, bf16[2,704,512]{2,1,0:T(8,128)(2,1)} %get-tuple-element.96, bf16[2,704,512]{2,1,0:T(8,128)(2,1)S(1)} %copy-done.21, ...), kind=kLoop, calls=%fused_computation.59 | loop fusion | flops 12976128 | bytes 21626880 | tf_op jit(solution)/shard_map/convert_element_type | solution.py:1703
  320.7 0.8 copy.88
  321.5 0.8 copy.89
  (84 shorter events, 1.5 us)
Async XLA Ops:
  7.2 105.6 %all-gather.2.cloned.1.call-start = ((), (), s32[]{:S(2)}) async-start(), calls=%async_computation | async-start | bytes 6488064 | tf_op jit(solution)/shard_map/all_gather | solution.py:1672
  14.4 40.9 %copy-start.27 = (f32[256,4]{0,1:T(4,128)S(1)}, f32[256,4]{0,1:T(4,128)}, u32[]{:S(2)}) copy-start(f32[256,4]{0,1:T(4,128)} %param.40) | copy-start | bytes 12292
  14.4 40.9 %copy-start.25 = (f32[3,512,32]{1,2,0:T(8,128)S(1)}, f32[3,512,32]{1,2,0:T(8,128)}, u32[]{:S(2)}) copy-start(f32[3,512,32]{1,2,0:T(8,128)} %constant.28.clone) | copy-start | bytes 589828
  14.4 40.9 %copy-start.29 = (f32[32,4]{0,1:T(4,128)S(1)}, f32[32,4]{0,1:T(4,128)}, u32[]{:S(2)}) copy-start(f32[32,4]{0,1:T(4,128)} %param.37) | copy-start | bytes 1540
  14.4 40.9 %copy-start.34 = (pred[3,512]{1,0:T(4,128)(4,1)S(1)}, pred[3,512]{1,0:T(4,128)(4,1)}, u32[]{:S(2)}) copy-start(pred[3,512]{1,0:T(4,128)(4,1)} %constant.29.clone) | copy-start | bytes 4612
  55.2 50.9 %copy-start.3 = (bf16[656,256]{1,0:T(8,128)(2,1)}, bf16[656,256]{1,0:T(8,128)(2,1)S(1)}, u32[]{:S(2)}) copy-start(bf16[656,256]{1,0:T(8,128)(2,1)S(1)} %get-tuple-element.68.refs_10_.refs_4_) | copy-start | bytes 1007620
  55.2 50.9 %copy-start.10 = (f32[8,1024]{1,0:T(8,128)}, f32[8,1024]{1,0:T(8,128)S(1)}, u32[]{:S(2)}) copy-start(f32[8,1024]{1,0:T(8,128)S(1)} %get-tuple-element.67.refs_9_.refs_1_) | copy-start | bytes 98308
  112.8 93.5 %copy-start = (bf16[1024,256]{1,0:T(8,128)(2,1)S(1)}, bf16[1024,256]{1,0:T(8,128)(2,1)}, u32[]{:S(2)}) copy-start(bf16[1024,256]{1,0:T(8,128)(2,1)} %refs_16_.1) | copy-start | bytes 1572868
  112.8 93.5 %copy-start.1 = (bf16[1024,256]{1,0:T(8,128)(2,1)S(1)}, bf16[1024,256]{1,0:T(8,128)(2,1)}, u32[]{:S(2)}) copy-start(bf16[1024,256]{1,0:T(8,128)(2,1)} %refs_5_.3) | copy-start | bytes 1572868
  112.8 93.5 %copy-start.2 = (bf16[1024,256]{1,0:T(8,128)(2,1)S(1)}, bf16[1024,256]{1,0:T(8,128)(2,1)}, u32[]{:S(2)}) copy-start(bf16[1024,256]{1,0:T(8,128)(2,1)} %get-tuple-element.72.refs_0_.refs_4_) | copy-start | bytes 1572868
  112.8 93.5 %copy-start.5 = (f32[1024,128]{1,0:T(8,128)S(1)}, f32[1024,128]{1,0:T(8,128)}, u32[]{:S(2)}) copy-start(f32[1024,128]{1,0:T(8,128)} %get-tuple-element.79.refs_1_) | copy-start | bytes 1572868
  112.8 93.5 %copy-start.6 = (f32[1024,128]{1,0:T(8,128)S(1)}, f32[1024,128]{1,0:T(8,128)}, u32[]{:S(2)}) copy-start(f32[1024,128]{1,0:T(8,128)} %get-tuple-element.83.refs_9_) | copy-start | bytes 1572868
  112.8 93.6 %copy-start.7 = (f32[1024,128]{1,0:T(8,128)S(1)}, f32[1024,128]{1,0:T(8,128)}, u32[]{:S(2)}) copy-start(f32[1024,128]{1,0:T(8,128)} %get-tuple-element.80.refs_2_) | copy-start | bytes 1572868
  208.5 92.1 %copy-start.30 = (f32[256,4]{0,1:T(4,128)S(1)}, f32[256,4]{0,1:T(4,128)}, u32[]{:S(2)}) copy-start(f32[256,4]{0,1:T(4,128)} %param.41) | copy-start | bytes 12292
  208.5 92.1 %copy-start.31 = (f32[256,4]{0,1:T(4,128)S(1)}, f32[256,4]{0,1:T(4,128)}, u32[]{:S(2)}) copy-start(f32[256,4]{0,1:T(4,128)} %param.42) | copy-start | bytes 12292
  208.5 92.8 %copy-start.23 = (f32[2,256,1,1,64]{1,4,3,2,0:T(8,128)S(1)}, f32[2,256,1,1,64]{1,4,3,2,0:T(8,128)}, u32[]{:S(2)}) copy-start(f32[2,256,1,1,64]{1,4,3,2,0:T(8,128)} %param.46) | copy-start | bytes 393220
  208.5 94.7 %copy-start.19 = (f32[1,1,64,2,3,256]{5,3,4,2,1,0:T(2,128)S(1)}, f32[1,1,64,2,3,256]{5,3,4,2,1,0:T(2,128)}, u32[]{:S(2)}) copy-start(f32[1,1,64,2,3,256]{5,3,4,2,1,0:T(2,128)} %param.43) | copy-start | bytes 1179652
  301.2 7.3 %copy-start.22 = (bf16[704,512]{1,0:T(8,128)(2,1)S(1)}, bf16[704,512]{1,0:T(8,128)(2,1)}, u32[]{:S(2)}) copy-start(bf16[704,512]{1,0:T(8,128)(2,1)} %get-tuple-element.97) | copy-start | bytes 2162692
  303.2 5.4 %copy-start.16 = (f32[1,704,512]{2,1,0:T(8,128)S(1)}, f32[1,704,512]{2,1,0:T(8,128)}, u32[]{:S(2)}) copy-start(f32[1,704,512]{2,1,0:T(8,128)} %param.52) | copy-start | bytes 4325380
  303.2 5.4 %copy-start.20 = (f32[1,704,512]{2,1,0:T(8,128)S(1)}, f32[1,704,512]{2,1,0:T(8,128)}, u32[]{:S(2)}) copy-start(f32[1,704,512]{2,1,0:T(8,128)} %param.53) | copy-start | bytes 4325380
  308.5 5.0 %copy-start.15 = (f32[1,512,2,704]{1,3,2,0:T(8,128)S(1)}, f32[1,512,2,704]{1,3,2,0:T(8,128)}, u32[]{:S(2)}) copy-start(f32[1,512,2,704]{1,3,2,0:T(8,128)} %param.49) | copy-start | bytes 8650756
  308.5 5.0 %copy-start.17 = (f32[1,512,2,704]{1,3,2,0:T(8,128)S(1)}, f32[1,512,2,704]{1,3,2,0:T(8,128)}, u32[]{:S(2)}) copy-start(f32[1,512,2,704]{1,3,2,0:T(8,128)} %param.50) | copy-start | bytes 8650756
  308.6 5.1 %copy-start.18 = (f32[1,512,2,704]{1,3,2,0:T(8,128)S(1)}, f32[1,512,2,704]{1,3,2,0:T(8,128)}, u32[]{:S(2)}) copy-start(f32[1,512,2,704]{1,3,2,0:T(8,128)} %param.51) | copy-start | bytes 8650756
  308.6 6.1 %copy-start.21 = (bf16[2,704,512]{2,1,0:T(8,128)(2,1)S(1)}, bf16[2,704,512]{2,1,0:T(8,128)(2,1)}, u32[]{:S(2)}) copy-start(bf16[2,704,512]{2,1,0:T(8,128)(2,1)} %get-tuple-element.95) | copy-start | bytes 4325380
  (14 other events, 32.8 us)
Sparse Core Ops, SparseCore 0:
  55.4 57.4 all-gather.1

commit v4 on v3

--- a/solution.py
+++ b/solution.py
@@ -105,8 +105,8 @@
 
 
 def attention_forward_kernel(
-    x_ref, gain_ref, weight_ref, place_row, length_ref, vector_ref,
-    first_ref, qkv_ref, attended_ref, lse_ref, bias, placed_out, between,
+    x_ref, gain_ref, weight_ref, length_ref, vector_ref,
+    first_ref, qkv_ref, attended_ref, lse_ref, bias, between,
 ):
     quarters, tokens, part = x_ref.shape
     width = quarters * part
@@ -124,12 +124,11 @@
         first = (x_ref[q].astype(f32) * inverse * gain_ref[q, :1]).astype(bf16)
         first_ref[q] = first
         total = total + dot_nn(first, weight_ref[q * part : (q + 1) * part, : 3 * hc])
-    to_given = given_table(place_row, tokens)
     all_starts = sequence_starts(length_ref, tokens)
     scale = jnp.where(
         lax.broadcasted_iota(jnp.int32, (1, 3 * hc), 1) < hc, HD ** (-0.5), 1.0
     )
-    qkv_ref[...] = dot_tn(to_given, (total * scale).astype(bf16)).astype(bf16)
+    qkv_ref[...] = (total * scale).astype(bf16)
     between(-1)
     for a in range(tokens // TILE):
         rows = slice(a * TILE, (a + 1) * TILE)
@@ -165,12 +164,10 @@
         out, lse = lax.fori_loop(
             0, head_count, one_head, (jnp.zeros((TILE, hc), f32), jnp.zeros((TILE, 128), f32))
         )
-        placed_out[rows, :] = out.astype(bf16)
-        lse_ref[rows, :] = lse
+        attended_ref[rows, :] = out.astype(bf16)
+        lane = lax.broadcasted_iota(jnp.int32, (TILE, 128), 1)
+        lse_ref[rows, :] = jnp.where(lane == 127, inverse[rows], lse)
         between(a)
-    lane = lax.broadcasted_iota(jnp.int32, (tokens, 128), 1)
-    lse_ref[...] = jnp.where(lane == 127, inverse, lse_ref[...])
-    attended_ref[...] = dot_nn(to_given, placed_out[...]).astype(bf16)
 
 
 def microseconds(time):
@@ -186,10 +183,9 @@
 
 
 def attention_backward_kernel(
-    branch_ref, qkv_ref, lse_ref, attended_ref, first_ref, weight_ref,
-    place_row, length_ref, vector_ref,
+    branch_ref, qkv_ref, lse_ref, attended_ref, first_ref, weight_ref, length_ref, vector_ref,
     dfirst_ref, dweight_ref, dvector_ref,
-    bias, dbias, grad_ref, dqkv, dkv, between, after_dfirst,
+    bias, dbias, grad_ref, dqkv, dkv, before, after,
 ):
     quarters, tokens, part = branch_ref.shape
     hc = weight_ref.shape[1] // 4
@@ -198,21 +194,19 @@
     fill_bias(vector_ref, bias)
     dbias[...] = jnp.zeros_like(dbias)
     dkv[...] = jnp.zeros_like(dkv)
-    total = jnp.zeros((tokens, hc), f32)
-    for q in range(quarters):
-        dims = slice(q * part, (q + 1) * part)
-        total = total + dot_nn(branch_ref[q], weight_ref[dims, 3 * hc :])
-        dweight_ref[dims, 3 * hc :] = dot_tn(branch_ref[q], attended_ref[...]).astype(bf16)
-    to_given = given_table(place_row, tokens)
     all_starts = sequence_starts(length_ref, tokens)
-    grad_ref[...] = dot_tn(to_given, total.astype(bf16)).astype(bf16)
-    for a in range(tokens // TILE):
+    for a in reversed(range(tokens // TILE)):
         rows = slice(a * TILE, (a + 1) * TILE)
         blocks = range(max(0, a - reach + 1), a + 1)
         starts = all_starts[rows, :]
         visible = [
             b * TILE + lax.broadcasted_iota(jnp.int32, (TILE, TILE), 1) >= starts for b in blocks
         ]
+        before(a)
+        total = jnp.zeros((TILE, hc), f32)
+        for q in range(quarters):
+            total = total + dot_nn(branch_ref[q, rows], weight_ref[q * part : (q + 1) * part, 3 * hc :])
+        grad_ref[rows, :] = total.astype(bf16)
 
         def one_head(head, dquery):
             mine = head_lanes((TILE, hc), head)
@@ -243,15 +237,19 @@
 
         dquery = lax.fori_loop(0, head_count, one_head, jnp.zeros((TILE, hc), f32))
         dqkv[rows, :hc] = (dquery * HD ** (-0.5)).astype(bf16)
-        between(a)
-    dqkv[:, hc:] = dkv[...].astype(bf16)
-    given = dot_nn(to_given, dqkv[...]).astype(bf16)
-    for q in range(quarters):
-        dfirst_ref[q] = dot_nt(given, weight_ref[q * part : (q + 1) * part, : 3 * hc]).astype(bf16)
-    after_dfirst()
+        dqkv[rows, hc:] = dkv[rows, :].astype(bf16)
+        for q in range(quarters):
+            dfirst_ref[q, rows] = dot_nt(
+                dqkv[rows, :], weight_ref[q * part : (q + 1) * part, : 3 * hc]
+            ).astype(bf16)
+        after(a)
     for q in range(quarters):
         dims = slice(q * part, (q + 1) * part)
-        dweight_ref[dims, : 3 * hc] = dot_tn(first_ref[q], given).astype(bf16)
+        dweight_ref[dims, : 3 * hc] = dot_tn(first_ref[q], dqkv[...]).astype(bf16)
+        dweight_ref[dims, 3 * hc :] = dot_tn(branch_ref[q], attended_ref[...]).astype(bf16)
+
+
+def bias_sums(dbias, dvector_ref):
     for i in range(dbias.shape[0]):
         wide = jnp.concatenate([dbias[i], jnp.zeros((TILE, TILE), f32)], axis=1)
         level = wide[:8]
@@ -347,7 +345,7 @@
     attended_ref, weight_ref, layer_ref, gain_ref, router_ref, slot_ref,
     second_ref, mixed_ref, gate_ref, column_ref,
     core_out, core_in, keep, col_out, col_in, stat, stat_in,
-    core_send, core_recv, col_send, col_recv, stat_send, stat_recv, after_crossing,
+    core_send, core_recv, col_send, col_recv, stat_send, stat_recv,
 ):
     row, col = lax.axis_index("row"), lax.axis_index("col")
     tokens, part = layer_ref.shape
@@ -356,56 +354,65 @@
     heads = slice(3 * weight_ref.shape[1] // 4, weight_ref.shape[1])
     own_rows = pl.ds(pl.multiple_of(row * wide, wide), wide)
     other_rows = pl.ds(pl.multiple_of((1 - row) * wide, wide), wide)
-    cores = []
-    for i in range(PIECES):
+    own_columns = pl.ds(pl.multiple_of(col * part, part), part)
+
+    def core_copy(i):
+        return remote(core_out.at[i], core_in.at[i], core_send.at[i], core_recv.at[i], {"row": 1 - row})
+
+    def col_copy(i, k):
+        return remote(
+            col_out.at[i, k - 1], col_in.at[i, k - 1], col_send.at[i, k - 1], col_recv.at[i, k - 1],
+            {"col": (col + k) % columns},
+        )
+
+    def multiply(i):
         at = slice(i * size, (i + 1) * size)
         core_out[i] = dot_nt(attended_ref[at, :], weight_ref[other_rows, heads]).astype(bf16)
-        copy = remote(core_out.at[i], core_in.at[i], core_send.at[i], core_recv.at[i], {"row": 1 - row})
-        copy.start()
-        cores.append(copy)
+        core_copy(i).start()
         keep[i] = dot_nt(attended_ref[at, :], weight_ref[own_rows, heads])
-    own_columns = pl.ds(pl.multiple_of(col * part, part), part)
-    crossing = []
-    for i in range(PIECES):
-        cores[i].wait_recv()
+
+    def cross(i):
+        core_copy(i).wait_recv()
         keep[i] = keep[i] + core_in[i].astype(f32)
         for k in range(1, columns):
             to = (col + k) % columns
             col_out[i, k - 1] = keep[i, :, pl.ds(pl.multiple_of(to * part, part), part)].astype(bf16)
-            copy = remote(
-                col_out.at[i, k - 1], col_in.at[i, k - 1], col_send.at[i, k - 1], col_recv.at[i, k - 1], {"col": to}
+            col_copy(i, k).start()
+
+    def rest():
+        ones = jnp.where(lax.broadcasted_iota(jnp.int32, router_ref.shape, 0) == experts, 1.0, 0.0)
+        scaled_router = router_ref[...] * gain_ref[1:2]
+        for i in range(PIECES):
+            at = slice(i * size, (i + 1) * size)
+            total = layer_ref[at, :].astype(f32) + keep[i, :, own_columns]
+            for k in range(1, columns):
+                col_copy(i, k).wait_recv()
+                total = total + col_in[i, k - 1].astype(f32)
+            second_ref[at, :] = total
+            stat[:, at] = dot_exact(scaled_router, total, ((1,), (1,))) + dot_exact(
+                ones, total * total, ((1,), (1,))
             )
-            copy.start()
-            crossing.append(copy)
-    after_crossing()
-    ones = jnp.where(lax.broadcasted_iota(jnp.int32, router_ref.shape, 0) == experts, 1.0, 0.0)
-    for i in range(PIECES):
-        at = slice(i * size, (i + 1) * size)
-        total = layer_ref[at, :].astype(f32) + keep[i, :, own_columns]
-        for k in range(1, columns):
-            crossing[i * (columns - 1) + k - 1].wait_recv()
-            total = total + col_in[i, k - 1].astype(f32)
-        second_ref[at, :] = total
-        stat[:, at] = dot_exact(router_ref[...] * gain_ref[...], total, ((1,), (1,))) + dot_exact(
-            ones, total * total, ((1,), (1,))
-        )
-    total = sum_of_peers(stat, stat_in, stat_send, stat_recv, columns)
-    inverse = lax.rsqrt(total[experts : experts + 1] / D + norm_epsilon)
-    routed = slot_ref[...] >= 0
-    logits = jnp.where(routed, total * inverse, hidden_score)
-    shares = jnp.where(routed, jnp.exp(logits - jnp.max(logits, axis=0, keepdims=True)), 0.0)
-    gates = shares / jnp.sum(shares, axis=0, keepdims=True)
-    gate_ref[...] = gates
-    number = lax.broadcasted_iota(jnp.int32, gates.shape, 0)
-    lanes = (gates.shape[0], 128)
-    eye = jnp.where(
-        lax.broadcasted_iota(jnp.int32, lanes, 0) == lax.broadcasted_iota(jnp.int32, lanes, 1), 1.0, 0.0
-    )
-    table = dot_exact(jnp.where(number == experts, inverse, gates), eye, ((0,), (0,)))
-    column_ref[...] = table
-    mixed_ref[...] = (second_ref[...] * table[:, experts : experts + 1] * gain_ref[...]).astype(bf16)
-    for copy in cores + crossing:
-        copy.wait_send()
+        total = sum_of_peers(stat, stat_in, stat_send, stat_recv, columns)
+        inverse = lax.rsqrt(total[experts : experts + 1] / D + norm_epsilon)
+        routed = slot_ref[...] >= 0
+        logits = jnp.where(routed, total * inverse, hidden_score)
+        shares = jnp.where(routed, jnp.exp(logits - jnp.max(logits, axis=0, keepdims=True)), 0.0)
+        gates = shares / jnp.sum(shares, axis=0, keepdims=True)
+        gate_ref[...] = gates
+        number = lax.broadcasted_iota(jnp.int32, gates.shape, 0)
+        lanes = (gates.shape[0], 128)
+        eye = jnp.where(
+            lax.broadcasted_iota(jnp.int32, lanes, 0) == lax.broadcasted_iota(jnp.int32, lanes, 1), 1.0, 0.0
+        )
+        table = dot_exact(jnp.where(number == experts, inverse, gates), eye, ((0,), (0,)))
+        column_ref[...] = table
+        mixed_ref[...] = (second_ref[...] * table[:, experts : experts + 1] * gain_ref[1:2]).astype(bf16)
+        for i in range(PIECES):
+            core_copy(i).wait_send()
+            for k in range(1, columns):
+                col_copy(i, k).wait_send()
+
+    return multiply, cross, rest
 
 
 def nearest_first(experts):
@@ -418,14 +425,14 @@
 
 
 def attend_kernel(columns, experts, *refs):
-    x_hbm, gains_ref, weight_hbm, place_row, length_ref, vector_ref, layer_ref, gain_ref, router_ref, slot_ref = refs[:10]
+    x_hbm, gains_ref, weight_hbm, length_ref, vector_ref, layer_ref, gain_ref, router_ref, slot_ref, shares = refs[:10]
     grad_rows = refs[10 : 10 + experts]
     (
-        first_hbm, qkv_hbm, attended_hbm, lse_hbm, second_hbm, column_hbm, mixed_ref, gate_ref, came, crossed,
+        first_hbm, qkv_hbm, attended_hbm, lse_hbm, second_hbm, column_hbm, mixed_ref, gate_ref, came, crossed, share_out,
         first_ref, qkv_ref, attended_ref, lse_ref, second_ref, column_ref,
-        bias, placed_out, core_out, core_in, keep, col_out, col_in, stat, stat_in,
+        bias, core_out, core_in, keep, col_out, col_in, stat, stat_in,
         core_send, core_recv, col_send, col_recv, stat_send, stat_recv,
-        z_send, z_recv, x_send, x_recv, store, x_ref, weight_ref, load,
+        z_send, z_recv, x_send, x_recv, store, x_ref, weight_ref, load, share_send, share_recv,
     ) = refs[10 + experts :]
     loads = [
         pltpu.make_async_copy(x_hbm, x_ref, load.at[0]),
@@ -434,7 +441,15 @@
     for copy in loads:
         copy.start()
     ex, col = lax.axis_index("ex"), lax.axis_index("col")
-    greet(grid_peers(columns) + [{"ex": (ex + s) % experts} for s in range(1, experts)])
+    greet(
+        grid_peers(columns)
+        + [{"ex": (ex + s) % experts} for s in range(1, experts)]
+        + [{"half": 1 - lax.axis_index("half")}]
+    )
+    share = remote(
+        shares, share_out, share_send.at[0], share_recv.at[0], {"half": 1 - lax.axis_index("half")}
+    )
+    share.start()
 
     def z_copy(s):
         return remote(grad_rows[s], came.at[s], z_send.at[s], z_recv.at[s], {"ex": (ex + s) % experts})
@@ -444,31 +459,39 @@
             came.at[s], crossed.at[s, k - 1], x_send.at[s, k - 1], x_recv.at[s, k - 1], {"col": (col + k) % columns}
         )
 
-    order = farthest_first(experts)
-    z_copy(order[0]).start()
-    done = [0]
+    far, *near = farthest_first(experts)
+    for s in near + [far]:
+        z_copy(s).start()
     for copy in loads:
         copy.wait()
 
-    def advance():
-        n = done[0]
-        z_copy(order[n]).wait_send()
-        if n + 1 < len(order):
-            z_copy(order[n + 1]).start()
-        z_copy(order[n]).wait_recv()
-        if n + 1 < len(order):
-            for k in range(1, columns):
-                x_copy(order[n], k).start()
-        done[0] = n + 1
+    def go_on(s):
+        z_copy(s).wait_recv()
+        for k in range(1, columns):
+            x_copy(s, k).start()
+
+    multiply, cross, rest = project_part(
+        columns, experts,
+        attended_ref, weight_ref, layer_ref, gain_ref, router_ref, slot_ref,
+        second_ref, mixed_ref, gate_ref, column_ref,
+        core_out, core_in, keep, col_out, col_in, stat, stat_in,
+        core_send, core_recv, col_send, col_recv, stat_send, stat_recv,
+    )
 
     def between(a):
+        if a >= 0:
+            multiply(a)
+        if a > 0:
+            cross(a - 1)
         if a == 2:
-            advance()
+            for s in near[:-1]:
+                go_on(s)
 
     attention_forward_kernel(
-        x_ref, gains_ref, weight_ref, place_row, length_ref, vector_ref,
-        first_ref, qkv_ref, attended_ref, lse_ref, bias, placed_out, between,
-    )
+        x_ref, gains_ref, weight_ref, length_ref, vector_ref,
+        first_ref, qkv_ref, attended_ref, lse_ref, bias, between,
+    )
+    cross(PIECES - 1)
 
     def stored(pairs, first):
         copies = [pltpu.make_async_copy(a, b, store.at[first + i]) for i, (a, b) in enumerate(pairs)]
@@ -480,27 +503,21 @@
         [(first_ref, first_hbm), (qkv_ref, qkv_hbm), (attended_ref, attended_hbm), (lse_ref, lse_hbm)], 0
     )
 
-    def after_crossing():
-        while done[0] + 1 < len(order):
-            advance()
-
-    project_part(
-        columns, experts,
-        attended_ref, weight_ref, layer_ref, gain_ref, router_ref, slot_ref,
-        second_ref, mixed_ref, gate_ref, column_ref,
-        core_out, core_in, keep, col_out, col_in, stat, stat_in,
-        core_send, core_recv, col_send, col_recv, stat_send, stat_recv, after_crossing,
-    )
+    go_on(far)
+    rest()
     stores = stores + stored([(second_ref, second_hbm), (column_ref, column_hbm)], 4)
-    advance()
+    z_copy(near[-1]).wait_recv()
     for copy in stores:
         copy.wait()
-    for s in order[:-1]:
+    share.wait()
+    for s in [far] + near[:-1]:
         for k in range(1, columns):
             x_copy(s, k).wait()
-
-
-def attend(x, gains, weight, placing, lengths, vectors, layer_in, gain, router_rows, slots, grad_rows, columns):
+    for s in near + [far]:
+        z_copy(s).wait_send()
+
+
+def attend(x, gains, weight, lengths, vectors, layer_in, gain, router_rows, slots, shares, grad_rows, columns):
     quarters, tokens, part = x.shape
     experts = len(grad_rows)
     ext = grad_rows[0].shape[0]
@@ -525,15 +542,15 @@
             jax.ShapeDtypeStruct((rows, tokens), f32),
             jax.ShapeDtypeStruct((experts, ext, part), bf16),
             jax.ShapeDtypeStruct((experts, others, ext, part), bf16),
+            jax.ShapeDtypeStruct(shares.shape, bf16),
         ),
-        in_specs=[hbm(), vmem(), hbm(), vmem(), pl.BlockSpec(memory_space=pltpu.SMEM)]
+        in_specs=[hbm(), vmem(), hbm(), pl.BlockSpec(memory_space=pltpu.SMEM)]
         + [vmem()] * 5
-        + [hbm()] * experts,
-        out_specs=(hbm(),) * 6 + (vmem(),) * 2 + (hbm(),) * 2,
+        + [hbm()] * (1 + experts),
+        out_specs=(hbm(),) * 6 + (vmem(),) * 2 + (hbm(),) * 3,
         scratch_shapes=[pltpu.VMEM(each.shape, each.dtype) for each in kept]
         + [
             pltpu.VMEM((vectors.shape[0], TILE, TILE), f32),
-            pltpu.VMEM((tokens, hc), bf16),
             pltpu.VMEM((PIECES, size, columns * part), bf16),
             pltpu.VMEM((PIECES, size, columns * part), bf16),
             pltpu.VMEM((PIECES, size, columns * part), f32),
@@ -544,25 +561,25 @@
             dma((PIECES,)), dma((PIECES,)), dma((PIECES, others)), dma((PIECES, others)),
             dma((quarters - 1,)), dma((quarters - 1,)),
             dma((experts,)), dma((experts,)), dma((experts, others)), dma((experts, others)), dma((6,)),
-            pltpu.VMEM(x.shape, bf16), pltpu.VMEM(weight.shape, bf16), dma((2,)),
+            pltpu.VMEM(x.shape, bf16), pltpu.VMEM(weight.shape, bf16), dma((2,)), dma((1,)), dma((1,)),
         ],
         compiler_params=pltpu.CompilerParams(
             collective_id=1, has_side_effects=True, vmem_limit_bytes=52 * MIB
         ),
         cost_estimate=microseconds(45),
         name="attend",
-    )(x, gains, weight, placing, lengths, vectors, layer_in, gain, router_rows, slots, *grad_rows)
+    )(x, gains, weight, lengths, vectors, layer_in, gain, router_rows, slots, shares, *grad_rows)
 
 
 def gather_kernel(columns, experts, *refs):
     layer_ref, gain_ref, shard_ref, place_row, route_ref, cotangent_ref = refs[:6]
-    x_ref, gains_ref, weight_ref, slot_row_ref, slot_column_ref, crossed_ref = refs[6:12]
-    slot_grads = refs[12 : 12 + experts]
+    x_ref, gains_ref, weight_ref, slot_row_ref, slot_column_ref, crossed_ref, placed_ref, placed_cot = refs[6:14]
+    slot_grads = refs[14 : 14 + experts]
     (
         x_send, x_recv, own_send, own_recv, pass_send, pass_recv, gain_send, gain_recv,
         swap_send, swap_recv, z_send, z_recv, y_send, y_recv, place, cross_send, cross_recv,
         stay, slots, slot_store,
-    ) = refs[12 + experts :]
+    ) = refs[14 + experts :]
     ex, half = lax.axis_index("ex"), lax.axis_index("half")
     row, col = lax.axis_index("row"), lax.axis_index("col")
     mine = row * columns + col
@@ -573,7 +590,7 @@
         + [{"half": 1 - half}]
     )
     spread = Spread(
-        x_ref, layer_ref, columns, x_send, x_recv, own_send, own_recv, pass_send, pass_recv, stay
+        x_ref, placed_ref, columns, x_send, x_recv, own_send, own_recv, pass_send, pass_recv, stay
     )
     member = 2 * ex + half
     swap = remote(
@@ -585,7 +602,6 @@
     )
     place_shard = pltpu.make_async_copy(shard_ref.at[row], weight_ref.at[row, member], place.at[0])
     place_shard.start()
-    spread.start()
 
     def z_copy(s, a):
         block = weight_ref.at[a, member]
@@ -610,6 +626,9 @@
     arrived.wait_recv()
     z_copy(*queue[1]).start()
     y_copy(0, 1 - row).start()
+    to_given = given_table(place_row, tokens)
+    placed_ref[...] = dot_tn(to_given, layer_ref[...]).astype(bf16)
+    spread.start()
     gains_ref[mine] = gain_ref[...]
     gain_copies = [
         remote(gain_ref, gains_ref.at[mine], gain_send.at[i], gain_recv.at[i], where)
@@ -618,26 +637,29 @@
     for copy in gain_copies:
         copy.start()
 
-    lane = lax.broadcasted_iota(jnp.int32, (tokens, 128), 1)
-    placed_hits = (route_ref[:, :1] == lane) | (route_ref[:, 1:2] == lane)
-    to_given = given_table(place_row, tokens)
-    hits = dot_nn(to_given, jnp.where(placed_hits, 1.0, 0.0).astype(bf16))
+    number = lax.broadcasted_iota(jnp.int32, (128, tokens), 0)
+    hits = jnp.where((route_ref[:1] == number) | (route_ref[1:] == number), 1.0, 0.0)
     low_hits = hits.astype(bf16)
     first_at = lax.broadcasted_iota(jnp.int32, (tokens, tokens), 0)
     second_at = lax.broadcasted_iota(jnp.int32, (tokens, tokens), 1)
-    up_to = jnp.where(second_at <= first_at, 1.0, 0.0).astype(bf16)
-    slot_column_ref[...] = jnp.where(hits > 0.5, dot_nn(up_to, low_hits) - 1.0, -1.0)
-    from_on = jnp.where(first_at <= second_at, 1.0, 0.0).astype(bf16)
-    same = jnp.where(first_at == second_at, 1.0, 0.0).astype(bf16)
-    rows = slot_row_ref.shape[0]
-    row_counts = dot_tn(low_hits, from_on)[:rows]
-    slot_row_ref[...] = jnp.where(dot_tn(low_hits, same)[:rows] > 0.5, row_counts - 1.0, -1.0)
+
+    def slot_columns():
+        placed_cot[...] = dot_tn(to_given, cotangent_ref[...]).astype(bf16)
+        up_to = jnp.where(second_at <= first_at, 1.0, 0.0).astype(bf16)
+        same = jnp.where(first_at == second_at, 1.0, 0.0).astype(bf16)
+        slot_column_ref[...] = jnp.where(dot_nt(same, low_hits) > 0.5, dot_nt(up_to, low_hits) - 1.0, -1.0)
+
+    def slot_rows():
+        from_on = jnp.where(first_at <= second_at, 1.0, 0.0).astype(bf16)
+        rows = slot_row_ref.shape[0]
+        row_counts = dot_nn(low_hits, from_on)[:rows]
+        slot_row_ref[...] = jnp.where(hits[:rows] > 0.5, row_counts - 1.0, -1.0)
 
     def cotangent_slots(s):
         e = (ex + s) % experts
         ext = slot_grads[s].shape[0]
         hit = slot_row_ref[pl.ds(e, 1), :] == lax.broadcasted_iota(jnp.int32, (ext, tokens), 0).astype(f32)
-        slots[s] = dot_nn(jnp.where(hit, 1.0, 0.0).astype(bf16), cotangent_ref[...]).astype(bf16)
+        slots[s] = dot_nn(jnp.where(hit, 1.0, 0.0).astype(bf16), placed_cot[...]).astype(bf16)
         pltpu.make_async_copy(slots.at[s], slot_grads[s], slot_store.at[s]).start()
 
     crossing = [
@@ -647,21 +669,25 @@
         )
         for k in range(1, columns)
     ]
-    cotangent_slots(0)
-    for copy in crossing:
-        copy.start()
-    made = 1
+    def first_slots():
+        cotangent_slots(0)
+        for copy in crossing:
+            copy.start()
+
+    jobs = [slot_columns, slot_rows, first_slots] + [functools.partial(cotangent_slots, s) for s in range(1, experts)]
+    jobs.pop(0)()
     for i, (s, a) in enumerate(queue):
         z_copy(s, a).wait_send()
         if i + 2 < len(queue):
             z_copy(*queue[i + 2]).start()
         z_arrival(s, a).wait_recv()
         y_copy(s, a).start()
-        if i == 0:
-            spread.hand_on()
-        while made < experts * (i + 1) // len(queue):
-            cotangent_slots(made)
-            made += 1
+        if i < PIECES:
+            spread.hand_on_piece(i)
+        if jobs:
+            jobs.pop(0)()
+    while jobs:
+        jobs.pop(0)()
     spread.finish()
     for copy in gain_copies + crossing:
         copy.wait()
@@ -716,10 +742,20 @@
         else:
             pltpu.make_async_copy(self.source.at[at], self.out.at[self.mine, at], self.stay.at[i]).start()
 
-    def hand_on(self):
-        for across, passed in zip(self.across, self.passed):
-            across.wait_recv()
-            passed.start()
+    def hand_on_piece(self, i):
+        others = len(self.across) // PIECES
+        for n in range(i * others, (i + 1) * others):
+            self.across[n].wait_recv()
+            self.passed[n].start()
+
+    def wait_piece(self, i):
+        others = len(self.across) // PIECES
+        for copy in self.passed[i * others : (i + 1) * others] + [self.own[i]]:
+            copy.wait_recv()
+
+    def wait_sends(self):
+        for copy in self.across + self.own + self.passed:
+            copy.wait_send()
 
     def finish(self):
         if self.stay is not None:
@@ -727,10 +763,9 @@
             for i in range(PIECES):
                 at = pl.ds(i * size, size)
                 pltpu.make_async_copy(self.source.at[at], self.out.at[self.mine, at], self.stay.at[i]).wait()
-        for copy in self.own + self.passed:
-            copy.wait_recv()
-        for copy in self.across + self.own + self.passed:
-            copy.wait_send()
+        for i in range(PIECES):
+            self.wait_piece(i)
+        self.wait_sends()
 
 
 def spread_semaphores(columns):
@@ -752,10 +787,12 @@
             jax.ShapeDtypeStruct((stat_rows, tokens), f32),
             jax.ShapeDtypeStruct((tokens, 128), f32),
             jax.ShapeDtypeStruct((columns - 1, ext, part), bf16),
+            jax.ShapeDtypeStruct((tokens, part), bf16),
+            jax.ShapeDtypeStruct((tokens, part), bf16),
         )
         + (jax.ShapeDtypeStruct((ext, part), bf16),) * experts,
         in_specs=[vmem()] * 6,
-        out_specs=(hbm(), vmem(), hbm(), vmem(), vmem()) + (hbm(),) * (1 + experts),
+        out_specs=(hbm(), vmem(), hbm(), vmem(), vmem(), hbm(), vmem(), vmem()) + (hbm(),) * experts,
         scratch_shapes=spread_semaphores(columns)
         + [
             dma((quarters - 1,)), dma((quarters - 1,)), dma((1,)), dma((1,)),
@@ -775,14 +812,15 @@
     columns, experts,
     *refs,
 ):
-    mixed_ref, slot_ref, gate_ref, weight_hbm, own_grads, own_crossed, came, crossed = refs[:8]
+    mixed_ref, slot_ref, gate_ref, shares, share_came, own_grads, own_crossed, came, crossed = refs[:9]
     (
         home_ref, y_hbm, y_far, keep_up, keep_down, away_up, away_down,
         x, xs, grads, weight, da, db, scaled, core_out, core_in, keep, col_out, col_in,
         load, grad_load, grad_send, grad_recv, z_send, z_recv, own_send, own_recv, col_send, col_recv, pass_send, pass_recv,
         core_send, core_recv, back_send, back_recv, home_send, home_recv, y_send, y_recv, y_sem, store, far_send, far_recv,
         free, last_send, last_recv, on_send, on_recv, y_far_send, y_far_recv,
-    ) = refs[8:]
+        hand_send, hand_recv,
+    ) = refs[9:]
     ex, half = lax.axis_index("ex"), lax.axis_index("half")
     row, col = lax.axis_index("row"), lax.axis_index("col")
     tokens, part = mixed_ref.shape
@@ -800,10 +838,32 @@
 
     own_dims = pl.ds(pl.multiple_of(row * wide, wide), wide)
     other_dims = pl.ds(pl.multiple_of((1 - row) * wide, wide), wide)
-    loads = [pltpu.make_async_copy(weight_hbm.at[row], weight.at[:, :, own_dims], load.at[0])]
-    handed = [
-        remote(weight_hbm.at[1 - row], weight.at[:, :, own_dims], load.at[1], load.at[2], {"row": 1 - row})
-    ]
+    at_home = row == half
+    loads, handed = [], []
+
+    def to_row(source, place, i, stays):
+        here = pltpu.make_async_copy(source, place, load.at[i])
+        there = remote(source, place, hand_send.at[i], hand_recv.at[i], {"row": 1 - row})
+
+        def start():
+            pl.when(stays)(here.start)
+            pl.when(jnp.logical_not(stays))(there.start)
+
+        def wait():
+            pl.when(stays)(here.wait)
+            pl.when(jnp.logical_not(stays))(there.wait_send)
+
+        def arrive():
+            pl.when(stays)(there.wait_recv)
+
+        return start, wait, arrive
+
+    own_start, own_wait, own_arrive = to_row(shares, weight.at[:, :, own_dims], 0, at_home)
+    came_start, came_wait, came_arrive = to_row(
+        share_came, weight.at[:, :, own_dims], 1, jnp.logical_not(at_home)
+    )
+    own_start()
+    came_start()
     final_chunk = farthest_first(experts)[-1]
     for s in range(experts):
         for k in range(columns):
@@ -900,6 +960,8 @@
     z_copy(nth(2)).start()
     z_copy(nth(1)).wait_recv()
     spread(nth(1))
+    for wait in (own_wait, own_arrive, came_wait, came_arrive):
+        wait()
 
     def core_copy(s):
         return remote(core_out.at[s], core_in.at[s], core_send.at[s], core_recv.at[s], {"row": 1 - row})
@@ -1086,16 +1148,16 @@
             for k in range(1, columns):
                 y_far_copy(k).start()
 
+    low = flat(scaled)
+    for q in range(quarters):
+        weight[2, :, q * part : (q + 1) * part] = dot_tn(low, flat(grads, q)).astype(bf16)
+    store_gradients(1)
     send_home(final, last % 2)
     for g, hidden in enumerate((da, db)):
         low = flat(hidden)
         for q in range(quarters):
             weight[g, :, q * part : (q + 1) * part] = dot_tn(low, flat(x, q)).astype(bf16)
     store_gradients(0)
-    low = flat(scaled)
-    for q in range(quarters):
-        weight[2, :, q * part : (q + 1) * part] = dot_tn(low, flat(grads, q)).astype(bf16)
-    store_gradients(1)
     home_ref[0] = after_columns(0, 2)
     wait_gradients(0)
     wait_gradients(1)
@@ -1120,11 +1182,11 @@
             back_copy(s, k).wait_send()
 
 
-def expert_block(mixed, slots, gates, weights, own_grads, own_crossed, came, crossed, columns):
+def expert_block(mixed, slots, gates, shares, share_came, own_grads, own_crossed, came, crossed, columns):
     tokens, part = mixed.shape
     quarters = 2 * columns
     experts, ext, _ = came.shape
-    _, _, ff, wide = weights.shape
+    _, ff, wide = shares.shape
     dma = pltpu.SemaphoreType.DMA
     others = columns - 1
     return pl.pallas_call(
@@ -1135,7 +1197,7 @@
             jax.ShapeDtypeStruct((others, ext, part), bf16),
         )
         + (jax.ShapeDtypeStruct((2, ff, wide), bf16), jax.ShapeDtypeStruct((ff, wide), bf16)) * 2,
-        in_specs=[vmem()] * 3 + [hbm()] * 5,
+        in_specs=[vmem()] * 3 + [hbm()] * 6,
         out_specs=(vmem(),) + (hbm(),) * 6,
         scratch_shapes=[
             pltpu.VMEM((quarters, experts, ext, part), bf16),
@@ -1150,20 +1212,21 @@
             pltpu.VMEM((3, columns, ext, part), f32),
             pltpu.VMEM((experts, others, ext, part), bf16),
             pltpu.VMEM((experts, others, ext, part), bf16),
-            dma((3,)), dma((experts, columns)), dma((experts, columns)), dma((experts, columns)),
+            dma((2,)), dma((experts, columns)), dma((experts, columns)), dma((experts, columns)),
             dma((experts,)), dma((experts,)), dma((experts,)), dma((experts,)),
             dma((experts, others)), dma((experts, others)), dma((experts, others)), dma((experts, others)),
             dma((experts,)), dma((experts,)), dma((experts, others)), dma((experts, others)),
             dma((experts,)), dma((experts,)), dma((experts,)), dma((experts,)), dma((experts,)),
             dma((2,)), dma((2,)), dma((2,)), pltpu.SemaphoreType.REGULAR,
             dma((others,)), dma((others,)), dma((others,)), dma((others,)), dma((others,)), dma((others,)),
+            dma((2,)), dma((2,)),
         ],
         compiler_params=pltpu.CompilerParams(
             collective_id=2, has_side_effects=True, vmem_limit_bytes=56 * MIB
         ),
         cost_estimate=microseconds(80),
         name="expert_block",
-    )(mixed, slots, gates, weights, own_grads, own_crossed, came, crossed)
+    )(mixed, slots, gates, shares, share_came, own_grads, own_crossed, came, crossed)
 
 
 def settle_part(
@@ -1214,7 +1277,7 @@
         dmixed = dmixed + dot_exact(dlogits[:, : router_ref.shape[0]], router_ref[...], ((1,), (0,)))
         dmixed_ref[at, :] = dmixed
         stat[:, at] = dot_exact(
-            jnp.ones((8, part), f32), second_ref[at, :] * dmixed * gain_ref[...], ((1,), (1,))
+            jnp.ones((8, part), f32), second_ref[at, :] * dmixed * gain_ref[1:2], ((1,), (1,))
         )
         for n in range(len(peers)):
             stat_copy(i, n).start()
@@ -1230,38 +1293,42 @@
         row_total = dot_exact(total, first_row, ((0,), (0,)))[:, :1]
         inverse = column_ref[at, experts : experts + 1]
         two = cotangent_ref[at, :].astype(f32) + inverse * (
-            dmixed_ref[at, :] * gain_ref[...] - second_ref[at, :] * (inverse * inverse * row_total / D)
+            dmixed_ref[at, :] * gain_ref[1:2] - second_ref[at, :] * (inverse * inverse * row_total / D)
         )
         two_ref[at, :] = two
         low[at, :] = two.astype(bf16)
         spread.start_piece(i)
 
-    for i in range(PIECES):
+    for i in reversed(range(PIECES)):
         combine(i)
-        if i > 0:
-            close(i - 1)
-    close(PIECES - 1)
+        if i + 1 < PIECES:
+            close(i + 1)
+            if i + 2 < PIECES:
+                spread.hand_on_piece(i + 2)
+    close(0)
     after_spread()
-    rows = drouter_ref.shape[0]
-    drouter_ref[...] = dot_exact(dlogit_ref[...], mixed_ref[...].astype(f32), ((0,), (0,)))[:rows]
-    normed = second_ref[...] * column_ref[:, experts : experts + 1]
-    dgain_ref[...] = jnp.broadcast_to(
-        jnp.sum(dmixed_ref[...] * normed, axis=0, keepdims=True), dgain_ref.shape
-    )
-    spread.hand_on()
-    spread.finish()
+
+    def sums():
+        rows = drouter_ref.shape[0]
+        drouter_ref[...] = dot_exact(dlogit_ref[...], mixed_ref[...].astype(f32), ((0,), (0,)))[:rows]
+        normed = second_ref[...] * column_ref[:, experts : experts + 1]
+        dgain_ref[...] = jnp.broadcast_to(
+            jnp.sum(dmixed_ref[...] * normed, axis=0, keepdims=True), dgain_ref.shape
+        )
+
     for i in range(PIECES):
         for n in range(len(peers)):
             stat_copy(i, n).wait_send()
+    return spread, sums
 
 
 def finish_part(
     columns, experts,
     dfirst_ref, dweight_ref, small, layer_ref, two_ref, gain_ref, inverse_ref,
-    input_grad_ref, qkv_grad_ref, proj_grad_ref, sums_ref,
+    placed_grad, qkv_grad_ref, proj_grad_ref, sums_ref,
     core_in, keep, col_out, col_in, stat, stat_in, y_in, z_out, z_in, held, row_out, row_in, small_in,
     core_send, core_recv, col_send, col_recv, stat_send, stat_recv,
-    y_send, y_recv, z_send, z_recv, row_send, row_recv, small_send, small_recv, others, while_waiting,
+    y_send, y_recv, z_send, z_recv, row_send, row_recv, small_send, small_recv, others, others_meanwhile, while_waiting,
 ):
     ex, half = lax.axis_index("ex"), lax.axis_index("half")
     row, col = lax.axis_index("row"), lax.axis_index("col")
@@ -1293,28 +1360,26 @@
         )
 
     queue = [(s, a) for s in nearest_first(experts)[::-1] + [0] for a in range(2)]
-    crossing = []
     cell = {}
 
-    def start():
-        for i in range(PIECES):
-            core_copy(i).start()
-
-    def cross():
-        for i in range(PIECES):
-            at = slice(i * size, (i + 1) * size)
-            core_copy(i).wait_recv()
-            for j in range(columns):
-                keep[j, at] = dfirst_ref[row * columns + j, at].astype(f32) + core_in[j, at].astype(f32)
-            for k in range(1, columns):
-                to = (col + k) % columns
-                col_out[k - 1, at] = keep[to, at].astype(bf16)
-                copy = remote(
-                    col_out.at[k - 1, pl.ds(i * size, size)], col_in.at[k - 1, pl.ds(i * size, size)],
-                    col_send.at[i, k - 1], col_recv.at[i, k - 1], {"col": to},
-                )
-                copy.start()
-                crossing.append(copy)
+    def col_copy(i, k):
+        at = pl.ds(i * size, size)
+        return remote(
+            col_out.at[k - 1, at], col_in.at[k - 1, at], col_send.at[i, k - 1], col_recv.at[i, k - 1],
+            {"col": (col + k) % columns},
+        )
+
+    def start(i):
+        core_copy(i).start()
+
+    def cross(i):
+        at = slice(i * size, (i + 1) * size)
+        core_copy(i).wait_recv()
+        for j in range(columns):
+            keep[j, at] = dfirst_ref[row * columns + j, at].astype(f32) + core_in[j, at].astype(f32)
+        for k in range(1, columns):
+            col_out[k - 1, at] = keep[(col + k) % columns, at].astype(bf16)
+            col_copy(i, k).start()
 
     def normed():
         return layer_ref[...].astype(f32) * inverse_ref[:, 127:128]
@@ -1325,14 +1390,15 @@
         return remote(stat, stat_in.at[n], stat_send.at[n], stat_recv.at[n], peers[n])
 
     def arrive():
-        for copy in crossing:
-            copy.wait_recv()
+        for i in range(PIECES):
+            for k in range(1, columns):
+                col_copy(i, k).wait_recv()
         dnorm = keep[col]
         for k in range(1, columns):
             dnorm = dnorm + col_in[k - 1].astype(f32)
         keep[col] = dnorm
         stat[...] = dot_exact(
-            jnp.ones((8, part), f32), layer_ref[...].astype(f32) * (dnorm * gain_ref[...]), ((1,), (1,))
+            jnp.ones((8, part), f32), layer_ref[...].astype(f32) * (dnorm * gain_ref[:1]), ((1,), (1,))
         )
         for n in range(len(peers)):
             stat_copy(n).start()
@@ -1352,14 +1418,15 @@
         first_row = jnp.where(lax.broadcasted_iota(jnp.int32, (8, 128), 0) == 0, 1.0, 0.0)
         row_total = dot_exact(total, first_row, ((0,), (0,)))[:, :1]
         inverse = inverse_ref[:, 127:128]
-        input_grad_ref[...] = (
-            two_ref[...] + inverse * (keep[col] * gain_ref[...] - normed() * (inverse * row_total / D))
+        placed_grad[...] = (
+            two_ref[...] + inverse * (keep[col] * gain_ref[:1] - normed() * (inverse * row_total / D))
         ).astype(bf16)
 
     def rest():
         for at in queue[:2]:
             y_copy(*at).start()
-        cross()
+        cross(0)
+        others_meanwhile()
         for n, (s, a) in enumerate(queue):
             y_copy(s, a).wait_send()
             if n + 2 < len(queue):
@@ -1372,9 +1439,9 @@
                 z_copy(s, a).start()
             else:
                 held[a] = total
-            if n == len(queue) // 2:
+            if n == 2:
                 arrive()
-            if n == len(queue) - 2:
+            if n == 4:
                 close()
         while_waiting()
         for s in nearest_first(experts)[::-1]:
@@ -1395,17 +1462,19 @@
             for k in range(3):
                 qkv_grad_ref[:, k, at_row, :] = values[:, k * hc : (k + 1) * hc]
         swap.wait_send()
-        for copy in cell["smalls"] + crossing:
+        for copy in cell["smalls"]:
             copy.wait_send()
         for n in range(len(peers)):
             stat_copy(n).wait_send()
         for i in range(PIECES):
             core_copy(i).wait_send()
+            for k in range(1, columns):
+                col_copy(i, k).wait_send()
         for s, a in queue:
             if s > 0:
                 z_copy(s, a).wait_send()
 
-    return start, rest
+    return start, cross, rest
 
 
 def tail_kernel(columns, experts, *refs):
@@ -1425,7 +1494,7 @@
     branch_ref, two_ref, drouter_ref, dgain_ref, dfirst_ref, dweight_ref, dvector_ref, small = take(8)
     y_own, y_in, y_home = take(3)
     y_load, y_send, y_recv, y_away, y_came, half_send, half_recv = take(7)
-    y_far_in = take(1)[0]
+    y_far_in, placed_out, placed_grad = take(3)
     settle_scratch = take(7 + 6)
     attention_scratch = take(5)
     finish_scratch = take(13 + 14)
@@ -1485,25 +1554,29 @@
     y_stay.wait()
     y_far_load.wait()
     y_sum(far, [y_far_in[k - 1] for k in range(1, columns)])
-    settle_part(
+    spread, settle_sums = settle_part(
         columns, experts,
         home_ref, slot_ref, column_ref, second_ref, mixed_ref, cotangent_ref, gain_two, router_ref,
         branch_ref, two_ref, drouter_ref, dgain_ref, *settle_scratch, after_spread,
     )
     ways = near + [0]
-
-    def between(a):
-        last = second_ref.shape[0] // TILE - 1
-        if a == last:
-            while ways:
-                y_homeward(ways.pop(0))
-        elif a > 0 and len(ways) > 1:
-            y_homeward(ways.pop(0))
+    tokens, part = second_ref.shape
+    stat_rows = drouter_ref.shape[0]
+
+    def others_meanwhile():
+        settle_sums()
+        bias_sums(attention_scratch[1], dvector_ref)
+        small[8:16] = dgain_ref[...]
+        small[16 : 16 + stat_rows] = drouter_ref[...]
+        pieces = 2 * TILE // part
+        for i in range(dvector_ref.shape[0]):
+            for n in range(pieces):
+                at = 16 + stat_rows + i * pieces + n
+                small[at : at + 1] = dvector_ref[i : i + 1, n * part : (n + 1) * part]
 
     def while_waiting():
         for s in range(1, experts):
             y_copy(s).wait_recv()
-        tokens = second_ref.shape[0]
         ext = y_own.shape[1]
         size = tokens // PIECES
         lane = lax.broadcasted_iota(jnp.int32, (size, 128), 1)
@@ -1514,27 +1587,40 @@
                 place = jnp.sum(jnp.where(lane == (ex + s) % experts, slot_ref[at, :], 0.0), axis=1, keepdims=True)
                 hit = place == lax.broadcasted_iota(jnp.int32, (size, ext), 1).astype(f32)
                 total = total + dot_nn(jnp.where(hit, 1.0, 0.0).astype(bf16), y_home[s])
-            layer_out_ref[at, :] = total.astype(bf16)
-
-    start, rest = finish_part(
+            placed_out[at, :] = total.astype(bf16)
+        to_given = given_table(place_row, tokens)
+        layer_out_ref[...] = dot_nn(to_given, placed_out[...]).astype(bf16)
+        input_grad_ref[...] = dot_nn(to_given, placed_grad[...]).astype(bf16)
+
+    start, cross, rest = finish_part(
         columns, experts,
         dfirst_ref, dweight_ref, small, layer_ref, two_ref, gain_one, lse_ref,
-        input_grad_ref, qkv_grad_ref, proj_grad_ref, sums_ref, *finish_scratch, members, while_waiting,
-    )
+        placed_grad, qkv_grad_ref, proj_grad_ref, sums_ref, *finish_scratch, members, others_meanwhile, while_waiting,
+    )
+
+    def before(a):
+        if a + 1 == PIECES:
+            spread.hand_on_piece(1)
+        elif a == 2:
+            spread.hand_on_piece(0)
+        spread.wait_piece(a)
+
+    def after(a):
+        start(a)
+        if a + 1 < PIECES:
+            cross(a + 1)
+        if a == 0:
+            while ways:
+                y_homeward(ways.pop(0))
+        elif a + 2 < PIECES and len(ways) > 1:
+            y_homeward(ways.pop(0))
+
     attention_backward_kernel(
-        branch_ref, qkv_ref, lse_ref, attended_ref, first_ref, weight_ref, place_row, length_ref, vector_ref,
-        dfirst_ref, dweight_ref, dvector_ref, *attention_scratch, between, start,
-    )
-    part = second_ref.shape[1]
-    stat_rows = drouter_ref.shape[0]
-    small[8:16] = dgain_ref[...]
-    small[16 : 16 + stat_rows] = drouter_ref[...]
-    pieces = 2 * TILE // part
-    for i in range(dvector_ref.shape[0]):
-        for n in range(pieces):
-            at = 16 + stat_rows + i * pieces + n
-            small[at : at + 1] = dvector_ref[i : i + 1, n * part : (n + 1) * part]
+        branch_ref, qkv_ref, lse_ref, attended_ref, first_ref, weight_ref, length_ref, vector_ref,
+        dfirst_ref, dweight_ref, dvector_ref, *attention_scratch, before, after,
+    )
     rest()
+    spread.wait_sends()
     for copy in halves:
         copy.wait()
     for s in near + [0]:
@@ -1585,6 +1671,8 @@
             dma((2,)), dma((experts, others)), dma((experts, others)), dma((experts,)), dma((experts,)), dma((2,)), dma((2,)),
             pltpu.VMEM((others, ext, part), bf16),
             pltpu.VMEM((tokens, part), bf16),
+            pltpu.VMEM((tokens, part), bf16),
+            pltpu.VMEM((tokens, part), bf16),
             pltpu.VMEM((tokens, part), f32),
             pltpu.VMEM((tokens, 128), f32),
             pltpu.VMEM((8, tokens), f32),
@@ -1657,32 +1745,28 @@
     qkv_low = jnp.moveaxis(qkv_weight[0, 0].astype(bf16), 1, 0).reshape(2, -1, 3 * hc)
     proj_low = jnp.swapaxes(proj_weight[:, :, 0, 0].astype(bf16), 1, 2)
     shard = jnp.concatenate([qkv_low, proj_low], axis=2)
-    gains_eight = jnp.pad(norm_gains, ((0, 6), (0, 0)))
     stat_rows = (experts + 8) // 8 * 8
-    x_all, gains_all, weight, slot_rows, slot_columns, own_crossed, *grad_rows = gather(
-        layer_in, gains_eight, shard, placing, routes, cotangent, stat_rows, ext, experts, columns
-    )
-    weight = weight.reshape(D, 4 * hc)
     ff = expert_down.shape[1]
-    weights = jnp.concatenate(
+    shares = jnp.concatenate(
         [jnp.transpose(expert_up[0], (1, 2, 0)).reshape(2 * ff, wide).astype(bf16), expert_down[0].astype(bf16)]
-    )
-
-    x_all, weights = lax.optimization_barrier((x_all, weights))
-    weights = lax.all_gather(weights, "half", axis=0, tiled=True).reshape(2, 3, ff, wide)
+    ).reshape(3, ff, wide)
     vectors = bias_vectors(rel_bias, tokens)
     router_rows = jnp.pad(router.T, ((0, stat_rows - experts), (0, 0)))
-    first, qkv, attended, lse, second, table, mixed, gates, came, crossed = attend(
-        x_all, gains_all, weight, placing, lengths, vectors, layer_in, norm_gains[1:], router_rows, slot_rows,
+    x_all, gains_all, weight, slot_rows, slot_columns, own_crossed, placed, placed_cot, *grad_rows = gather(
+        layer_in, norm_gains, shard, placing, routes.T, cotangent, stat_rows, ext, experts, columns
+    )
+    weight = weight.reshape(D, 4 * hc)
+    first, qkv, attended, lse, second, table, mixed, gates, came, crossed, share_came = attend(
+        x_all, gains_all, weight, lengths, vectors, placed, norm_gains, router_rows, slot_rows, shares,
         grad_rows, columns,
     )
     home, y, y_far, keep_up, keep_down, away_up, away_down = expert_block(
-        mixed, slot_rows, gates, weights, grad_rows[0], own_crossed, came, crossed, columns
+        mixed, slot_rows, gates, shares, share_came, grad_rows[0], own_crossed, came, crossed, columns
     )
     layer_out, input_grad, grad_qkv, grad_proj, sums, came_up, came_down = tail(
-        home, slot_columns, table, second, mixed, cotangent, norm_gains[1:],
-        router_rows, qkv, lse, attended, first, weight, placing, lengths, vectors, layer_in, norm_gains[:1], y, y_far, away_up, away_down,
-        stat_rows, experts, columns,
+        home, slot_columns, table, second, mixed, placed_cot, norm_gains,
+        router_rows, qkv, lse, attended, first, weight, placing, lengths, vectors, placed, norm_gains,
+        y, y_far, away_up, away_down, stat_rows, experts, columns,
     )
     grad_gains = jnp.stack([sums[0], sums[8]])
     grad_router = sums[16 : 16 + experts].T

time: 334 us -> 311 us (0.931)
  the two profiles are of different devices: /device:TPU:0 before, /device:TPU:9 now
where the time goes in v4:
time: 311 us; the launch traced here: 306 us
  Pallas kernels  272 us (87%)
  other arithmetic  23.6 us (8%)
  local copies, waits for them, and re-layouts  6.74 us (2%)
    pallas_call x1, Pallas kernels, tail(): pl.pallas_call(functools.partial(tail_kernel, columns, experts), out_shap...  95 us
    pallas_call x1, Pallas kernels, expert_block(): pl.pallas_call(functools.partial(expert_kernel, columns, experts), out_sh...  89.4 us
    pallas_call x1, Pallas kernels, attend(): pl.pallas_call(functools.partial(attend_kernel, columns, experts), out_sh...  52.3 us
    pallas_call x1, Pallas kernels, gather(): pl.pallas_call(functools.partial(gather_kernel, columns, experts), out_sh...  35.1 us
    convert_element_type x3, other arithmetic, local(): out = out + group + (group[0].astype(bf16),)  14.8 us

profile of v4, /device:TPU:9, one launch (start us, length us, event | category | flops | bytes accessed | tf_op | source)
XLA Modules:
  0.0 305.8 jit_solution(13028827661656594428)
XLA Ops:
  0.7 0.8 pad.4.refs_7_
  1.5 1.2 fusion.6
  2.7 0.9 fusion.15
  3.6 1.1 convert_bitcast_fusion.1
  4.9 0.2 reshape.83
  5.2 2.0 convert_element_type.60
  7.3 1.5 pad_maximum_fusion
  8.8 35.1 %gather.1 = (bf16[4,1024,256]{2,1,0:T(8,128)(2,1)}, f32[4,2,256]{2,1,0:T(2,128)S(1)}, bf16[2,8,64,1024]{3,2,1,0:T(8,128)(2,1)}, f32[8,1024]{1,0:T(8,128)S(1)}, f...) custom-call(bf16[1024,256]{1,0:T(8,128)(2,1)} %refs_0_.1, ...), custom_call_target="tpu_custom_call" | custom-call | bytes 105000000 | tf_op jit(solution)/shard_map/gather/pallas_call | solution.py:781
  43.9 52.3 %attend.1 = (bf16[4,1024,256]{2,1,0:T(8,128)(2,1)}, bf16[1024,768]{1,0:T(8,128)(2,1)}, bf16[1024,256]{1,0:T(8,128)(2,1)S(1)}, f32[1024,128]{1,0:T(8,128)}, f32[1...) custom-call(bf16[4,1024,256]{2,1,0:T(8,128)(2,1)} %get-tuple-element, ...), custom_call_target="tpu_custom_call" | custom-call | bytes 157500000 | tf_op jit(solution)/shard_map/attend/pallas_call | solution.py:537
  96.3 0.6 copy-done.12
  96.9 89.4 %expert_block.1 = (bf16[4,656,256]{2,1,0:T(8,128)(2,1)}, bf16[2,4,656,256]{3,2,1,0:T(8,128)(2,1)}, bf16[1,656,256]{2,1,0:T(8,128)(2,1)}, bf16[2,704,512]{2,1,0:T...) custom-call(bf16[1024,256]{1,0:T(8,128)(2,1)} %get-tuple-element.73.refs_0_.refs_4_, ...), custom_call_target="tpu_custom_call" | custom-call | bytes 280000000 | tf_op jit(solution)/shard_map/expert_block/pallas_call | solution.py:1192
  186.4 1.1 copy-done.3
  187.5 1.0 copy-done.8
  188.6 95.0 %tail.1 = (bf16[1024,256]{1,0:T(8,128)(2,1)S(1)}, bf16[1024,256]{1,0:T(8,128)(2,1)S(1)}, f32[64,3,2,256]{3,2,1,0:T(2,128)S(1)}, f32[2,64,256]{2,1,0:T(8,128)S(1)...) custom-call(bf16[4,656,256]{2,1,0:T(8,128)(2,1)} %get-tuple-element.79.refs_0_, ...), custom_call_target="tpu_custom_call" | custom-call | bytes 315000000 | tf_op jit(solution)/shard_map/tail/pallas_call | solution.py:1646
  283.6 0.6 multiply_subtract_fusion.4
  284.2 0.6 multiply_subtract_fusion.3
  284.9 0.9 add_subtract_fusion
  285.8 1.9 convert_bitcast_fusion.2
  287.7 3.8 %fusion.29 = (bf16[1,1,64,2,3,256]{5,3,4,2,1,0:T(2,128)(2,1)}, f32[1,1,64,2,3,256]{5,3,4,2,1,0:T(2,128)}, f32[1,1,64,2,3,256]{5,3,4,2,1,0:T(2,128)}, f32[1,1,64,2,3,256]{5,3,4,2,1,0:T(2,128)}) fusion(f32[1,1,64,2,3,256]{5,3,4,2,1,0:T(2,128)S(1)} %copy-done.21, f32[64,3,2,256]{3,2,1,0:T(2,128)S(1)} %get-tuple-element.95, ...), kind=kLoop, calls=%fused_computation.60 | loop fusion | flops 1474560 | bytes 2949120 | tf_op jit(solution)/shard_map/convert_element_type | solution.py:1787
  291.6 5.0 %fusion.23 = (bf16[1,704,512]{2,1,0:T(8,128)(2,1)}, f32[1,704,512]{2,1,0:T(8,128)}, f32[1,704,512]{2,1,0:T(8,128)}, f32[1,704,512]{2,1,0:T(8,128)}) fusion(f32[1,704,512]{2,1,0:T(8,128)S(1)} %copy-done.18, bf16[704,512]{1,0:T(8,128)(2,1)S(1)} %get-tuple-element.100, bf16[704,512]{1,0:T(8,128)(2,1)S(1)} %copy-done.24, f32[1,704,512]{2,1,0:T(8,128)S(1)} %copy-done.22, ...), kind=kLoop, calls=%fused_computation.58 | loop fusion | flops 6488064 | bytes 10813440 | tf_op jit(solution)/shard_map/convert_element_type | solution.py:1787
  296.7 1.0 copy-done.23
  297.7 6.1 %fusion.26 = (bf16[1,512,2,704]{1,3,2,0:T(8,128)(2,1)}, f32[1,512,2,704]{1,3,2,0:T(8,128)}, f32[1,512,2,704]{1,3,2,0:T(8,128)}, f32[1,512,2,704]{1,3,2,0:T(8,128)}) fusion(f32[1,512,2,704]{1,3,2,0:T(8,128)S(1)} %copy-done.16, bf16[2,704,512]{2,1,0:T(8,128)(2,1)} %get-tuple-element.98, bf16[2,704,512]{2,1,0:T(8,128)(2,1)S(1)} %copy-done.23, ...), kind=kLoop, calls=%fused_computation.59 | loop fusion | flops 12976128 | bytes 21626880 | tf_op jit(solution)/shard_map/convert_element_type | solution.py:1787
  303.7 0.8 copy.86
  304.5 0.8 copy.87
  (76 shorter events, 0.6 us)
Async XLA Ops:
  7.3 36.7 %copy-start.15 = (s32[1,4]{1,0:T(1,128)S(1)}, s32[1,4]{1,0:T(1,128)}, u32[]{:S(2)}) copy-start(s32[1,4]{1,0:T(1,128)} %refs_14_.1) | copy-start | bytes 52
  43.9 52.3 %copy-start.2 = (bf16[656,256]{1,0:T(8,128)(2,1)}, bf16[656,256]{1,0:T(8,128)(2,1)S(1)}, u32[]{:S(2)}) copy-start(bf16[656,256]{1,0:T(8,128)(2,1)S(1)} %get-tuple-element.69.refs_10_.refs_5_) | copy-start | bytes 1007620
  43.9 52.3 %copy-start.9 = (bf16[1,656,256]{2,1,0:T(8,128)(2,1)}, bf16[1,656,256]{2,1,0:T(8,128)(2,1)S(1)}, u32[]{:S(2)}) copy-start(bf16[1,656,256]{2,1,0:T(8,128)(2,1)S(1)} %get-tuple-element.76.refs_6_) | copy-start | bytes 1007620
  43.9 52.3 %copy-start.10 = (f32[8,1024]{1,0:T(8,128)}, f32[8,1024]{1,0:T(8,128)S(1)}, u32[]{:S(2)}) copy-start(f32[8,1024]{1,0:T(8,128)S(1)} %get-tuple-element.68.refs_8_.refs_1_) | copy-start | bytes 98308
  96.9 89.5 %copy-start = (bf16[1024,256]{1,0:T(8,128)(2,1)S(1)}, bf16[1024,256]{1,0:T(8,128)(2,1)}, u32[]{:S(2)}) copy-start(bf16[1024,256]{1,0:T(8,128)(2,1)} %get-tuple-element.67.refs_5_.refs_16_) | copy-start | bytes 1572868
  96.9 89.5 %copy-start.1 = (bf16[1024,256]{1,0:T(8,128)(2,1)S(1)}, bf16[1024,256]{1,0:T(8,128)(2,1)}, u32[]{:S(2)}) copy-start(bf16[1024,256]{1,0:T(8,128)(2,1)} %get-tuple-element.73.refs_0_.refs_4_) | copy-start | bytes 1572868
  96.9 89.5 %copy-start.4 = (f32[1024,128]{1,0:T(8,128)S(1)}, f32[1024,128]{1,0:T(8,128)}, u32[]{:S(2)}) copy-start(f32[1024,128]{1,0:T(8,128)} %get-tuple-element.80.refs_1_) | copy-start | bytes 1572868
  96.9 89.5 %copy-start.5 = (bf16[1024,256]{1,0:T(8,128)(2,1)S(1)}, bf16[1024,256]{1,0:T(8,128)(2,1)}, u32[]{:S(2)}) copy-start(bf16[1024,256]{1,0:T(8,128)(2,1)} %get-tuple-element.83.refs_5_) | copy-start | bytes 1572868
  96.9 89.5 %copy-start.6 = (f32[1024,128]{1,0:T(8,128)S(1)}, f32[1024,128]{1,0:T(8,128)}, u32[]{:S(2)}) copy-start(f32[1024,128]{1,0:T(8,128)} %get-tuple-element.85.refs_9_) | copy-start | bytes 1572868
  96.9 89.5 %copy-start.7 = (f32[1024,128]{1,0:T(8,128)S(1)}, f32[1024,128]{1,0:T(8,128)}, u32[]{:S(2)}) copy-start(f32[1024,128]{1,0:T(8,128)} %get-tuple-element.81.refs_2_) | copy-start | bytes 1572868
  188.5 95.1 %copy-start.34 = (f32[2,256]{1,0:T(2,128)S(1)}, f32[2,256]{1,0:T(2,128)}, u32[]{:S(2)}) copy-start(f32[2,256]{1,0:T(2,128)} %param.35) | copy-start | bytes 6148
  188.5 95.1 %copy-start.35 = (f32[2,256]{1,0:T(2,128)S(1)}, f32[2,256]{1,0:T(2,128)}, u32[]{:S(2)}) copy-start(f32[2,256]{1,0:T(2,128)} %param.36) | copy-start | bytes 6148
  188.5 95.8 %copy-start.28 = (f32[256,4]{0,1:T(4,128)S(1)}, f32[256,4]{0,1:T(4,128)}, u32[]{:S(2)}) copy-start(f32[256,4]{0,1:T(4,128)} %param.40) | copy-start | bytes 12292
  188.5 95.8 %copy-start.30 = (f32[256,4]{0,1:T(4,128)S(1)}, f32[256,4]{0,1:T(4,128)}, u32[]{:S(2)}) copy-start(f32[256,4]{0,1:T(4,128)} %param.41) | copy-start | bytes 12292
  188.5 95.8 %copy-start.31 = (f32[256,4]{0,1:T(4,128)S(1)}, f32[256,4]{0,1:T(4,128)}, u32[]{:S(2)}) copy-start(f32[256,4]{0,1:T(4,128)} %param.42) | copy-start | bytes 12292
  188.5 96.4 %copy-start.27 = (f32[3,512,32]{1,2,0:T(8,128)S(1)}, f32[3,512,32]{1,2,0:T(8,128)}, u32[]{:S(2)}) copy-start(f32[3,512,32]{1,2,0:T(8,128)} %constant.30.clone) | copy-start | bytes 589828
  188.5 96.4 %copy-start.29 = (f32[32,4]{0,1:T(4,128)S(1)}, f32[32,4]{0,1:T(4,128)}, u32[]{:S(2)}) copy-start(f32[32,4]{0,1:T(4,128)} %param.37) | copy-start | bytes 1540
  188.5 96.4 %copy-start.32 = (f32[32,4]{0,1:T(4,128)S(1)}, f32[32,4]{0,1:T(4,128)}, u32[]{:S(2)}) copy-start(f32[32,4]{0,1:T(4,128)} %param.38) | copy-start | bytes 1540
  188.5 96.4 %copy-start.33 = (f32[32,4]{0,1:T(4,128)S(1)}, f32[32,4]{0,1:T(4,128)}, u32[]{:S(2)}) copy-start(f32[32,4]{0,1:T(4,128)} %param.39) | copy-start | bytes 1540
  188.5 97.3 %copy-start.25 = (f32[2,256,1,1,64]{1,4,3,2,0:T(8,128)S(1)}, f32[2,256,1,1,64]{1,4,3,2,0:T(8,128)}, u32[]{:S(2)}) copy-start(f32[2,256,1,1,64]{1,4,3,2,0:T(8,128)} %param.46) | copy-start | bytes 393220
  188.6 99.2 %copy-start.26 = (f32[1,1,64,2,3,256]{5,3,4,2,1,0:T(2,128)S(1)}, f32[1,1,64,2,3,256]{5,3,4,2,1,0:T(2,128)}, u32[]{:S(2)}) copy-start(f32[1,1,64,2,3,256]{5,3,4,2,1,0:T(2,128)} %param.44) | copy-start | bytes 1179652
  285.8 5.7 %copy-start.24 = (bf16[704,512]{1,0:T(8,128)(2,1)S(1)}, bf16[704,512]{1,0:T(8,128)(2,1)}, u32[]{:S(2)}) copy-start(bf16[704,512]{1,0:T(8,128)(2,1)} %get-tuple-element.99) | copy-start | bytes 2162692
  291.6 5.1 %copy-start.20 = (f32[1,512,2,704]{1,3,2,0:T(8,128)S(1)}, f32[1,512,2,704]{1,3,2,0:T(8,128)}, u32[]{:S(2)}) copy-start(f32[1,512,2,704]{1,3,2,0:T(8,128)} %param.51) | copy-start | bytes 8650756
  291.6 6.1 %copy-start.23 = (bf16[2,704,512]{2,1,0:T(8,128)(2,1)S(1)}, bf16[2,704,512]{2,1,0:T(8,128)(2,1)}, u32[]{:S(2)}) copy-start(bf16[2,704,512]{2,1,0:T(8,128)(2,1)} %get-tuple-element.97) | copy-start | bytes 4325380
  (12 other events, 33.5 us)

commit v5 on v4

--- a/solution.py
+++ b/solution.py
@@ -643,17 +643,14 @@
     first_at = lax.broadcasted_iota(jnp.int32, (tokens, tokens), 0)
     second_at = lax.broadcasted_iota(jnp.int32, (tokens, tokens), 1)
 
-    def slot_columns():
+    def slot_tables():
+        from_on = jnp.where(first_at <= second_at, 1.0, 0.0).astype(bf16)
+        table = jnp.where(hits > 0.5, dot_nn(low_hits, from_on) - 1.0, -1.0)
+        slot_row_ref[...] = table[: slot_row_ref.shape[0]]
+        slot_column_ref[...] = table.T
+
+    def place_cotangent():
         placed_cot[...] = dot_tn(to_given, cotangent_ref[...]).astype(bf16)
-        up_to = jnp.where(second_at <= first_at, 1.0, 0.0).astype(bf16)
-        same = jnp.where(first_at == second_at, 1.0, 0.0).astype(bf16)
-        slot_column_ref[...] = jnp.where(dot_nt(same, low_hits) > 0.5, dot_nt(up_to, low_hits) - 1.0, -1.0)
-
-    def slot_rows():
-        from_on = jnp.where(first_at <= second_at, 1.0, 0.0).astype(bf16)
-        rows = slot_row_ref.shape[0]
-        row_counts = dot_nn(low_hits, from_on)[:rows]
-        slot_row_ref[...] = jnp.where(hits[:rows] > 0.5, row_counts - 1.0, -1.0)
 
     def cotangent_slots(s):
         e = (ex + s) % experts
@@ -674,7 +671,7 @@
         for copy in crossing:
             copy.start()
 
-    jobs = [slot_columns, slot_rows, first_slots] + [functools.partial(cotangent_slots, s) for s in range(1, experts)]
+    jobs = [place_cotangent, slot_tables, first_slots] + [functools.partial(cotangent_slots, s) for s in range(1, experts)]
     jobs.pop(0)()
     for i, (s, a) in enumerate(queue):
         z_copy(s, a).wait_send()
@@ -1328,7 +1325,7 @@
     placed_grad, qkv_grad_ref, proj_grad_ref, sums_ref,
     core_in, keep, col_out, col_in, stat, stat_in, y_in, z_out, z_in, held, row_out, row_in, small_in,
     core_send, core_recv, col_send, col_recv, stat_send, stat_recv,
-    y_send, y_recv, z_send, z_recv, row_send, row_recv, small_send, small_recv, others, others_meanwhile, while_waiting,
+    y_send, y_recv, z_send, z_recv, row_send, row_recv, small_send, small_recv, others_meanwhile, while_waiting,
 ):
     ex, half = lax.axis_index("ex"), lax.axis_index("half")
     row, col = lax.axis_index("row"), lax.axis_index("col")
@@ -1360,7 +1357,6 @@
         )
 
     queue = [(s, a) for s in nearest_first(experts)[::-1] + [0] for a in range(2)]
-    cell = {}
 
     def col_copy(i, k):
         at = pl.ds(i * size, size)
@@ -1403,14 +1399,19 @@
         for n in range(len(peers)):
             stat_copy(n).start()
         small[:8] = jnp.broadcast_to(jnp.sum(dnorm * normed(), axis=0, keepdims=True), (8, part))
-        cell["smalls"] = [
-            remote(small, small_in.at[i], small_send.at[i], small_recv.at[i], where)
-            for i, where in enumerate(others)
-        ]
-        for copy in cell["smalls"]:
-            copy.start()
+        small_over_y.start()
+
+    small_over_y = remote(small, small_in.at[0], small_send.at[0], small_recv.at[0], {"half": 1 - half})
+    pair = small_in.at[experts]
+
+    def small_over_z(s):
+        return remote(pair, small_in.at[s], small_send.at[s], small_recv.at[s], {"ex": (ex + s) % experts})
 
     def close():
+        small_over_y.wait_recv()
+        small_in[experts] = small[...] + small_in[0]
+        for s in range(1, experts):
+            small_over_z(s).start()
         total = stat[...]
         for n in range(len(peers)):
             stat_copy(n).wait_recv()
@@ -1451,10 +1452,10 @@
         row_out[...] = held[1 - row].astype(bf16)
         swap = remote(row_out, row_in, row_send.at[0], row_recv.at[0], {"row": 1 - row})
         swap.start()
-        sums = small[...]
-        for i, copy in enumerate(cell["smalls"]):
-            copy.wait_recv()
-            sums = sums + small_in[i]
+        sums = small_in[experts]
+        for s in range(1, experts):
+            small_over_z(s).wait_recv()
+            sums = sums + small_in[s]
         sums_ref[...] = sums
         swap.wait_recv()
         for at_row, values in ((row, held[row]), (1 - row, row_in[...].astype(f32))):
@@ -1462,8 +1463,9 @@
             for k in range(3):
                 qkv_grad_ref[:, k, at_row, :] = values[:, k * hc : (k + 1) * hc]
         swap.wait_send()
-        for copy in cell["smalls"]:
-            copy.wait_send()
+        small_over_y.wait_send()
+        for s in range(1, experts):
+            small_over_z(s).wait_send()
         for n in range(len(peers)):
             stat_copy(n).wait_send()
         for i in range(PIECES):
@@ -1499,13 +1501,11 @@
     attention_scratch = take(5)
     finish_scratch = take(13 + 14)
     ex, half, col = lax.axis_index("ex"), lax.axis_index("half"), lax.axis_index("col")
-    members = [
-        {"ex": (ex + s) % experts, "half": (half + h) % 2}
-        for s in range(experts)
-        for h in range(2)
-        if s + h > 0
-    ]
-    greet(grid_peers(columns) + members)
+    greet(
+        grid_peers(columns)
+        + [{"ex": (ex + s) % experts} for s in range(1, experts)]
+        + [{"half": 1 - half}]
+    )
 
     halves = [
         remote(source, out, half_send.at[i], half_recv.at[i], {"half": 1 - half})
@@ -1595,7 +1595,7 @@
     start, cross, rest = finish_part(
         columns, experts,
         dfirst_ref, dweight_ref, small, layer_ref, two_ref, gain_one, lse_ref,
-        placed_grad, qkv_grad_ref, proj_grad_ref, sums_ref, *finish_scratch, members, others_meanwhile, while_waiting,
+        placed_grad, qkv_grad_ref, proj_grad_ref, sums_ref, *finish_scratch, others_meanwhile, while_waiting,
     )
 
     def before(a):
@@ -1642,7 +1642,6 @@
     rows, width = D // (4 * experts), 4 * hc
     small = (16 + stat_rows + vectors.size // part, part)
     dma = pltpu.SemaphoreType.DMA
-    members = 2 * experts
     return pl.pallas_call(
         functools.partial(tail_kernel, columns, experts),
         out_shape=(
@@ -1698,11 +1697,11 @@
             pltpu.VMEM((2, rows, width), f32),
             pltpu.VMEM((rows, width), bf16),
             pltpu.VMEM((rows, width), bf16),
-            pltpu.VMEM((members - 1,) + small, f32),
+            pltpu.VMEM((experts + 1,) + small, f32),
             dma((PIECES,)), dma((PIECES,)), dma((PIECES, others)), dma((PIECES, others)),
             dma((quarters - 1,)), dma((quarters - 1,)),
             dma((experts, 2)), dma((experts, 2)), dma((experts, 2)), dma((experts, 2)),
-            dma((1,)), dma((1,)), dma((members - 1,)), dma((members - 1,)),
+            dma((1,)), dma((1,)), dma((experts,)), dma((experts,)),
         ],
         compiler_params=pltpu.CompilerParams(
             collective_id=3, has_side_effects=True, vmem_limit_bytes=47 * MIB

time: 311 us -> 305 us (0.981)
  the two profiles are of different devices: /device:TPU:9 before, /device:TPU:0 now
where the time goes in v5:
time: 305 us; the launch traced here: 301 us
  Pallas kernels  267 us (88%)
  other arithmetic  23.6 us (8%)
  local copies, waits for them, and re-layouts  6.74 us (2%)
    pallas_call x1, Pallas kernels, expert_block(): pl.pallas_call(functools.partial(expert_kernel, columns, experts), out_sh...  89.6 us
    pallas_call x1, Pallas kernels, tail(): pl.pallas_call(functools.partial(tail_kernel, columns, experts), out_shap...  86 us
    pallas_call x1, Pallas kernels, attend(): pl.pallas_call(functools.partial(attend_kernel, columns, experts), out_sh...  51.6 us
    pallas_call x1, Pallas kernels, gather(): pl.pallas_call(functools.partial(gather_kernel, columns, experts), out_sh...  39.5 us
    convert_element_type x3, other arithmetic, local(): out = out + group + (group[0].astype(bf16),)  14.8 us

profile of v5, /device:TPU:0, one launch (start us, length us, event | category | flops | bytes accessed | tf_op | source)
XLA Modules:
  0.0 300.6 jit_solution(7227683366082248817)
XLA Ops:
  0.7 0.8 pad.4.refs_7_
  1.5 1.2 fusion.6
  2.7 0.9 fusion.15
  3.6 1.1 convert_bitcast_fusion.1
  4.9 0.2 reshape.83
  5.2 2.0 convert_element_type.60
  7.3 1.5 pad_maximum_fusion
  8.8 39.5 %gather.1 = (bf16[4,1024,256]{2,1,0:T(8,128)(2,1)}, f32[4,2,256]{2,1,0:T(2,128)S(1)}, bf16[2,8,64,1024]{3,2,1,0:T(8,128)(2,1)}, f32[8,1024]{1,0:T(8,128)S(1)}, f...) custom-call(bf16[1024,256]{1,0:T(8,128)(2,1)} %refs_0_.1, ...), custom_call_target="tpu_custom_call" | custom-call | bytes 105000000 | tf_op jit(solution)/shard_map/gather/pallas_call | solution.py:778
  48.4 51.6 %attend.1 = (bf16[4,1024,256]{2,1,0:T(8,128)(2,1)}, bf16[1024,768]{1,0:T(8,128)(2,1)}, bf16[1024,256]{1,0:T(8,128)(2,1)S(1)}, f32[1024,128]{1,0:T(8,128)}, f32[1...) custom-call(bf16[4,1024,256]{2,1,0:T(8,128)(2,1)} %get-tuple-element, ...), custom_call_target="tpu_custom_call" | custom-call | bytes 157500000 | tf_op jit(solution)/shard_map/attend/pallas_call | solution.py:537
  100.1 0.6 copy-done.12
  100.7 89.6 %expert_block.1 = (bf16[4,656,256]{2,1,0:T(8,128)(2,1)}, bf16[2,4,656,256]{3,2,1,0:T(8,128)(2,1)}, bf16[1,656,256]{2,1,0:T(8,128)(2,1)}, bf16[2,704,512]{2,1,0:T...) custom-call(bf16[1024,256]{1,0:T(8,128)(2,1)} %get-tuple-element.73.refs_0_.refs_4_, ...), custom_call_target="tpu_custom_call" | custom-call | bytes 280000000 | tf_op jit(solution)/shard_map/expert_block/pallas_call | solution.py:1189
  190.4 1.1 copy-done.3
  191.5 1.0 copy-done.8
  192.5 86.0 %tail.1 = (bf16[1024,256]{1,0:T(8,128)(2,1)S(1)}, bf16[1024,256]{1,0:T(8,128)(2,1)S(1)}, f32[64,3,2,256]{3,2,1,0:T(2,128)S(1)}, f32[2,64,256]{2,1,0:T(8,128)S(1)...) custom-call(bf16[4,656,256]{2,1,0:T(8,128)(2,1)} %get-tuple-element.79.refs_0_, ...), custom_call_target="tpu_custom_call" | custom-call | bytes 315000000 | tf_op jit(solution)/shard_map/tail/pallas_call | solution.py:1645
  278.6 0.6 multiply_subtract_fusion.4
  279.2 0.6 multiply_subtract_fusion.3
  279.9 0.9 add_subtract_fusion
  280.8 1.9 convert_bitcast_fusion.2
  282.7 3.8 %fusion.29 = (bf16[1,1,64,2,3,256]{5,3,4,2,1,0:T(2,128)(2,1)}, f32[1,1,64,2,3,256]{5,3,4,2,1,0:T(2,128)}, f32[1,1,64,2,3,256]{5,3,4,2,1,0:T(2,128)}, f32[1,1,64,2,3,256]{5,3,4,2,1,0:T(2,128)}) fusion(f32[1,1,64,2,3,256]{5,3,4,2,1,0:T(2,128)S(1)} %copy-done.21, f32[64,3,2,256]{3,2,1,0:T(2,128)S(1)} %get-tuple-element.95, ...), kind=kLoop, calls=%fused_computation.60 | loop fusion | flops 1474560 | bytes 2949120 | tf_op jit(solution)/shard_map/convert_element_type | solution.py:1786
  286.6 5.0 %fusion.23 = (bf16[1,704,512]{2,1,0:T(8,128)(2,1)}, f32[1,704,512]{2,1,0:T(8,128)}, f32[1,704,512]{2,1,0:T(8,128)}, f32[1,704,512]{2,1,0:T(8,128)}) fusion(f32[1,704,512]{2,1,0:T(8,128)S(1)} %copy-done.18, bf16[704,512]{1,0:T(8,128)(2,1)S(1)} %get-tuple-element.100, bf16[704,512]{1,0:T(8,128)(2,1)S(1)} %copy-done.24, f32[1,704,512]{2,1,0:T(8,128)S(1)} %copy-done.22, ...), kind=kLoop, calls=%fused_computation.58 | loop fusion | flops 6488064 | bytes 10813440 | tf_op jit(solution)/shard_map/convert_element_type | solution.py:1786
  291.7 1.0 copy-done.23
  292.7 6.1 %fusion.26 = (bf16[1,512,2,704]{1,3,2,0:T(8,128)(2,1)}, f32[1,512,2,704]{1,3,2,0:T(8,128)}, f32[1,512,2,704]{1,3,2,0:T(8,128)}, f32[1,512,2,704]{1,3,2,0:T(8,128)}) fusion(f32[1,512,2,704]{1,3,2,0:T(8,128)S(1)} %copy-done.16, bf16[2,704,512]{2,1,0:T(8,128)(2,1)} %get-tuple-element.98, bf16[2,704,512]{2,1,0:T(8,128)(2,1)S(1)} %copy-done.23, ...), kind=kLoop, calls=%fused_computation.59 | loop fusion | flops 12976128 | bytes 21626880 | tf_op jit(solution)/shard_map/convert_element_type | solution.py:1786
  298.7 0.8 copy.86
  299.5 0.8 copy.87
  (76 shorter events, 0.6 us)
Async XLA Ops:
  7.3 41.1 %copy-start.15 = (s32[1,4]{1,0:T(1,128)S(1)}, s32[1,4]{1,0:T(1,128)}, u32[]{:S(2)}) copy-start(s32[1,4]{1,0:T(1,128)} %refs_14_.1) | copy-start | bytes 52
  48.3 51.7 %copy-start.2 = (bf16[656,256]{1,0:T(8,128)(2,1)}, bf16[656,256]{1,0:T(8,128)(2,1)S(1)}, u32[]{:S(2)}) copy-start(bf16[656,256]{1,0:T(8,128)(2,1)S(1)} %get-tuple-element.69.refs_10_.refs_5_) | copy-start | bytes 1007620
  48.3 51.7 %copy-start.9 = (bf16[1,656,256]{2,1,0:T(8,128)(2,1)}, bf16[1,656,256]{2,1,0:T(8,128)(2,1)S(1)}, u32[]{:S(2)}) copy-start(bf16[1,656,256]{2,1,0:T(8,128)(2,1)S(1)} %get-tuple-element.76.refs_6_) | copy-start | bytes 1007620
  48.3 51.7 %copy-start.10 = (f32[8,1024]{1,0:T(8,128)}, f32[8,1024]{1,0:T(8,128)S(1)}, u32[]{:S(2)}) copy-start(f32[8,1024]{1,0:T(8,128)S(1)} %get-tuple-element.68.refs_8_.refs_1_) | copy-start | bytes 98308
  100.7 89.6 %copy-start = (bf16[1024,256]{1,0:T(8,128)(2,1)S(1)}, bf16[1024,256]{1,0:T(8,128)(2,1)}, u32[]{:S(2)}) copy-start(bf16[1024,256]{1,0:T(8,128)(2,1)} %get-tuple-element.67.refs_5_.refs_16_) | copy-start | bytes 1572868
  100.7 89.6 %copy-start.1 = (bf16[1024,256]{1,0:T(8,128)(2,1)S(1)}, bf16[1024,256]{1,0:T(8,128)(2,1)}, u32[]{:S(2)}) copy-start(bf16[1024,256]{1,0:T(8,128)(2,1)} %get-tuple-element.73.refs_0_.refs_4_) | copy-start | bytes 1572868
  100.7 89.6 %copy-start.4 = (f32[1024,128]{1,0:T(8,128)S(1)}, f32[1024,128]{1,0:T(8,128)}, u32[]{:S(2)}) copy-start(f32[1024,128]{1,0:T(8,128)} %get-tuple-element.80.refs_1_) | copy-start | bytes 1572868
  100.7 89.6 %copy-start.5 = (bf16[1024,256]{1,0:T(8,128)(2,1)S(1)}, bf16[1024,256]{1,0:T(8,128)(2,1)}, u32[]{:S(2)}) copy-start(bf16[1024,256]{1,0:T(8,128)(2,1)} %get-tuple-element.83.refs_5_) | copy-start | bytes 1572868
  100.7 89.7 %copy-start.6 = (f32[1024,128]{1,0:T(8,128)S(1)}, f32[1024,128]{1,0:T(8,128)}, u32[]{:S(2)}) copy-start(f32[1024,128]{1,0:T(8,128)} %get-tuple-element.85.refs_9_) | copy-start | bytes 1572868
  100.7 89.7 %copy-start.7 = (f32[1024,128]{1,0:T(8,128)S(1)}, f32[1024,128]{1,0:T(8,128)}, u32[]{:S(2)}) copy-start(f32[1024,128]{1,0:T(8,128)} %get-tuple-element.81.refs_2_) | copy-start | bytes 1572868
  192.4 86.2 %copy-start.34 = (f32[2,256]{1,0:T(2,128)S(1)}, f32[2,256]{1,0:T(2,128)}, u32[]{:S(2)}) copy-start(f32[2,256]{1,0:T(2,128)} %param.35) | copy-start | bytes 6148
  192.4 86.2 %copy-start.35 = (f32[2,256]{1,0:T(2,128)S(1)}, f32[2,256]{1,0:T(2,128)}, u32[]{:S(2)}) copy-start(f32[2,256]{1,0:T(2,128)} %param.36) | copy-start | bytes 6148
  192.4 86.8 %copy-start.28 = (f32[256,4]{0,1:T(4,128)S(1)}, f32[256,4]{0,1:T(4,128)}, u32[]{:S(2)}) copy-start(f32[256,4]{0,1:T(4,128)} %param.40) | copy-start | bytes 12292
  192.4 86.8 %copy-start.30 = (f32[256,4]{0,1:T(4,128)S(1)}, f32[256,4]{0,1:T(4,128)}, u32[]{:S(2)}) copy-start(f32[256,4]{0,1:T(4,128)} %param.41) | copy-start | bytes 12292
  192.5 86.8 %copy-start.31 = (f32[256,4]{0,1:T(4,128)S(1)}, f32[256,4]{0,1:T(4,128)}, u32[]{:S(2)}) copy-start(f32[256,4]{0,1:T(4,128)} %param.42) | copy-start | bytes 12292
  192.5 87.4 %copy-start.27 = (f32[3,512,32]{1,2,0:T(8,128)S(1)}, f32[3,512,32]{1,2,0:T(8,128)}, u32[]{:S(2)}) copy-start(f32[3,512,32]{1,2,0:T(8,128)} %constant.30.clone) | copy-start | bytes 589828
  192.5 87.4 %copy-start.29 = (f32[32,4]{0,1:T(4,128)S(1)}, f32[32,4]{0,1:T(4,128)}, u32[]{:S(2)}) copy-start(f32[32,4]{0,1:T(4,128)} %param.37) | copy-start | bytes 1540
  192.5 87.4 %copy-start.32 = (f32[32,4]{0,1:T(4,128)S(1)}, f32[32,4]{0,1:T(4,128)}, u32[]{:S(2)}) copy-start(f32[32,4]{0,1:T(4,128)} %param.38) | copy-start | bytes 1540
  192.5 87.4 %copy-start.33 = (f32[32,4]{0,1:T(4,128)S(1)}, f32[32,4]{0,1:T(4,128)}, u32[]{:S(2)}) copy-start(f32[32,4]{0,1:T(4,128)} %param.39) | copy-start | bytes 1540
  192.5 88.3 %copy-start.25 = (f32[2,256,1,1,64]{1,4,3,2,0:T(8,128)S(1)}, f32[2,256,1,1,64]{1,4,3,2,0:T(8,128)}, u32[]{:S(2)}) copy-start(f32[2,256,1,1,64]{1,4,3,2,0:T(8,128)} %param.46) | copy-start | bytes 393220
  192.5 90.2 %copy-start.26 = (f32[1,1,64,2,3,256]{5,3,4,2,1,0:T(2,128)S(1)}, f32[1,1,64,2,3,256]{5,3,4,2,1,0:T(2,128)}, u32[]{:S(2)}) copy-start(f32[1,1,64,2,3,256]{5,3,4,2,1,0:T(2,128)} %param.44) | copy-start | bytes 1179652
  280.8 5.7 %copy-start.24 = (bf16[704,512]{1,0:T(8,128)(2,1)S(1)}, bf16[704,512]{1,0:T(8,128)(2,1)}, u32[]{:S(2)}) copy-start(bf16[704,512]{1,0:T(8,128)(2,1)} %get-tuple-element.99) | copy-start | bytes 2162692
  286.6 5.1 %copy-start.20 = (f32[1,512,2,704]{1,3,2,0:T(8,128)S(1)}, f32[1,512,2,704]{1,3,2,0:T(8,128)}, u32[]{:S(2)}) copy-start(f32[1,512,2,704]{1,3,2,0:T(8,128)} %param.51) | copy-start | bytes 8650756
  286.6 6.1 %copy-start.23 = (bf16[2,704,512]{2,1,0:T(8,128)(2,1)S(1)}, bf16[2,704,512]{2,1,0:T(8,128)(2,1)}, u32[]{:S(2)}) copy-start(bf16[2,704,512]{2,1,0:T(8,128)(2,1)} %get-tuple-element.97) | copy-start | bytes 4325380
  (12 other events, 33.5 us)
